TPU v7x, 32 devices: a whole 2x2x4 slice. The times are simulated.
32 devices in a mesh: dp: 16 (over z, y, x), tensor: 2 (over core).
Axes of the slice: x: 2, y: 2, z: 4, core: 2. Of those that a mesh axis runs over, the one named last changes fastest.
Arguments:
- hidden_in: bfloat16 [16, 1024, 768], P(None, 'dp'), may hold values from -6 to 6
- teacher: bfloat16 [16, 1024, 768], P(None, 'dp', 'tensor'), may hold values from -6 to 6
- loss_mask: int32 [16, 1024], P(None, 'dp'), may hold values from 0 to 1, as said below
- lengths: int32 [16], replicated, may hold values from 768 to 1024, as said below
- dealing: int32 [16], replicated, may hold values from 0 to 15, each once
- norm_gain: float32 [768], replicated, may hold values from 0.5 to 1.5
- w_gate: bfloat16 [768, 1536], P(None, 'tensor'), may hold values from -0.21875 to 0.21875
- w_value: bfloat16 [768, 1536], P(None, 'tensor'), may hold values from -0.21875 to 0.21875
- w_state: bfloat16 [768, 256], replicated, may hold values from -0.21875 to 0.21875
- w_step: bfloat16 [768, 2, 24], P(None, None, 'tensor'), may hold values from -0.21875 to 0.21875
- step_bias: float32 [2, 24], P(None, 'tensor'), may hold values from -4 to -1
- conv_value: float32 [4, 1536], P(None, 'tensor'), may hold values from -0.5 to 0.5
- conv_vbias: float32 [1536], P('tensor'), may hold values from -0.5 to 0.5
- conv_state: float32 [4, 256], replicated, may hold values from -0.5 to 0.5
- conv_sbias: float32 [256], replicated, may hold values from -0.5 to 0.5
- decay_log: float32 [24], P('tensor'), may hold values from -4 to 2
- skip_gain: float32 [24], P('tensor'), may hold values from 0.5 to 1.5
- out_gain: float32 [1536], P('tensor'), may hold values from 0.5 to 1.5
- w_out: bfloat16 [1536, 768], P('tensor'), may hold values from -0.15625 to 0.15625
Outputs:
- layer_out: bfloat16 [16, 1024, 768], P('dp', None, 'tensor')
- grad_in: bfloat16 [16, 1024, 768], P(None, 'dp', 'tensor')
- grad_norm_gain: float32 [768], replicated
- grad_w_gate: float32 [768, 1536], P(None, 'tensor')
- grad_w_value: float32 [768, 1536], P(None, 'tensor')
- grad_w_state: float32 [768, 256], replicated
- grad_w_step: float32 [768, 2, 24], P(None, None, 'tensor')
- grad_step_bias: float32 [2, 24], P(None, 'tensor')
- grad_conv_value: float32 [4, 1536], P(None, 'tensor')
- grad_conv_vbias: float32 [1536], P('tensor')
- grad_conv_state: float32 [4, 256], replicated
- grad_conv_sbias: float32 [256], replicated
- grad_decay_log: float32 [24], P('tensor')
- grad_skip_gain: float32 [24], P('tensor')
- grad_out_gain: float32 [1536], P('tensor')
- grad_w_out: float32 [1536, 768], P('tensor')
Inputs may be any that keep to these rules, and one draw needn't show every extreme that they name: `lengths`: the number of real tokens of each sequence; positions from it on are padding; some sequence has 1024 and some has 768. `loss_mask`: 1 marks a token that counts in the loss; position 0 of every sequence is marked. A permutation of 0 .. 15; slot j of the dealt order holds sequence dealing[j], and slots j .. are those of index j of dp.
All inputs are finite; a program needn't handle non-finite values.
Results may differ from a plain program's by a relative error of at most 0.0095.
Values may be sent and summed in bfloat16 or wider, within the bound.
No kernel may reach another device: no remote copies, remote signals or barrier semaphores. Data moves between devices by JAX's collectives and lax.ppermute only.
A program may use at most 192 MiB of HBM per device.

v0:
```python
import jax
import jax.numpy as jnp
from jax import lax
from jax.sharding import PartitionSpec as P

D = 768
INNER = 1536
P_SIZE = 64
N = 64
Q = 128


EPSILON = 1e-05
SCAN_PRECISION = lax.Precision.HIGH


def silu_slope(values):
    logistic = jax.nn.sigmoid(values)
    return logistic * (1.0 + values * (1.0 - logistic))


def causal_conv(inputs, kernel, shift_bias):
    conv_width = kernel.shape[0]
    extent = inputs.shape[-2]
    widths = [(0, 0)] * (inputs.ndim - 2) + [(conv_width - 1, 0), (0, 0)]
    padded = jnp.pad(inputs, widths)
    summed = shift_bias + jnp.zeros_like(inputs)
    for offset in range(conv_width):
        summed = summed + kernel[offset] * lax.slice_in_dim(
            padded, offset, offset + extent, axis=inputs.ndim - 2
        )
    return summed


def span_scan(values, inputs_b, outputs_c, dt_steps, decay_rate):
    extent = values.shape[0]
    blocks = extent // Q
    heads_here = values.shape[1]
    log_decay = (dt_steps * decay_rate[None, :]).reshape(blocks, Q, heads_here)
    cumulative = jnp.cumsum(log_decay, axis=1)
    scaled = (values * dt_steps[:, :, None]).reshape(blocks, Q, heads_here, P_SIZE)
    keys_b = inputs_b.reshape(blocks, Q, N)
    query_c = outputs_c.reshape(blocks, Q, N)
    scores = jnp.einsum("ctn,csn->cts", query_c, keys_b, precision=SCAN_PRECISION)
    lower_mask = (
        lax.broadcasted_iota(jnp.int32, (Q, Q), 0) >= lax.broadcasted_iota(jnp.int32, (Q, Q), 1)
    )[None, :, :, None]
    log_gaps = cumulative[:, :, None, :] - cumulative[:, None, :, :]
    within = jnp.where(lower_mask, jnp.exp(jnp.where(lower_mask, log_gaps, 0.0)), 0.0)
    inside = jnp.einsum(
        "ctsh,cshp->cthp", scores[:, :, :, None] * within, scaled, precision=SCAN_PRECISION
    )
    closing = cumulative[:, -1:, :]
    states = jnp.einsum(
        "csn,cshp->chnp",
        keys_b,
        jnp.exp(closing - cumulative)[:, :, :, None] * scaled,
        precision=SCAN_PRECISION,
    )
    passing = jnp.exp(closing[:, 0, :])

    def advance(running, element):
        block_state, factor = element
        return (factor[:, None, None] * running + block_state, running)

    _, entering = lax.scan(
        advance, jnp.zeros((heads_here, N, P_SIZE), jnp.float32), (states, passing)
    )
    across = (
        jnp.einsum("ctn,chnp->cthp", query_c, entering, precision=SCAN_PRECISION)
        * jnp.exp(cumulative)[:, :, :, None]
    )
    return (inside + across).reshape(extent, heads_here, P_SIZE)


def mix_sequence(values, states_in, dt_steps, decay_log, skip_gain):
    heads_here = decay_log.shape[0]
    decay_rate = -jnp.exp(decay_log)
    per_head = values.reshape(values.shape[0], heads_here, P_SIZE)
    forward_part = span_scan(
        per_head, states_in[:, :N], states_in[:, N : 2 * N], dt_steps[:, 0], decay_rate
    )
    reverse_part = jnp.flip(
        span_scan(
            jnp.flip(per_head, 0),
            jnp.flip(states_in[:, 2 * N : 3 * N], 0),
            jnp.flip(states_in[:, 3 * N :], 0),
            jnp.flip(dt_steps[:, 1], 0),
            decay_rate,
        ),
        0,
    )
    nothing = jnp.zeros_like(forward_part[:1])
    mixed = (
        jnp.concatenate([nothing, forward_part[:-1]], 0)
        + jnp.concatenate([reverse_part[1:], nothing], 0)
        + skip_gain[None, :, None] * per_head
    )
    return mixed.reshape(values.shape[0], -1)


def mixer(values, states_in, step_values, decay_now, skip_now):
    return jax.vmap(mix_sequence, in_axes=(0, 0, 0, None, None))(
        values, states_in, step_values, decay_now, skip_now
    )


def rounded(values):
    return lax.optimization_barrier(values.astype(jnp.bfloat16)).astype(jnp.float32)


def on_device(
    hidden_in,
    teacher,
    loss_mask,
    lengths,
    dealing,
    norm_gain,
    w_gate,
    w_value,
    w_state,
    w_step,
    step_bias,
    conv_value,
    conv_vbias,
    conv_state,
    conv_sbias,
    decay_log,
    skip_gain,
    out_gain,
    w_out,
):
    groups = lax.axis_size("dp")
    dp_rank = lax.axis_index("dp")
    splits = lax.axis_size("tensor")
    member = lax.axis_index("tensor")
    seqs_all, local_len, _ = hidden_in.shape
    half_width = teacher.shape[2]
    seq_here = seqs_all // groups
    full_len = local_len * groups
    row_count = seq_here * full_len
    inner_here = w_gate.shape[1]
    heads_here = decay_log.shape[0]
    arrival_pos = dp_rank * local_len + lax.broadcasted_iota(jnp.int32, (seqs_all, local_len), 1)
    marks_in = (loss_mask * (arrival_pos < lengths[:, None]).astype(jnp.int32)).astype(jnp.float32)
    token_total = lax.psum(jnp.sum(marks_in), "dp")
    order_marks = marks_in[dealing].astype(jnp.bfloat16)
    order_goal = teacher[dealing]
    arrived, targets, dealt_marks = (
        lax.all_to_all(hidden_in[dealing], "dp", split_axis=0, concat_axis=1, tiled=True),
        lax.all_to_all(order_goal, "dp", split_axis=0, concat_axis=1, tiled=True),
        lax.all_to_all(order_marks, "dp", split_axis=0, concat_axis=1, tiled=True),
    )
    dealt_lengths = lax.dynamic_slice_in_dim(lengths[dealing], dp_rank * seq_here, seq_here)
    live_tok = (
        lax.broadcasted_iota(jnp.int32, (seq_here, full_len), 1) < dealt_lengths[:, None]
    ).astype(jnp.float32)
    inputs = arrived.astype(jnp.float32)
    inv_rms = lax.rsqrt(jnp.mean(inputs * inputs, -1, keepdims=True) + EPSILON)
    normed_raw = inputs * inv_rms
    normed = (normed_raw * norm_gain).astype(jnp.bfloat16)
    flat_in = normed.reshape(row_count, -1)
    joint = jnp.concatenate([w_gate, w_value, w_step.reshape(w_step.shape[0], -1)], 1)
    head_proj = jnp.dot(flat_in, joint, preferred_element_type=jnp.float32)
    state_pre = jnp.dot(flat_in, w_state, preferred_element_type=jnp.float32)
    gate_pre = head_proj[:, :inner_here].reshape(seq_here, full_len, inner_here)
    conv_in = jnp.concatenate([head_proj[:, inner_here : 2 * inner_here], state_pre], 1).reshape(
        seq_here, full_len, -1
    )
    raw_step = head_proj[:, 2 * inner_here :].reshape(seq_here, full_len, 2, heads_here) + step_bias
    kernel = jnp.concatenate([conv_value, conv_state], 1)
    pre_act = causal_conv(conv_in, kernel, jnp.concatenate([conv_vbias, conv_sbias], 0))
    activated = rounded(jax.nn.silu(pre_act))
    dt_steps = jax.nn.softplus(raw_step) * live_tok[:, :, None, None]
    mixed, mixer_back = jax.vjp(
        mixer,
        activated[..., :inner_here],
        activated[..., inner_here:],
        dt_steps,
        decay_log,
        skip_gain,
    )
    gate_act = jax.nn.silu(gate_pre)
    gated = mixed * gate_act
    square_sum = lax.psum(jnp.sum(gated * gated, -1), "tensor")
    out_inv = lax.rsqrt(square_sum / INNER + EPSILON)[..., None]
    scaled_g = gated * out_inv
    branch = (scaled_g * out_gain).astype(jnp.bfloat16).reshape(row_count, inner_here)
    partial_out = jnp.dot(branch, w_out, preferred_element_type=jnp.float32)
    out_half = lax.psum_scatter(partial_out, "tensor", scatter_dimension=1, tiled=True)
    own_input = lax.dynamic_slice_in_dim(
        inputs.reshape(row_count, -1), member * half_width, half_width, 1
    )
    result = own_input + out_half
    layer_out = result.astype(jnp.bfloat16).reshape(seq_here, full_len, half_width)
    factor_scale = row_count / token_total
    d_layer = (
        (result - targets.reshape(row_count, half_width).astype(jnp.float32))
        * dealt_marks.reshape(row_count, 1).astype(jnp.float32)
        * factor_scale
    )
    d_out = d_layer.astype(jnp.bfloat16)
    piece = lax.all_gather(d_out, "tensor", axis=1, tiled=True)
    d_branch_now = lax.dot_general(
        piece, w_out, (((1,), (1,)), ((), ())), preferred_element_type=jnp.float32
    )
    added = lax.dot_general(
        branch, piece, (((0,), (0,)), ((), ())), preferred_element_type=jnp.float32
    )
    d_branch = d_branch_now
    d_branch = d_branch.reshape(seq_here, full_len, inner_here)
    grad_out_gain = jnp.sum(d_branch * scaled_g, (0, 1))
    upstream = d_branch * out_gain
    dot_sum = lax.psum(jnp.sum(upstream * gated, -1), "tensor")
    d_gated = out_inv * upstream - gated * out_inv**3 * dot_sum[..., None] / INNER
    d_mixed = d_gated * gate_act
    d_gate = d_gated * mixed * silu_slope(gate_pre)
    d_values, d_states, d_dt, grad_decay, grad_skip = mixer_back(d_mixed)
    d_raw = d_dt * live_tok[:, :, None, None] * jax.nn.sigmoid(raw_step)
    grad_step_bias = jnp.sum(d_raw, (0, 1))
    d_pre = jnp.concatenate([d_values, d_states], -1) * silu_slope(pre_act)
    conv_width = kernel.shape[0]
    padded_in = jnp.pad(conv_in, ((0, 0), (conv_width - 1, 0), (0, 0)))
    padded_grad = jnp.pad(d_pre, ((0, 0), (0, conv_width - 1), (0, 0)))
    grad_kernel = jnp.stack(
        [
            jnp.sum(d_pre * padded_in[:, offset : offset + full_len], (0, 1))
            for offset in range(conv_width)
        ],
        0,
    )
    grad_conv_bias = jnp.sum(d_pre, (0, 1))
    d_conv_in = jnp.zeros_like(d_pre)
    for offset in range(conv_width):
        start_at = conv_width - 1 - offset
        d_conv_in = d_conv_in + kernel[offset] * padded_grad[:, start_at : start_at + full_len]
    d_heads = jnp.concatenate(
        [
            d_gate.reshape(row_count, -1),
            d_conv_in[..., :inner_here].reshape(row_count, -1),
            d_raw.reshape(row_count, -1),
        ],
        1,
    ).astype(jnp.bfloat16)
    share = row_count // splits
    row_start = member * share
    d_state_part = lax.psum_scatter(
        d_conv_in[..., inner_here:].reshape(row_count, -1),
        "tensor",
        scatter_dimension=0,
        tiled=True,
    ).astype(jnp.bfloat16)
    grad_joint = lax.dot_general(
        flat_in, d_heads, (((0,), (0,)), ((), ())), preferred_element_type=jnp.float32
    )
    own_rows = lax.dynamic_slice_in_dim(flat_in, row_start, share, 0)
    grad_state = lax.dot_general(
        own_rows, d_state_part, (((0,), (0,)), ((), ())), preferred_element_type=jnp.float32
    )
    d_normed = lax.dot_general(
        d_heads, joint, (((1,), (1,)), ((), ())), preferred_element_type=jnp.float32
    )
    state_back = lax.dot_general(
        d_state_part, w_state, (((1,), (1,)), ((), ())), preferred_element_type=jnp.float32
    )
    d_normed = lax.dynamic_update_slice_in_dim(
        d_normed, lax.dynamic_slice_in_dim(d_normed, row_start, share, 0) + state_back, row_start, 0
    )
    grad_norm_part = jnp.sum(d_normed * normed_raw.reshape(row_count, -1), 0)
    d_normed_half = lax.psum_scatter(d_normed, "tensor", scatter_dimension=1, tiled=True)
    gain_half = lax.dynamic_slice_in_dim(norm_gain, member * half_width, half_width, 0)
    upstream_in = d_normed_half * gain_half
    dot_in = lax.psum(jnp.sum(upstream_in * own_input, -1), "tensor")
    inv_flat = inv_rms.reshape(row_count, 1)
    d_input = inv_flat * upstream_in - own_input * inv_flat**3 * dot_in[:, None] / D + d_layer
    returned = lax.all_to_all(
        d_input.astype(jnp.bfloat16).reshape(seq_here, full_len, half_width),
        "dp",
        split_axis=1,
        concat_axis=0,
        tiled=True,
    )
    inverse = (
        jnp.zeros((seqs_all,), jnp.int32)
        .at[dealing]
        .set(lax.broadcasted_iota(jnp.int32, (seqs_all,), 0))
    )
    grad_in = returned[inverse]
    grad_gate = grad_joint[:, :inner_here]
    grad_value = grad_joint[:, inner_here : 2 * inner_here]
    grad_step = grad_joint[:, 2 * inner_here :].reshape(w_step.shape)
    heads_sum = lax.psum(
        (
            grad_gate,
            grad_value,
            grad_step,
            grad_step_bias,
            grad_kernel[:, :inner_here],
            grad_conv_bias[:inner_here],
            grad_decay,
            grad_skip,
            grad_out_gain,
            added,
        ),
        "dp",
    )
    shared_sum = lax.psum(
        (grad_norm_part, grad_state, grad_kernel[:, inner_here:], grad_conv_bias[inner_here:]),
        ("dp", "tensor"),
    )
    return (
        layer_out,
        grad_in,
        shared_sum[0],
        heads_sum[0],
        heads_sum[1],
        shared_sum[1],
        heads_sum[2],
        heads_sum[3],
        heads_sum[4],
        heads_sum[5],
        shared_sum[2],
        shared_sum[3],
        heads_sum[6],
        heads_sum[7],
        heads_sum[8],
        heads_sum[9],
    )


def solution(mesh):
    return jax.shard_map(
        on_device,
        mesh=mesh,
        in_specs=(
            P(None, "dp", None),
            P(None, "dp", "tensor"),
            P(None, "dp"),
            P(),
            P(),
            P(),
            P(None, "tensor"),
            P(None, "tensor"),
            P(),
            P(None, None, "tensor"),
            P(None, "tensor"),
            P(None, "tensor"),
            P("tensor"),
            P(),
            P(),
            P("tensor"),
            P("tensor"),
            P("tensor"),
            P("tensor", None),
        ),
        out_specs=(
            P("dp", None, "tensor"),
            P(None, "dp", "tensor"),
            P(),
            P(None, "tensor"),
            P(None, "tensor"),
            P(),
            P(None, None, "tensor"),
            P(None, "tensor"),
            P(None, "tensor"),
            P("tensor"),
            P(),
            P(),
            P("tensor"),
            P("tensor"),
            P("tensor"),
            P("tensor", None),
        ),
        check_vma=False,
    )
```

profile of v0, /device:TPU:0, one launch (start us, length us, event | category | flops | bytes accessed | tf_op | source)
XLA Modules:
  0.0 1261.1 jit_solution(6160384283023629927)
XLA Ops:
  10.5 8.4 all-to-all-start
  21.9 31.2 %all-to-all-done = bf16[16,64,768]{2,1,0:T(8,128)(2,1)S(1)} async-done(((bf16[16,64,768]{2,1,0:T(8,128)(2,1)}), bf16[16,64,768]{2,1,0:T(8,128)(2,1)S(1)}, u32[]{:S(2)}, u32[]{:S(2)}) %all-to-all-start) | async-done | bytes 1572896 | tf_op jit(solution)/shard_map/all_to_all | solution.py:150
  62.6 23.5 %fusion.239 = f32[1,8,128,12]{3,1,2,0:T(8,128)S(1)} fusion(f32[1,8,128,12]{3,1,2,0:T(8,128)S(1)} %copy.563), kind=kOutput, calls=%fused_computation.363 | output fusion | flops 1560576 | bytes 98304 | tf_op jit(solution)/shard_map/jvp(vmap(jit(cumsum)))/reduce_window_sum | solution.py:40
  133.8 27.5 %while.68 = (s32[]{:T(128)}, f32[1,12,64,64]{3,2,1,0:T(8,128)S(1)}, f32[8,1,12,64,64]{4,3,2,1,0:T(8,128)}, f32[8,1,12,1,1]{2,4,3,1,0:T(1,128)S(1)}, f32[8,1,12]{...) while((s32[]{:T(128)}, f32[1,12,64,64]{3,2,1,0:T(8,128)S(1)}, ...), condition=%wide.region_3.4_spmd.clone, body=%wide.region_2.0_spmd.clone.sunk | while | flops 196611 | bytes 1966904 | solution.py:66
  179.3 16.0 %copy.576 = f32[1,1024,12,64]{1,0,3,2:T(1,128)} copy(f32[1,1024,12,64]{1,3,2,0:T(8,128)S(1)} %bitcast.570) | data formatting | bytes 6291456 | tf_op jit(solution)/shard_map/jvp(vmap())/reshape | solution.py:79
  195.3 33.0 %rev.34 = f32[1,1024,12,64]{1,0,3,2:T(1,128)} reverse(f32[1,1024,12,64]{1,0,3,2:T(1,128)} %copy.576), dimensions={1} | reverse | bytes 6291456 | tf_op jit(solution)/shard_map/jvp(vmap(jit(_flip)))/rev | solution.py:85
  239.9 17.1 %while.69 = (s32[]{:T(128)}, f32[1,12,64,64]{3,2,1,0:T(8,128)S(1)}, f32[8,1,12,64,64]{4,3,2,1,0:T(8,128)}, f32[8,1,12,1,1]{2,4,3,1,0:T(1,128)S(1)}, f32[8,1,12]{...) while((s32[]{:T(128)}, f32[1,12,64,64]{3,2,1,0:T(8,128)S(1)}, ...), condition=%wide.region_6.7_spmd.clone, body=%wide.region_5.6_spmd.clone.sunk | while | flops 196611 | bytes 1967368 | solution.py:66
  275.5 33.4 %reverse.1 = f32[1,1024,12,64]{1,0,3,2:T(1,128)} reverse(f32[1,1024,12,64]{1,0,3,2:T(1,128)} %bitcast.585), dimensions={1} | reverse | bytes 6291456
  309.0 8.6 slice.252
  317.6 8.1 multiply_add_fusion.1
  342.5 7.8 all-to-all-start.2
  361.8 46.7 %psum.127 = f32[]{:T(128)} all-reduce(f32[]{:T(128)} %get-tuple-element.849), channel_id=1, replica_groups=mesh['dp'=16,'tensor'=2] {'dp'}, use_global_device_ids=true, to_apply=%region_11.12 | all-reduce | flops 1 | bytes 8 | tf_op jit(solution)/shard_map/psum | solution.py:146
  442.4 8.3 pad.42
  450.7 33.0 %rev.38 = f32[1,1024,12,64]{1,0,3,2:T(1,128)S(1)} reverse(f32[1,1024,12,64]{1,0,3,2:T(1,128)} %pad.42), dimensions={1} | reverse | bytes 6291456 | tf_op jit(solution)/shard_map/transpose(jvp(vmap(jit(_flip))))/rev | solution.py:83
  508.2 65.5 %while.71 = (s32[]{:T(128)}, f32[1,12,64,64]{3,2,1,0:T(8,128)}, f32[8,1,12,64,64]{4,3,2,1,0:T(8,128)}, f32[8,1,12]{2,1,0:T(1,128)S(1)}, f32[8,1,12,64,64]{3,4,2,...) while((s32[]{:T(128)}, f32[1,12,64,64]{3,2,1,0:T(8,128)}, ...), condition=%wide.region_19.20_spmd.clone, body=%wide.region_17.19_spmd.clone.sunk | while | flops 294904 | bytes 2360664 | solution.py:66
  590.0 59.8 %while.70 = (s32[]{:T(128)}, f32[1,12,64,64]{3,2,1,0:T(8,128)S(1)}, f32[8,1,12,64,64]{4,3,2,1,0:T(8,128)}, f32[8,1,12]{2,1,0:T(1,128)}, f32[8,1,12,64,64]{3,4,2,...) while((s32[]{:T(128)}, f32[1,12,64,64]{3,2,1,0:T(8,128)S(1)}, ...), condition=%wide.region_16.17_spmd.clone, body=%wide.region_14.16_spmd.clone.sunk | while | flops 294904 | bytes 2163592 | solution.py:66
  677.6 15.1 %fusion.26 = (f32[8,128,12]{1,2,0:T(8,128)}, f32[8,128,12]{1,2,0:T(8,128)}, f32[8,128,128]{2,1,0:T(8,128)S(1)}, f32[8,128,128]{2,1,0:T(8,128)S(1)}, f32[8,128,12]{1,2,0:T(8,128)}, /*index=5*/f32[8,128,12]{1,2,0:T(8,128)}) fusion(f32[8,128,128]{2,1,0:T(8,128)S(1)} %copy-done.89, f32[8,128,12]{1,2,0:T(8,128)S(1)} %copy-done.103, ...), kind=kOutput, calls=%fused_computation.77 | convolution fusion | flops 638271488 | bytes 14991360 | tf_op jit(solution)/shard_map/transpose(jvp(vmap(ctsh,cshp->cthp)))/dot_general | solution.py:50
  715.3 33.0 %rev.39 = f32[1,1024,12,64]{1,0,3,2:T(1,128)} reverse(f32[1,1024,12,64]{1,0,3,2:T(1,128)} %get-tuple-element.865), dimensions={1} | reverse | bytes 6291456 | tf_op jit(solution)/shard_map/transpose(jvp(vmap(jit(_flip))))/rev | solution.py:85
  748.3 10.5 multiply_add_fusion
  801.9 12.7 %fusion.229 = (f32[1024]{0:T(1024)}, f32[1024]{0:T(1024)S(1)}, f32[1024]{0:T(1024)S(1)}, f32[1024]{0:T(1024)}, f32[1024]{0:T(1024)}, /*index=5*/f32[1,1024,1024]{1,2,0:T(8,128)S(1)}) fusion(f32[1024,256]{0,1:T(8,128)} %copy-done.33, f32[1024,768]{0,1:T(8,128)S(1)} %copy-done.22, f32[1,1024,1024]{1,2,0:T(8,128)} %copy-done.20, ...), kind=kLoop, calls=%fused_computation.353 | loop fusion | flops 19917824 | bytes 20992000 | tf_op jit(solution)/shard_map/reduce_sum | solution.py:232
  886.4 96.0 %all-reduce.15 = (f32[2,12]{1,0:T(2,128)}, f32[4,768]{1,0:T(4,128)}, f32[768]{0:T(1024)}, f32[12]{0:T(128)}, f32[12]{0:T(128)}, /*index=5*/f32[768]{0:T(1024)}) all-reduce(f32[2,12]{1,0:T(2,128)S(1)} %copy-done.149, f32[4,768]{1,0:T(4,128)S(1)} %slice.185, f32[768]{0:T(1024)S(1)} %bitcast.648, ...), channel_id=1, replica_groups=mesh['dp'=16,'tensor'=2] {'dp'}, use_global_device_ids=true, to_apply=%region_48.49 | all-reduce | flops 4656 | bytes 37248 | tf_op jit(solution)/shard_map/psum | solution.py:292
  987.6 39.8 %all-reduce.14 = (f32[768]{0:T(1024)}, f32[4,256]{1,0:T(4,128)}, f32[256]{0:T(256)}) all-reduce(f32[768]{0:T(1024)S(1)} %multiply_reduce_fusion.5, f32[4,256]{1,0:T(4,128)S(1)} %pad_maximum_fusion.7, f32[256]{0:T(256)S(1)} %slice.151), channel_id=1, replica_groups=mesh['dp'=16,'tensor'=2] {'dp','tensor'}, use_global_device_ids=true, to_apply=%region_42.43 | all-reduce | flops 2048 | bytes 16384 | tf_op jit(solution)/shard_map/psum | solution.py:307
  1027.4 87.1 %all-reduce.22.cloned.1.call-done = (f32[768,768]{0,1:T(8,128)}, f32[768,768]{0,1:T(8,128)}, f32[768,2,12]{0,2,1:T(8,128)}, f32[768,768]{1,0:T(8,128)}) async-done(((f32[768,768]{0,1:T(8,128)}, f32[768,768]{0,1:T(8,128)}, f32[768,2,12]{0,2,1:T(8,128)}, f32[768,768]{1,0:T(8,128)}), (f32[768,768]{0,1:T(8,128)}, f32[768,768]{0,1:T(8,128)}, f32[768,2,12]{0,2,1:T(8,128)}, ...) | async-done | bytes 7151632 | tf_op jit(solution)/shard_map/psum | solution.py:292
  1123.7 124.7 %all-reduce.20.cloned.1.call-done = f32[768,256]{1,0:T(8,128)} async-done(((f32[768,256]{1,0:T(8,128)}), f32[768,256]{1,0:T(8,128)}) %all-reduce.20.cloned.1.call-update) | async-done | bytes 786448 | tf_op jit(solution)/shard_map/psum | solution.py:307
  (759 shorter events, 565.9 us)
Async XLA Ops:
  10.5 43.1 %copy-start.130 = (f32[768]{0:T(1024)S(1)}, f32[768]{0:T(1024)}, u32[]{:S(2)}) copy-start(f32[768]{0:T(1024)} %param.32) | copy-start | bytes 9220
  10.5 42.6 %all-to-all-start = ((bf16[16,64,768]{2,1,0:T(8,128)(2,1)}), bf16[16,64,768]{2,1,0:T(8,128)(2,1)S(1)}, u32[]{:S(2)}, u32[]{:S(2)}) async-start(bf16[16,64,768]{2,1,0:T(8,128)(2,1)} %gather_fusion), calls=%async_computation | async-start | bytes 3145728 | tf_op jit(solution)/shard_map/all_to_all | solution.py:150
  18.9 392.3 %reduce-scatter.4.cloned.1.call-start = ((), (), s32[]{:S(2)}) async-start(), calls=%async_computation.7 | async-start | bytes 4718592 | tf_op jit(solution)/shard_map/reduce_scatter | solution.py:190
  19.9 34.1 %copy-start.97 = (bf16[768,24]{1,0:T(8,128)(2,1)}, bf16[768,24]{1,0:T(8,128)(2,1)S(1)}, u32[]{:S(2)}) copy-start(bf16[768,24]{1,0:T(8,128)(2,1)S(1)} %copy.558) | copy-start | bytes 110596
  21.2 39.6 %copy-start.122 = (f32[1024]{0:T(1024)}, f32[1024]{0:T(1024)S(1)}, u32[]{:S(2)}) copy-start(f32[1024]{0:T(1024)S(1)} %fusion.212) | copy-start | bytes 12292
  21.9 66.3 %copy-start.145 = (f32[12]{0:T(128)}, f32[12]{0:T(128)S(1)}, u32[]{:S(2)}) copy-start(f32[12]{0:T(128)S(1)} %exponential_negate_fusion) | copy-start | bytes 148
  21.9 74.6 %copy-start.108 = (f32[1,1024]{1,0:T(1,128)}, f32[1,1024]{1,0:T(1,128)S(1)}, u32[]{:S(2)}) copy-start(f32[1,1024]{1,0:T(1,128)S(1)} %get-tuple-element.888) | copy-start | bytes 12292
  21.9 74.6 %copy-start.110 = (f32[1,1024]{1,0:T(1,128)}, f32[1,1024]{1,0:T(1,128)S(1)}, u32[]{:S(2)}) copy-start(f32[1,1024]{1,0:T(1,128)S(1)} %get-tuple-element.889) | copy-start | bytes 12292
  21.9 74.6 %copy-start.112 = (f32[1,1024]{1,0:T(1,128)}, f32[1,1024]{1,0:T(1,128)S(1)}, u32[]{:S(2)}) copy-start(f32[1,1024]{1,0:T(1,128)S(1)} %get-tuple-element.890) | copy-start | bytes 12292
  21.9 74.6 %copy-start.114 = (f32[1,1024]{1,0:T(1,128)}, f32[1,1024]{1,0:T(1,128)S(1)}, u32[]{:S(2)}) copy-start(f32[1,1024]{1,0:T(1,128)S(1)} %get-tuple-element.891) | copy-start | bytes 12292
  53.1 356.2 %copy-start.18 = (bf16[16,64,768]{2,1,0:T(8,128)(2,1)}, bf16[16,64,768]{2,1,0:T(8,128)(2,1)S(1)}, u32[]{:S(2)}) copy-start(bf16[16,64,768]{2,1,0:T(8,128)(2,1)S(1)} %all-to-all-done) | copy-start | bytes 4718596
  118.0 47.3 %copy-start.50 = (bf16[8,8,8,128]{3,2,1,0:T(8,128)(2,1)}, bf16[8,8,8,128]{3,2,1,0:T(8,128)(2,1)S(1)}, u32[]{:S(2)}) copy-start(bf16[8,8,8,128]{3,2,1,0:T(8,128)(2,1)S(1)} %copy.702) | copy-start | bytes 393220
  125.6 135.1 %copy-start.43 = (f32[8,8,8,128]{3,2,1,0:T(8,128)}, f32[8,8,8,128]{3,2,1,0:T(8,128)S(1)}, u32[]{:S(2)}) copy-start(f32[8,8,8,128]{3,2,1,0:T(8,128)S(1)} %copy.705) | copy-start | bytes 786436
  342.5 15.0 %all-to-all-start.2 = ((bf16[16,1,64]{2,1,0:T(2,128)(2,1)}), bf16[16,1,64]{2,1,0:T(2,128)(2,1)S(1)}, u32[]{:S(2)}, u32[]{:S(2)}) async-start(bf16[16,1,64]{2,1,0:T(2,128)(2,1)} %copy.594), calls=%async_computation.3 | async-start | bytes 16384 | tf_op jit(solution)/shard_map/all_to_all | solution.py:152
  357.5 53.8 %all-to-all-start.1 = ((bf16[16,64,384]{2,1,0:T(8,128)(2,1)}), bf16[16,64,384]{2,1,0:T(8,128)(2,1)}, u32[]{:S(2)}, u32[]{:S(2)}) async-start(bf16[16,64,384]{2,1,0:T(8,128)(2,1)} %gather_fusion.2), calls=%async_computation.2 | async-start | bytes 1572864 | tf_op jit(solution)/shard_map/all_to_all | solution.py:151
  361.8 61.0 %all-gather.2.cloned.1.call-start = ((), (), s32[]{:S(2)}) async-start(), calls=%async_computation.8 | async-start | bytes 2359296 | tf_op jit(solution)/shard_map/all_gather | solution.py:203
  415.3 423.9 %reduce-scatter.6.cloned.1.call-start = ((), (), s32[]{:S(2)}) async-start(), calls=%async_computation.9 | async-start | bytes 1572864 | tf_op jit(solution)/shard_map/reduce_scatter | solution.py:247
  508.2 65.5 %copy-start.5 = (f32[96,8,8,128]{3,2,1,0:T(8,128)S(1)}, f32[96,8,8,128]{3,2,1,0:T(8,128)}, u32[]{:S(2)}) copy-start(f32[96,8,8,128]{3,2,1,0:T(8,128)} %copy-done.3) | copy-start | bytes 9437188
  822.0 38.5 %reduce-scatter.8.cloned.1.call-start = ((), (), s32[]{:S(2)}) async-start(), calls=%async_computation.10 | async-start | bytes 4718592 | tf_op jit(solution)/shard_map/reduce_scatter | solution.py:270
  842.3 272.1 %all-reduce.22.cloned.1.call-start = ((), (), s32[]{:S(2)}) async-start(), calls=%async_computation.12 | async-start | bytes 14352384 | tf_op jit(solution)/shard_map/psum | solution.py:292
  871.3 111.1 %copy-start.59 = (f32[512,256]{0,1:T(8,128)S(1)}, f32[512,256]{0,1:T(8,128)}, u32[]{:S(2)}) copy-start(f32[512,256]{0,1:T(8,128)} %reduce-scatter.6.cloned.1.call-done) | copy-start | bytes 1572868
  877.3 108.0 %copy-start.19 = (bf16[16,64,768]{2,1,0:T(8,128)(2,1)S(1)}, bf16[16,64,768]{2,1,0:T(8,128)(2,1)}, u32[]{:S(2)}) copy-start(bf16[16,64,768]{2,1,0:T(8,128)(2,1)} %copy-done.18) | copy-start | bytes 4718596
  878.3 243.0 %all-to-all-start.3 = ((bf16[16,2,12288]{2,1,0:T(2,128)(2,1)}), bf16[16,2,12288]{2,1,0:T(2,128)(2,1)S(1)}, u32[]{:S(2)}, u32[]{:S(2)}) async-start(bf16[16,2,12288]{2,1,0:T(2,128)(2,1)} %reshape.1455), calls=%async_computation.6 | async-start | bytes 1572864 | tf_op jit(solution)/shard_map/all_to_all | solution.py:276
  885.2 363.3 %all-reduce.20.cloned.1.call-start = ((), (), s32[]{:S(2)}) async-start(), calls=%async_computation.11 | async-start | bytes 1572864 | tf_op jit(solution)/shard_map/psum | solution.py:307
  (155 other events, 1165.3 us)
Sparse Core Ops, SparseCore 0:
  339.9 12.9 reduce-scatter.3
  415.4 7.3 all-gather.1
  822.2 9.7 reduce-scatter.5
  842.5 12.1 reduce-scatter.7
  863.2 251.2 all-reduce.21
  1120.3 128.0 all-reduce.19
where the time goes:
time: 1280 us; the launch traced here: 1260 us
  local copies, waits for them, and re-layouts  434 us (34%)
  waiting for transfers between devices  255 us (20%)
  other arithmetic  205 us (16%)
  blocking collectives  190 us (15%)
  matrix products  132 us (10%)
  starting transfers between devices  27.6 us (2%)
  between operations  17.4 us (1%)
    psum x1, waiting for transfers between devices, on_device(): lax.psum((grad_norm_part, grad_state, grad_kernel[:, inner_here:], grad_c...  125 us
    psum x1, blocking collectives, on_device(): lax.psum((grad_gate, grad_value, grad_step, grad_step_bias, grad_kernel[:...  96 us
    unnamed x364, local copies, waits for them, and re-layouts  91.7 us
    psum x1, waiting for transfers between devices, on_device(): lax.psum((grad_gate, grad_value, grad_step, grad_step_bias, grad_kernel[:...  87.1 us
    dynamic_slice x64, local copies, waits for them, and re-layouts, span_scan(): lax.scan(advance, jnp.zeros((heads_here, N, P_SIZE), jnp.float32), (state...  77.9 us
    rev x2, local copies, waits for them, and re-layouts, mix_sequence(): jnp.flip(per_head, 0)  66.1 us
    psum x1, blocking collectives, on_device(): token_total = lax.psum(jnp.sum(marks_in), 'dp')  46.7 us
    dot_general x6, matrix products, span_scan(): jnp.einsum('ctsh,cshp->cthp', scores[:, :, :, None] * within, scaled, pre...  46.5 us
  transfers between devices with their start and end apart: 10, of which 5 were waited for; matrix products, arithmetic and copies ran while one was open for 5% of the time, Pallas kernels for 0%

commit v1 on v0

v1 whole, which is shorter than its diff:
```python
import jax
import jax.numpy as jnp
from jax import lax
from jax.experimental import pallas as pl
from jax.experimental.pallas import tpu as pltpu
from jax.sharding import PartitionSpec as P

D = 768
INNER = 1536
PS = 64
N = 64
Q = 128
EPS = 1e-5
NOMARK = 256.0
BF = jnp.bfloat16
F32 = jnp.float32
HI = lax.Precision.HIGHEST
VMEM_LIMIT = 58 * 1024 * 1024

NN = (((1,), (0,)), ((), ()))
NT = (((1,), (1,)), ((), ()))


def mm(a, b, dims=NN):
    return lax.dot_general(a, b, dims, preferred_element_type=F32)


def mm_hi(a, b):
    return lax.dot_general(a, b, NN, precision=HI, preferred_element_type=F32)


def lanes(c, width=Q):
    return pl.ds(pl.multiple_of(c * width, width), width)


def iota2(shape, dim):
    return lax.broadcasted_iota(jnp.int32, shape, dim)


def log1p_exp(z):
    w = 1.0 + z
    return jnp.where(w == 1.0, z, jnp.log(w) * (z / jnp.where(w == 1.0, 1.0, w - 1.0)))


RAW, DT, CUM, CUE, ROWV, INV = 0, 24, 48, 72, 96, 120


def deal_kernel(dealing, src, dst):
    count, _, width = dst.shape
    if src.shape[2] == width:
        col = pl.ds(0, width)
    else:
        col = pl.ds(pl.multiple_of(lax.axis_index("tensor") * width, width), width)

    @pl.loop(0, count)
    def _(j):
        dst[j] = src[dealing[j], :, col]


def undeal_kernel(dealing, src, dst):
    @pl.loop(0, dst.shape[0])
    def _(j):
        dst[dealing[j]] = src[j]


def forward_kernel(
    length, xo, xs, wt, wot, cc, cd, rc,
    xT, nT, rows, dec, gate, uO, preO, act, cs, eO, mixed, sin, pO, pF,
    u_s, raw_s, w_s, dS, run, vw, bu,
):
    T = xo.shape[0]
    CH = T // Q
    C = gate.shape[0]
    HH = C // PS
    half = xo.shape[1]
    m = lax.axis_index("tensor")
    own = pl.multiple_of(m * half, half)
    other = pl.multiple_of((1 - m) * half, half)

    @pl.loop(0, CH)
    def _(c):
        l = lanes(c)
        xT[pl.ds(own, half), l] = xo[l, :].astype(F32).T.astype(BF)
        xT[pl.ds(other, half), l] = xs[l, :].astype(F32).T.astype(BF)
        x = xT[:, l].astype(F32)
        inv = lax.rsqrt(jnp.sum(x * x, 0, keepdims=True) / D + EPS)
        rows[INV : INV + 8, l] = jnp.broadcast_to(inv, (8, Q))
        nT[:, l] = (x * inv * cd[:, 0:1]).astype(BF)

    @pl.loop(0, T // 256)
    def _(j):
        l = lanes(j, 256)
        n = nT[:, l]
        gate[:, l] = mm(wt[0:C, :], n)
        u_s[:, l] = mm(wt[C : 2 * C + 256, :], n)
        raw_s[:, l] = mm(wt[2 * C + 256 : 2 * C + 288, :], n)

    raw = raw_s[0:24, :] + rc[:, 0:1]
    live = (iota2((1, T), 1) < length[0]).astype(F32)
    dt = (jnp.maximum(raw, 0.0) + log1p_exp(jnp.exp(-jnp.abs(raw)))) * live
    la = dt * rc[:, 1:2]
    rows[RAW : RAW + 24, :] = raw
    rows[DT : DT + 24, :] = dt
    upper = (iota2((Q, Q), 0) <= iota2((Q, Q), 1)).astype(F32)
    lower = (iota2((Q, Q), 0) >= iota2((Q, Q), 1)).astype(F32)
    stacked = jnp.concatenate([la[:, c * Q : (c + 1) * Q] for c in range(CH)], 0)
    cum_f = mm_hi(stacked, upper)
    cum_b = mm_hi(stacked, lower)
    first = iota2((24, Q), 0) < HH
    for c in range(CH):
        r = slice(24 * c, 24 * c + 24)
        k = slice(Q * c, Q * c + Q)
        cum = jnp.where(first, cum_f[r], cum_b[r])
        dtc = dt[:, k]
        rows[CUM : CUM + 24, k] = cum
        rows[CUE : CUE + 24, k] = cum - la[:, k]
        rows[ROWV : ROWV + 24, k] = jnp.where(
            dtc > 0.0, cum - jnp.log(jnp.where(dtc > 0.0, dtc, 1.0)), 1e30
        )
        tot = jnp.broadcast_to(jnp.sum(la[:, k], 1, keepdims=True), (24, Q))
        dec[c] = jnp.exp(tot)
        w_s[:, k] = jnp.exp(tot - cum) * dtc

    at = iota2((64, T), 1)

    @pl.loop(0, u_s.shape[0] // 64)
    def _(b):
        r = pl.ds(pl.multiple_of(b * 64, 64), 64)
        uu = u_s[r, :]
        col = cc[r, :]
        pre = col[:, 4:5] + col[:, 3:4] * uu
        for back in (1, 2, 3):
            shifted = jnp.where(at >= back, pltpu.roll(uu, back, 1), 0.0)
            pre = pre + col[:, 3 - back : 4 - back] * shifted
        uO[r, :] = uu.astype(BF)
        preO[r, :] = pre.astype(BF)
        act[r, :] = (pre * jax.nn.sigmoid(pre)).astype(BF)

    cs[0:64, :] = pltpu.roll(act[C + 64 : C + 128, :].astype(F32), 1, 1).astype(BF)
    cs[64:128, :] = pltpu.roll(act[C + 192 : C + 256, :].astype(F32), T - 1, 1).astype(BF)

    zeros = jnp.zeros((64, Q), BF)

    @pl.loop(0, CH)
    def _(c):
        l = lanes(c)
        for h in range(HH):
            v = act[64 * h : 64 * h + 64, l].astype(F32)
            vw[64 * h : 64 * h + 64, 0:Q] = (v * w_s[h : h + 1, l]).astype(BF)
            vw[64 * h : 64 * h + 64, Q : 2 * Q] = (v * w_s[HH + h : HH + h + 1, l]).astype(BF)
        both = jnp.concatenate(
            [
                jnp.concatenate([act[C : C + 64, l], zeros], 1),
                jnp.concatenate([zeros, act[C + 128 : C + 192, l]], 1),
            ],
            0,
        )
        dS[c] = mm(vw[...], both, NT)

    run[...] = jnp.zeros_like(run)
    low = iota2((64, Q), 1) < 64
    low_h = iota2((HH, Q), 1) < 64

    @pl.loop(0, CH)
    def _(i):
        d = jnp.where(low_h, dec[i][0:HH], dec[CH - 1 - i][HH : 2 * HH])
        for h in range(HH):
            r = slice(64 * h, 64 * h + 64)
            now = run[r, :]
            sin[i, r, :] = now.astype(BF)
            run[r, :] = now * d[h : h + 1] + jnp.where(low, dS[i, r, :], dS[CH - 1 - i, r, :])

    before = iota2((Q, Q), 1) < iota2((Q, Q), 0)
    after = iota2((Q, Q), 1) > iota2((Q, Q), 0)
    top = iota2((Q, Q), 0) < 64

    @pl.loop(0, CH)
    def _(c):
        l = lanes(c)
        bf = act[C : C + 64, l]
        bb = act[C + 128 : C + 192, l]
        cf = cs[0:64, l]
        cb = cs[64:128, l]
        gf = mm(cf.astype(F32).T.astype(BF), bf)
        gb = mm(cb.astype(F32).T.astype(BF), bb)
        g = jnp.where(before, gf, jnp.where(after, gb, 0.0))
        cue = rows[CUE : CUE + 24, l]
        cols = jnp.concatenate([cue, jnp.zeros((Q - 24, Q), F32)], 0).T
        ecue = jnp.exp(cue)
        zc = jnp.zeros((64, Q), BF)
        yf = mm(sin[c], jnp.concatenate([cf, zc], 0))
        yb = mm(sin[CH - 1 - c], jnp.concatenate([zc, cb], 0))
        total = jnp.zeros((1, Q), F32)
        for j in range(HH // 2):
            ms = []
            for h in (2 * j, 2 * j + 1):
                gap = jnp.where(
                    before,
                    cols[:, h : h + 1] - rows[ROWV + h : ROWV + h + 1, l],
                    cols[:, HH + h : HH + h + 1] - rows[ROWV + HH + h : ROWV + HH + h + 1, l],
                )
                e = jnp.exp(jnp.where(before | after, gap, -1e30))
                eO[c, h] = e.astype(BF)
                ms.append((e * g).astype(BF))
            v = act[128 * j : 128 * j + 128, l]
            vz = jnp.zeros_like(v)
            pair = jnp.concatenate([jnp.where(top, v, vz), jnp.where(top, vz, v)], 1)
            y = mm(pair, jnp.concatenate(ms, 1), NT)
            for k in (0, 1):
                h = 2 * j + k
                r = slice(64 * h, 64 * h + 64)
                mix = (
                    y[64 * k : 64 * k + 64]
                    + ecue[h : h + 1] * yf[r]
                    + ecue[HH + h : HH + h + 1] * yb[r]
                    + cc[r, 5:6] * v[64 * k : 64 * k + 64].astype(F32)
                )
                mixed[r, l] = mix
                gt = gate[r, l]
                gated = mix * (gt * jax.nn.sigmoid(gt))
                total = total + jnp.sum(gated * gated, 0, keepdims=True)
                bu[r, l] = (gated * cc[r, 6:7]).astype(BF)
        pF[D : D + 8, l] = jnp.broadcast_to(total, (8, Q))
        top_part = total.astype(BF).astype(F32)
        pO[D : D + 16, l] = jnp.where(
            iota2((16, Q), 0) == 0, top_part, jnp.where(iota2((16, Q), 0) == 1, total - top_part, 0.0)
        ).astype(BF)

    @pl.loop(0, T // 256)
    def _(j):
        l = lanes(j, 256)
        part = mm(wot[...], bu[:, l])
        pF[0:D, l] = part
        pO[0:D, l] = part.astype(BF)


def middle_kernel(
    scale, p0, p1, xT, to, ts, wo, wg, nT, gate, mixed, act, cc, cd,
    lo, doT, dyT, dgate, small, m0, m1, m2, m3,
    res_s, tea_s, branch, dbr, dot_s, acc_g, acc_s, q_s,
):
    T = to.shape[0]
    CH = T // Q
    C = gate.shape[0]
    half = to.shape[1]
    m = lax.axis_index("tensor")
    own = pl.multiple_of(m * half, half)
    other = pl.multiple_of((1 - m) * half, half)

    @pl.loop(0, CH)
    def _(c):
        l = lanes(c)
        tea_s[pl.ds(own, half), :] = to[l, :].astype(F32).T
        tea_s[pl.ds(other, half), :] = ts[l, :].astype(F32).T
        pt = p0[0:D, l] + p1[0:D, l].astype(F32)
        sums = p1[D : D + 16, l].astype(F32)
        q = lax.rsqrt((p0[D : D + 1, l] + (sums[0:1] + sums[1:2])) / INNER + EPS)
        q_s[:, l] = jnp.broadcast_to(q, (8, Q))
        res = xT[:, l].astype(F32) + q * pt
        res_s[...] = res
        tea = tea_s[...]
        do = jnp.where(tea < 0.5 * NOMARK, (res - tea) * scale[0], 0.0).astype(BF)
        doT[:, l] = do
        dot_s[:, l] = jnp.broadcast_to(jnp.sum(do.astype(F32) * pt, 0, keepdims=True), (8, Q))
        lo[l, :] = res_s[pl.ds(own, half), :].T.astype(BF)

    acc_g[...] = jnp.zeros_like(acc_g)
    acc_s[...] = jnp.zeros_like(acc_s)

    @pl.loop(0, T // 256)
    def _(j):
        l = lanes(j, 256)
        dbr[...] = mm(wo[...], doT[:, l])
        q = q_s[0:1, l]
        q3 = q * q * q * dot_s[0:1, l] / INNER

        @pl.loop(0, C // 64)
        def _(b):
            r = pl.ds(pl.multiple_of(b * 64, 64), 64)
            d = dbr[r, :]
            g = gate[r, l]
            mix = mixed[r, l]
            sg = jax.nn.sigmoid(g)
            si = g * sg
            gated = mix * si
            gain = cc[r, 6:7]
            gq = gated * q
            branch[r, l] = (gq * gain).astype(BF)
            pg = d * gq
            acc_g[r, :] += pg[:, 0:Q] + pg[:, Q : 2 * Q]
            dgt = q * (d * gain) - gated * q3
            dy = dgt * si
            dyT[r, l] = dy
            ps = dy * act[r, l].astype(F32)
            acc_s[r, :] += ps[:, 0:Q] + ps[:, Q : 2 * Q]
            dgate[r, l] = (dgt * mix * (sg * (1.0 + g * (1.0 - sg)))).astype(BF)

    lane = iota2((C, Q), 1)
    small[...] = jnp.where(
        lane == 37,
        jnp.sum(acc_s[...], 1, keepdims=True),
        jnp.where(lane == 38, jnp.sum(acc_g[...], 1, keepdims=True), 0.0),
    )

    place = lax.axis_index("dp") % 4
    share = m0.shape[0]
    for k, ref in enumerate((m0, m1, m2, m3)):
        r = pl.ds(pl.multiple_of((place ^ k) * share, share), share)
        ref[:, 0:D] = mm(branch[r, :], doT[...], NT).astype(BF)
        gg = mm(nT[r, :], dgate[...], NT)
        ref[:, D : D + C] = gg.astype(BF)
        part = jnp.sum(gg * wg[r, :].astype(F32), 1, keepdims=True) / cd[r, 0:1]
        small[r, :] = jnp.where(iota2((share, Q), 1) == 41, part, small[r, :])


def backward_kernel(
    act, cs, rows, dec, e_in, sin, dyT, cc,
    dact, c_rows, r_rows, ci_rows, ri_rows, kk,
    dA, ain, run, vw, dye,
):
    T = act.shape[1]
    CH = T // Q
    C = dyT.shape[0]
    HH = C // PS
    zeros = jnp.zeros((64, Q), BF)

    @pl.loop(0, CH)
    def _(c):
        l = lanes(c)
        ecue = jnp.exp(rows[CUE : CUE + 24, l])
        for h in range(HH):
            dy = dyT[64 * h : 64 * h + 64, l]
            dye[64 * h : 64 * h + 64, 0:Q] = (dy * ecue[h : h + 1]).astype(BF)
            dye[64 * h : 64 * h + 64, Q : 2 * Q] = (dy * ecue[HH + h : HH + h + 1]).astype(BF)
        both = jnp.concatenate(
            [
                jnp.concatenate([cs[0:64, l], zeros], 1),
                jnp.concatenate([zeros, cs[64:128, l]], 1),
            ],
            0,
        )
        dA[c] = mm(dye[...], both, NT)

    run[...] = jnp.zeros_like(run)
    low = iota2((64, Q), 1) < 64
    low_h = iota2((HH, Q), 1) < 64

    @pl.loop(0, CH)
    def _(i):
        f = CH - 1 - i
        d = jnp.where(low_h, dec[f][0:HH], dec[i][HH : 2 * HH])
        for h in range(HH):
            r = slice(64 * h, 64 * h + 64)
            now = run[r, :]
            ain[i, r, :] = now.astype(BF)
            flow = jnp.sum(now * sin[f, r, :].astype(F32), 0, keepdims=True) * d[h : h + 1]
            kk[i, h : h + 1, :] = flow
            run[r, :] = now * d[h : h + 1] + jnp.where(low, dA[f, r, :], dA[i, r, :])

    before = iota2((Q, Q), 1) < iota2((Q, Q), 0)
    after = iota2((Q, Q), 1) > iota2((Q, Q), 0)
    left = iota2((Q, Q), 1) < 64
    top = iota2((Q, Q), 0) < 64
    lane = iota2((Q, Q), 1)

    @pl.loop(0, CH)
    def _(c):
        l = lanes(c)
        bf = act[C : C + 64, l]
        bb = act[C + 128 : C + 192, l]
        cf = cs[0:64, l]
        cb = cs[64:128, l]
        gf = mm(cf.astype(F32).T.astype(BF), bf)
        gb = mm(cb.astype(F32).T.astype(BF), bb)
        g = jnp.where(before, gf, jnp.where(after, gb, 0.0))
        ecue = jnp.exp(rows[CUE : CUE + 24, l])
        w = jnp.exp(
            jnp.where(
                iota2((24, Q), 0) < HH,
                rows[CUM : CUM + 24, l][:, Q - 1 : Q],
                rows[CUM : CUM + 24, l][:, 0:1],
            )
            - rows[CUM : CUM + 24, l]
        ) * rows[DT : DT + 24, l]
        for h in range(HH):
            r = slice(64 * h, 64 * h + 64)
            dy = dyT[r, l]
            v = act[r, l].astype(F32)
            dye[r, 0:Q] = (dy * ecue[h : h + 1]).astype(BF)
            dye[r, Q : 2 * Q] = (dy * ecue[HH + h : HH + h + 1]).astype(BF)
            vw[r, 0:Q] = (v * w[h : h + 1]).astype(BF)
            vw[r, Q : 2 * Q] = (v * w[HH + h : HH + h + 1]).astype(BF)
        zc = jnp.zeros((64, Q), BF)
        sf = sin[c]
        sb = sin[CH - 1 - c]
        af = ain[CH - 1 - c]
        ab = ain[c]
        yf = mm(sf, jnp.concatenate([cf, zc], 0))
        yb = mm(sb, jnp.concatenate([zc, cb], 0))
        vf = mm(af, jnp.concatenate([bf, zc], 0))
        vb = mm(ab, jnp.concatenate([zc, bb], 0))
        dcf = mm(sf.astype(F32).T.astype(BF)[0:64], dye[:, 0:Q])
        dcb = mm(sb.astype(F32).T.astype(BF)[64:128], dye[:, Q : 2 * Q])
        dbf = mm(af.astype(F32).T.astype(BF)[0:64], vw[:, 0:Q])
        dbb = mm(ab.astype(F32).T.astype(BF)[64:128], vw[:, Q : 2 * Q])
        dg = jnp.zeros((Q, Q), F32)
        rc_cols = jnp.zeros((Q, Q), F32)
        for j in range(HH // 2):
            r2 = slice(128 * j, 128 * j + 128)
            v = act[r2, l]
            dy_f = dyT[r2, l]
            dyt = dy_f.T.astype(BF)
            dy = dy_f.astype(BF)
            zb = jnp.zeros_like(dyt)
            dm2 = mm(jnp.concatenate([jnp.where(left, dyt, zb), jnp.where(left, zb, dyt)], 0), v)
            ms = []
            for k in (0, 1):
                h = 2 * j + k
                e = e_in[c, h].astype(F32)
                x = e * dm2[Q * k : Q * k + Q]
                dg = dg + x
                t = x * g
                tf = jnp.where(before, t, 0.0)
                ms.append((e * g).astype(BF))
                c_all = jnp.sum(t, 0, keepdims=True)
                c_f = jnp.sum(tf, 0, keepdims=True)
                c_rows[h : h + 1, l] = c_f
                c_rows[HH + h : HH + h + 1, l] = c_all - c_f
                r_all = jnp.sum(t, 1, keepdims=True)
                r_f = jnp.sum(tf, 1, keepdims=True)
                rc_cols = jnp.where(lane == h, r_f, rc_cols)
                rc_cols = jnp.where(lane == HH + h, r_all - r_f, rc_cols)
            dv = mm(
                jnp.concatenate([jnp.where(top, dy, zb), jnp.where(top, zb, dy)], 1),
                jnp.concatenate(ms, 0),
            )
            for k in (0, 1):
                h = 2 * j + k
                r = slice(64 * h, 64 * h + 64)
                v1 = v[64 * k : 64 * k + 64].astype(F32)
                dy1 = dy_f[64 * k : 64 * k + 64]
                f_in = vf[r] * w[h : h + 1]
                b_in = vb[r] * w[HH + h : HH + h + 1]
                ci_rows[h : h + 1, l] = jnp.sum(f_in * v1, 0, keepdims=True)
                ci_rows[HH + h : HH + h + 1, l] = jnp.sum(b_in * v1, 0, keepdims=True)
                ri_rows[h : h + 1, l] = jnp.sum(yf[r] * dy1, 0, keepdims=True) * ecue[h : h + 1]
                ri_rows[HH + h : HH + h + 1, l] = (
                    jnp.sum(yb[r] * dy1, 0, keepdims=True) * ecue[HH + h : HH + h + 1]
                )
                dact[r, l] = dv[64 * k : 64 * k + 64] + f_in + b_in + cc[r, 5:6] * dy1
        r_rows[:, l] = rc_cols.T[0:24, :]
        dgf = jnp.where(before, dg, 0.0).astype(BF)
        dgb = jnp.where(after, dg, 0.0).astype(BF)
        dact[C : C + 64, l] = dbf + mm(cf, dgf)
        dact[C + 64 : C + 128, l] = dcf + mm(bf, dgf, NT)
        dact[C + 128 : C + 192, l] = dbb + mm(cb, dgb)
        dact[C + 192 : C + 256, l] = dcb + mm(bb, dgb, NT)

    dact[C + 64 : C + 128, :] = pltpu.roll(dact[C + 64 : C + 128, :], T - 1, 1)
    dact[C + 192 : C + 256, :] = pltpu.roll(dact[C + 192 : C + 256, :], 1, 1)


def weights_kernel(
    length, dact, c_rows, r_rows, ci_rows, ri_rows, kk, rows, u_in, pre_in, dgate, nT, wcat, cc, cd, rc, small,
    dproj, b0, b1, b2, b3,
    small_s, dla_s,
):
    T = dact.shape[1]
    CH = T // Q
    C = dgate.shape[0]
    HH = C // PS
    low_h = iota2((HH, Q), 1) < 64

    ii, jj = iota2((Q, Q), 0), iota2((Q, Q), 1)
    gt = (ii > jj).astype(F32)
    ge = (ii >= jj).astype(F32)
    lt = (ii < jj).astype(F32)
    le = (ii <= jj).astype(F32)
    first = iota2((24, Q), 0) < HH
    cat = lambda ref: jnp.concatenate([ref[:, c * Q : (c + 1) * Q] for c in range(CH)], 0)
    r_in, c_in, c_x, r_x = cat(r_rows), cat(c_rows), cat(ci_rows), cat(ri_rows)
    rt = r_in + r_x
    as_f = mm_hi(rt, gt) - mm_hi(c_in, ge) + mm_hi(c_x, lt)
    as_b = mm_hi(rt, lt) - mm_hi(c_in, le) + mm_hi(c_x, gt)
    for c in range(CH):
        k = slice(24 * c, 24 * c + 24)
        l = slice(Q * c, Q * c + Q)
        kf = jnp.sum(jnp.where(low_h, kk[CH - 1 - c], 0.0), 1, keepdims=True)
        kb = jnp.sum(jnp.where(low_h, 0.0, kk[c]), 1, keepdims=True)
        dla_s[0:HH, l] = as_f[k][0:HH] + kf
        dla_s[HH : 2 * HH, l] = as_b[k][HH : 2 * HH] + kb
    dla = dla_s[...]
    dt = rows[DT : DT + 24, :]
    rate = rc[:, 1:2]
    live = (iota2((1, T), 1) < length[0]).astype(F32)
    sig = jax.nn.sigmoid(rows[RAW : RAW + 24, :])
    direct = (c_rows[...] + ci_rows[...]) * jnp.where(dt > 0.0, sig / jnp.where(dt > 0.0, dt, 1.0), 0.0)
    draw = (direct + rate * dla * sig) * live
    g_bias = jnp.sum(draw, 1, keepdims=True)
    g_decay = jnp.sum(dla * dt, 1, keepdims=True) * rate
    dproj[0:C, :] = dgate[...]
    dproj[2 * C + 256 : 2 * C + 384, :] = jnp.concatenate([draw, jnp.zeros((104, T), F32)], 0).astype(BF)

    at = iota2((64, T), 1)
    lane64 = iota2((64, Q), 1)

    @pl.loop(0, (C + 256) // 64)
    def _(b):
        r = pl.ds(pl.multiple_of(b * 64, 64), 64)
        pre = pre_in[r, :].astype(F32)
        sg = jax.nn.sigmoid(pre)
        dp = dact[r, :] * (sg * (1.0 + pre * (1.0 - sg)))
        uu = u_in[r, :].astype(F32)
        col = cc[r, :]
        du = col[:, 3:4] * dp
        base = jnp.where(b < C // 64, 32, 42)
        out = jnp.where(lane64 == base + 4, jnp.sum(dp, 1, keepdims=True), 0.0)
        out = jnp.where(lane64 == base + 3, jnp.sum(dp * uu, 1, keepdims=True), out)
        for back in (1, 2, 3):
            shifted = jnp.where(at >= back, pltpu.roll(uu, back, 1), 0.0)
            out = jnp.where(lane64 == base + 3 - back, jnp.sum(dp * shifted, 1, keepdims=True), out)
            ahead = jnp.where(at < T - back, pltpu.roll(dp, T - back, 1), 0.0)
            du = du + col[:, 3 - back : 4 - back] * ahead
        small_s[r, :] = out
        dproj[pl.ds(pl.multiple_of(b * 64 + C, 64), 64), :] = du.astype(BF)

    head_lane = iota2((24, Q), 1)
    sm = small[...] + small_s[0:C, :]
    small_s[0:C, :] = sm
    small_s[0:24, :] += jnp.where(head_lane == 39, g_bias, jnp.where(head_lane == 40, g_decay, 0.0))
    small_s[0:256, :] += small_s[C : C + 256, :]
    place = lax.axis_index("dp") % 4
    share = b0.shape[0]
    W = 2 * C + 256
    for k, ref in enumerate((b0, b1, b2, b3)):
        r = pl.ds(pl.multiple_of((place ^ k) * share, share), share)
        n = nT[r, :]
        gv = mm(n, dproj[C : 2 * C, :], NT)
        gs = mm(n, dproj[2 * C : W, :], NT)
        gt = mm(n, dproj[W : W + Q, :], NT)
        wide = (
            jnp.sum(gv * wcat[r, C : 2 * C].astype(F32), 1, keepdims=True)
            + jnp.sum(gs * wcat[r, 2 * C : W].astype(F32), 1, keepdims=True)
            + jnp.sum(gt * wcat[r, W : W + Q].astype(F32), 1, keepdims=True)
        ) / cd[r, 0:1]
        ref[:, 0:C] = gv.astype(BF)
        extra = jnp.where(iota2((share, Q), 1) == 41, wide, 0.0)
        fine = gt + small_s[r, :] + extra
        upper = fine.astype(BF)
        ref[:, C : C + Q] = upper + pltpu.roll(fine - upper.astype(F32), 64, 1).astype(BF)
        ref[:, C + Q : C + Q + 256] = gs.astype(BF)


def through_kernel(wcat, dproj, xT, cd, dno, dnx, dots, dn_s):
    T = xT.shape[1]
    half = dno.shape[0]
    m = lax.axis_index("tensor")
    own = pl.multiple_of(m * half, half)
    other = pl.multiple_of((1 - m) * half, half)
    gain = cd[:, 0:1]

    @pl.loop(0, T // 256)
    def _(j):
        l = lanes(j, 256)
        dn = mm(wcat[...], dproj[:, l])
        dot = jnp.sum(dn * xT[:, l].astype(F32) * gain, 0, keepdims=True)
        dots[:, l] = jnp.broadcast_to(dot, (8, 256))
        dn_s[...] = dn
        dno[:, l] = dn_s[pl.ds(own, half), :].astype(BF)
        dnx[0:half, l] = dn_s[pl.ds(other, half), :].astype(BF)
        top_part = dot.astype(BF).astype(F32)
        row = iota2((16, 256), 0)
        dnx[half : half + 16, l] = jnp.where(
            row == 0, top_part, jnp.where(row == 1, dot - top_part, 0.0)
        ).astype(BF)


def last_kernel(dno, dnr, d0, xT, doT, rows, cd, out):
    T = xT.shape[1]
    half = dno.shape[0]
    own = pl.multiple_of(lax.axis_index("tensor") * half, half)
    gain = cd[pl.ds(own, half), 0:1]

    @pl.loop(0, T // Q)
    def _(c):
        l = lanes(c)
        inv = rows[INV : INV + 1, l]
        sent = dnr[half : half + 16, l].astype(F32)
        k3 = inv * inv * inv * (d0[0:1, l] + sent[0:1] + sent[1:2]) / D
        e2 = (dno[:, l].astype(F32) + dnr[0:half, l].astype(F32)) * gain
        x = xT[pl.ds(own, half), l].astype(F32)
        dx = inv * e2 - x * k3 + doT[pl.ds(own, half), l].astype(F32)
        out[l, :] = dx.T.astype(BF)


def unpack_kernel(g0, g1, g2, g3, gv, gt, gs, ng, cv, vb, cst, sb, dl, sk, og, bias, sm):
    share = g0.shape[0]
    C = gv.shape[1]
    HH = C // PS
    place = lax.axis_index("dp") % 4
    for k, ref in enumerate((g0, g1, g2, g3)):
        r = pl.ds(pl.multiple_of((place ^ k) * share, share), share)
        gv[r, :] = ref[:, 0:C].astype(F32)
        mid = ref[:, C : C + Q].astype(F32)
        mid = mid + pltpu.roll(mid, 64, 1)
        gt[r, :] = mid[:, 0 : 2 * HH]
        sm[r, :] = mid
        gs[r, :] = ref[:, C + Q : C + Q + 256].astype(F32)
    turned = sm[...].T
    ng[...] = turned[41]
    cv[...] = turned[32:36]
    vb[...] = turned[36]
    cst[...] = turned[42:46, 0:256]
    sb[...] = turned[46, 0:256]
    og[...] = turned[38]
    dl[...] = turned[40, 0:HH] + turned[40, HH : 2 * HH]
    bias[0:1, :] = turned[39:40, 0:HH]
    bias[1:2, :] = turned[39:40, HH : 2 * HH]
    pick = (iota2((C, HH), 0) // PS == iota2((C, HH), 1)).astype(F32)
    sk[...] = mm_hi(turned[32:40], pick)[5]


def call(body, outs, scratch, args, smem, name, us=1.0):
    specs = [
        pl.BlockSpec(memory_space=pltpu.SMEM if i < smem else pltpu.VMEM) for i in range(len(args))
    ]
    return pl.pallas_call(
        body,
        out_shape=[jax.ShapeDtypeStruct(s, d) for s, d in outs],
        in_specs=specs,
        out_specs=[pl.BlockSpec(memory_space=pltpu.VMEM) for _ in outs],
        scratch_shapes=[pltpu.VMEM(s, d) for s, d in scratch],
        compiler_params=pltpu.CompilerParams(vmem_limit_bytes=VMEM_LIMIT),
        cost_estimate=pl.CostEstimate(
            flops=int(us * 9e8), bytes_accessed=int(us * 3e6), transcendentals=0
        ),
        name=name,
    )(*args)


def swap(x):
    return lax.ppermute(x, "tensor", [(0, 1), (1, 0)])


def across(x, groups, bit):
    return lax.ppermute(x, "dp", [(i, i ^ bit) for i in range(groups)])


def phases_of(groups):
    found, weight = [], 1
    while weight < groups:
        members = min(4, groups // weight)
        found.append((weight, members))
        weight *= members
    return found


def send_round(blocks, groups, weight):
    return [blocks[0]] + [across(b, groups, k * weight) for k, b in enumerate(blocks) if k]


def resplit(x, at):
    value = x[:, at : at + 64] + x[:, at + 64 : at + 128]
    upper = lax.reduce_precision(value, 8, 7)
    return jnp.concatenate([x[:, :at], upper, value - upper, x[:, at + 128 :]], 1)


def split(x, rank, weight, members):
    rows = x.shape[0] // members
    place = (rank // weight) % members
    return [lax.dynamic_slice_in_dim(x, (place ^ k) * rows, rows, 0) for k in range(members)]


def assemble(got, rank, weight):
    members = len(got)
    place = (rank // weight) % members
    parts = []
    for i in range(members):
        now = got[i]
        for p in range(1, members):
            now = jnp.where(place == p, got[i ^ p], now)
        parts.append(now)
    return jnp.concatenate(parts, 0)


def on_device(
    hidden_in, teacher, loss_mask, lengths, dealing, norm_gain, w_gate, w_value, w_state, w_step,
    step_bias, conv_value, conv_vbias, conv_state, conv_sbias, decay_log, skip_gain, out_gain, w_out,
):
    groups = lax.axis_size("dp")
    rank = lax.axis_index("dp")
    member = lax.axis_index("tensor")
    seqs, local, _ = hidden_in.shape
    half = teacher.shape[2]
    T = local * groups
    C = w_gate.shape[1]
    HH = decay_log.shape[0]
    CH = T // Q

    [dealt] = call(deal_kernel, [((seqs, local, half), BF)], [], (dealing, hidden_in), 1, "deal", 3.0)
    xo = lax.all_to_all(dealt, "dp", split_axis=0, concat_axis=0, tiled=True).reshape(T, half)

    pos = rank * local + lax.broadcasted_iota(jnp.int32, (seqs, local), 1)
    marks = (loss_mask > 0) & (pos < lengths[:, None])
    total = jnp.broadcast_to(jnp.sum(marks.astype(F32)), (8, Q))
    for bit in range(groups.bit_length() - 1):
        total = total + across(total, groups, 1 << bit)
    scale = (T / total[0, 0:1]).astype(F32)
    goal = jnp.where(marks[:, :, None], teacher, jnp.asarray(NOMARK, BF))
    [goal] = call(deal_kernel, [((seqs, local, half), BF)], [], (dealing, goal), 1, "deal_goal", 2.0)
    length = lax.dynamic_slice_in_dim(lengths, dealing[rank], 1, 0)

    wcat = jnp.concatenate(
        [w_gate, w_value, w_state, w_step.reshape(D, 2 * HH), jnp.zeros((D, Q - 2 * HH), BF)], 1
    )
    wt = wcat.T
    wot = w_out.T
    zc = jnp.zeros((256,), F32)
    cc = jnp.concatenate(
        [
            jnp.concatenate([conv_value, conv_state], 1),
            jnp.concatenate([conv_vbias, conv_sbias])[None],
            jnp.concatenate([jnp.repeat(skip_gain, PS), zc])[None],
            jnp.concatenate([out_gain, zc])[None],
            jnp.zeros((1, C + 256), F32),
        ],
        0,
    ).T
    cd = norm_gain[:, None]
    rate = -jnp.exp(decay_log)
    rc = jnp.stack([step_bias.reshape(-1), jnp.concatenate([rate, rate])], 1)

    xo, goal, wcat, wt, wot, cc, cd, rc, scale, length = lax.optimization_barrier(
        (xo, goal, wcat, wt, wot, cc, cd, rc, scale, length)
    )
    xs = swap(xo)
    to = lax.all_to_all(goal, "dp", split_axis=0, concat_axis=0, tiled=True).reshape(T, half)
    ts = swap(to)

    full = lambda n: ((n, T), BF)
    fullf = lambda n: ((n, T), F32)
    xT, nT, rows, dec, gate, u, pre, act, cs, e, mixed, sin, p_send, p0 = call(
        forward_kernel,
        [
            full(D), full(D), fullf(128), ((CH, 24, Q), F32), fullf(C), full(C + 256), full(C + 256),
            full(C + 256), full(128), ((CH, HH, Q, Q), BF), fullf(C), ((CH, C, Q), BF), full(D + 16),
            fullf(D + 8),
        ],
        [
            ((C + 256, T), F32), ((32, T), F32), ((24, T), F32), ((CH, C, Q), F32), ((C, Q), F32),
            ((C, 2 * Q), BF), ((C, T), BF),
        ],
        (length, xo, xs, wt, wot, cc, cd, rc),
        1,
        "forward",
        37.0,
    )
    p1 = swap(p_send)
    lo, doT, dyT, dgate, small, *mids = call(
        middle_kernel,
        [((T, half), BF), full(D), fullf(C), full(C), ((C, Q), F32)] + [((D // 4, D + C), BF)] * 4,
        [
            ((D, Q), F32), ((D, Q), F32), ((C, T), BF), ((C, 256), F32), ((8, T), F32), ((C, Q), F32),
            ((C, Q), F32), ((8, T), F32),
        ],
        (scale, p0, p1, xT, to, ts, w_out, w_gate, nT, gate, mixed, act, cc, cd),
        1,
        "middle",
        20.0,
    )
    phases = phases_of(groups)
    got_m = send_round(mids, groups, 1)
    rowsf = ((24, T), F32)
    dact, c_rows, r_rows, ci_rows, ri_rows, kk = call(
        backward_kernel,
        [fullf(C + 256), rowsf, rowsf, rowsf, rowsf, ((CH, HH, Q), F32)],
        [((CH, C, Q), F32), ((CH, C, Q), BF), ((C, Q), F32), ((C, 2 * Q), BF), ((C, 2 * Q), BF)],
        (act, cs, rows, dec, e, sin, dyT, cc),
        0,
        "backward",
        30.0,
    )
    now_m = sum(g.astype(F32) for g in got_m)
    now_m, dact = lax.optimization_barrier((now_m, dact))
    for weight, members in phases[1:]:
        blocks = split(now_m, rank, weight, members)
        got_m = send_round([b if k == 0 else b.astype(BF) for k, b in enumerate(blocks)], groups, weight)
        now_m = sum(g.astype(F32) for g in got_m)
    width = C + Q + 256
    dproj, b0, b1, b2, b3 = call(
        weights_kernel,
        [full(2 * C + 384)] + [((D // 4, width), BF)] * 4,
        [((C + 256, Q), F32), rowsf],
        (length, dact, c_rows, r_rows, ci_rows, ri_rows, kk, rows, u, pre, dgate, nT, wcat, cc, cd, rc, small),
        1,
        "weights",
        16.0,
    )
    gathered = lax.all_gather(now_m.astype(BF), "dp", axis=0, tiled=False)
    digits = [members for _, members in phases]
    count = len(digits)
    gathered = gathered.reshape(*reversed(digits), -1, D + C)
    order = tuple(reversed(range(count))) + (count, count + 1)
    gathered = gathered.transpose(order).reshape(D, D + C).astype(F32)
    got = send_round([b0, b1, b2, b3], groups, 1)
    dno, dnx, dots = call(
        through_kernel,
        [full(half), full(half + 16), ((8, T), F32)],
        [((D, 256), F32)],
        (wcat, dproj, xT, cd),
        0,
        "through",
        6.0,
    )
    dnr = swap(dnx)
    [dx] = call(
        last_kernel, [((T, half), BF)], [], (dno, dnr, dots, xT, doT, rows, cd), 0, "last", 5.0
    )
    dx, *got = lax.optimization_barrier((dx, *got))
    back = lax.all_to_all(dx.reshape(seqs, local, half), "dp", split_axis=0, concat_axis=0, tiled=True)
    [grad_in] = call(undeal_kernel, [((seqs, local, half), BF)], [], (dealing, back), 1, "undeal", 2.0)

    now = resplit(sum(g.astype(F32) for g in got), C)
    for weight, members in phases[1:]:
        blocks = split(now, rank, weight, members)
        got = send_round([b if k == 0 else b.astype(BF) for k, b in enumerate(blocks)], groups, weight)
        now = resplit(sum(g.astype(F32) for g in got), C)
    lane = lax.broadcasted_iota(jnp.int32, (1, Q + 256), 1)
    both = (lane >= Q) | ((lane % 64 >= 41) & (lane % 64 < 47))
    tail = now[:, C:]
    tail = resplit(tail + jnp.where(both, swap(tail.astype(BF)).astype(F32), 0.0), 0)
    now = jnp.concatenate([now[:, :C], tail], 1).astype(BF)
    for weight, members in reversed(phases[1:]):
        now = assemble(send_round([now] * members, groups, weight), rank, weight)
    got = send_round([now] * 4, groups, 1)
    gv, gt, gs, ng, cv, vb, cst, sb, dl, sk, og, bias = call(
        unpack_kernel,
        [
            ((D, C), F32), ((D, 2 * HH), F32), ((D, 256), F32), ((D,), F32), ((4, C), F32), ((C,), F32),
            ((4, 256), F32), ((256,), F32), ((HH,), F32), ((HH,), F32), ((C,), F32), ((2, HH), F32),
        ],
        [((D, Q), F32)],
        got,
        0,
        "unpack",
        3.0,
    )
    return (
        lo[None], grad_in, ng, gathered[:, D:], gv, gs, gt.reshape(D, 2, HH), bias, cv, vb, cst,
        sb, dl, sk, og, gathered[:, :D],
    )


def solution(mesh):
    dp, tp = "dp", "tensor"
    return jax.shard_map(
        on_device,
        mesh=mesh,
        in_specs=(
            P(None, dp, None), P(None, dp, tp), P(None, dp), P(), P(), P(), P(None, tp), P(None, tp), P(),
            P(None, None, tp), P(None, tp), P(None, tp), P(tp), P(), P(), P(tp), P(tp), P(tp), P(tp, None),
        ),
        out_specs=(
            P(dp, None, tp), P(None, dp, tp), P(), P(None, tp), P(None, tp), P(), P(None, None, tp),
            P(None, tp), P(None, tp), P(tp), P(), P(), P(tp), P(tp), P(tp), P(tp, None),
        ),
        check_vma=False,
    )
```

time: 1280 us -> 318 us (0.25); the launches traced: 1260 us -> 318 us
  local copies, waits for them, and re-layouts: 434 us -> 22.7 us
  other arithmetic: 205 us -> 7.99 us
  blocking collectives: 190 us -> 0 us
  waiting for transfers between devices: 255 us -> 80.4 us
  Pallas kernels: 0 us -> 137 us
  matrix products: 132 us -> 0 us
  starting transfers between devices: 27.6 us -> 52.9 us
    psum x2 -> x0, waiting for transfers between devices: 212 us -> none  [the longest x1 125 us: on_device(): lax.psum((grad_norm_part, grad_state, grad_kernel[:, inner_here:], grad_c...]
    psum x6 -> x0, blocking collectives: 190 us -> none  [the longest x1 96 us: on_device(): lax.psum((grad_gate, grad_value, grad_step, grad_step_bias, grad_kernel[:...]
    pallas_call x0 -> x10, Pallas kernels: none -> 137 us  [call(): pl.pallas_call(body, out_shape=[jax.ShapeDtypeStruct(s, d) for s, d in ou...]
    dot_general x31 -> x0, matrix products: 125 us -> none  [the longest x6 46.5 us: span_scan(): jnp.einsum('ctsh,cshp->cthp', scores[:, :, :, None] * within, scaled, pre...]
    rev x9 -> x0, local copies, waits for them, and re-layouts: 119 us -> none  [the longest x2 66.1 us: mix_sequence(): jnp.flip(per_head, 0)]
    unnamed x364 -> x55, local copies, waits for them, and re-layouts: 91.7 us -> 6.11 us
    ppermute x0 -> x27, waiting for transfers between devices: none -> 80.3 us  [the longest x22 75.1 us: across(): return lax.ppermute(x, 'dp', [(i, i ^ bit) for i in range(groups)])]
    dynamic_slice x67 -> x2, local copies, waits for them, and re-layouts: 78.7 us -> 1.18 us  [on_device(): length = lax.dynamic_slice_in_dim(lengths, dealing[rank], 1, 0)]
  transfers between devices with their start and end apart: 10 -> 31, of which waited for: 5 -> 14; matrix products, arithmetic and copies ran while one was open for 5% -> 6% of each run, Pallas kernels for 0% -> 24%
where the time goes in v1:
time: 318 us
  Pallas kernels  137 us (43%)
  waiting for transfers between devices  80.4 us (25%)
  starting transfers between devices  52.9 us (17%)
  local copies, waits for them, and re-layouts  22.7 us (7%)
  between operations  17.2 us (5%)
  other arithmetic  7.99 us (3%)
    pallas_call x10, Pallas kernels, call(): pl.pallas_call(body, out_shape=[jax.ShapeDtypeStruct(s, d) for s, d in ou...  137 us
    ppermute x22, waiting for transfers between devices, across(): return lax.ppermute(x, 'dp', [(i, i ^ bit) for i in range(groups)])  75.1 us
    ppermute x22, starting transfers between devices, across(): return lax.ppermute(x, 'dp', [(i, i ^ bit) for i in range(groups)])  37.7 us
  transfers between devices with their start and end apart: 31, of which 14 were waited for; matrix products, arithmetic and copies ran while one was open for 6% of the time, Pallas kernels for 24%

profile of v1, /device:TPU:0, one launch (start us, length us, event | category | flops | bytes accessed | tf_op | source)
XLA Modules:
  0.0 317.7 jit_solution(4866549224449542319)
XLA Ops:
  9.2 3.0 collective-permute-start
  14.8 6.1 %all-to-all-start = ((bf16[16,64,384]{2,1,0:T(8,128)(2,1)}), bf16[16,64,384]{2,1,0:T(8,128)(2,1)}, u32[]{:S(2)}, u32[]{:S(2)}) async-start(bf16[16,64,384]{2,1,0:T(8,128)(2,1)} %deal.1), calls=%async_computation | async-start | bytes 1572864 | tf_op jit(solution)/shard_map/all_to_all | solution.py:701
  33.4 4.6 %collective-permute-start.3 = (f32[8,128]{1,0:T(8,128)S(1)}, f32[8,128]{1,0:T(8,128)S(1)}, u32[]{:S(2)}, u32[]{:S(2)}) collective-permute-start(f32[8,128]{1,0:T(8,128)S(1)} %add.117), channel_id=1, source_target_pairs={{0,16},{2,18},{4,20},{6,22},{8,24},{10,26},{12,28},{14,30},{16,0},... | collective-permute-start | bytes 12296 | tf_op jit(solution)/shard_map/ppermute | solution.py:646
  44.1 3.7 %concatenate.34.wcat = bf16[768,1920]{1,0:T(8,128)(2,1)S(1)} concatenate(bf16[768,768]{1,0:T(8,128)(2,1)} %wg.1, bf16[768,768]{1,0:T(8,128)(2,1)} %param.26, bf16[768,256]{1,0:T(8,128)(2,1)} %param.27, bf16[768,24]{1,0:T(8,128)(2,1)S(1)} %copy.64, bf16[768,104]{1,0:T(8,128)(2,1)S(1)} %broadcast_in_dim.56), dimensions={1} | concatenate | bytes 5898240 | tf_op jit(solution)/shard_map/concatenate | solution.py:713
  53.7 3.8 %all-to-all-start.1 = ((bf16[16,64,384]{2,1,0:T(8,128)(2,1)}), bf16[16,64,384]{2,1,0:T(8,128)(2,1)S(1)}, u32[]{:S(2)}, u32[]{:S(2)}) async-start(bf16[16,64,384]{2,1,0:T(8,128)(2,1)} %deal_goal.1), calls=%async_computation.1 | async-start | bytes 1572864 | tf_op jit(solution)/shard_map/all_to_all | solution.py:737
  57.8 38.5 %forward.1 = (bf16[768,1024]{1,0:T(8,128)(2,1)}, bf16[768,1024]{1,0:T(8,128)(2,1)}, f32[128,1024]{1,0:T(8,128)}, f32[8,24,128]{2,1,0:T(8,128)}, f32[768,1024]{1,...) custom-call(s32[1]{0:T(128)} %dynamic_slice.31.length, ...), custom_call_target="tpu_custom_call" | custom-call | flops 33300000768 | bytes 111000000 | tf_op jit(solution)/shard_map/forward/pallas_call | solution.py:627
  96.8 4.1 %collective-permute-done.6.ts = bf16[1024,384]{1,0:T(8,128)(2,1)S(1)} collective-permute-done((bf16[1024,384]{1,0:T(8,128)(2,1)S(1)}, bf16[1024,384]{1,0:T(8,128)(2,1)S(1)}, u32[]{:S(2)}, u32[]{:S(2)}) %collective-permute-start.6) | collective-permute-done | bytes 786464 | tf_op jit(solution)/shard_map/ppermute | solution.py:642
  102.3 23.0 %middle.1 = (bf16[1024,384]{1,0:T(8,128)(2,1)}, bf16[768,1024]{1,0:T(8,128)(2,1)}, f32[768,1024]{1,0:T(8,128)}, bf16[768,1024]{1,0:T(8,128)(2,1)}, f32[768,128]{...) custom-call(f32[1]{0:T(128)} %bitcast.8.scale, ...), custom_call_target="tpu_custom_call" | custom-call | flops 17999998976 | bytes 60000000 | tf_op jit(solution)/shard_map/middle/pallas_call | solution.py:627
  128.8 22.8 %backward.1 = (f32[1024,1024]{1,0:T(8,128)}, f32[24,1024]{1,0:T(8,128)}, f32[24,1024]{1,0:T(8,128)}, f32[24,1024]{1,0:T(8,128)}, f32[24,1024]{1,0:T(8,128)}, /*index=5*/f32[8,12,128]{2,1,0:T(8,128)}) custom-call(bf16[1024,1024]{1,0:T(8,128)(2,1)} %get-tuple-element.97.act, bf16[128,1024]{1,0:T(8,128)(2,1)} %get-tuple-element.104.cs, ...), custom_call_target="tpu_custom_call" | custom-call | flops 27000000512 | bytes 90000000 | tf_op jit(solution)/shard_map/backward/pallas_call | solution.py:627
  151.6 3.6 %collective-permute-done.8 = bf16[192,1536]{1,0:T(8,128)(2,1)S(1)} collective-permute-done((bf16[192,1536]{1,0:T(8,128)(2,1)}, bf16[192,1536]{1,0:T(8,128)(2,1)S(1)}, u32[]{:S(2)}, u32[]{:S(2)}) %collective-permute-start.8) | collective-permute-done | bytes 589856 | tf_op jit(solution)/shard_map/ppermute | solution.py:646
  155.5 27.1 %weights.1 = (bf16[1920,1024]{1,0:T(8,128)(2,1)}, bf16[192,1152]{1,0:T(8,128)(2,1)}, bf16[192,1152]{1,0:T(8,128)(2,1)}, bf16[192,1152]{1,0:T(8,128)(2,1)}, bf16[192,1152]{1,0:T(8,128)(2,1)}) custom-call(s32[1]{0:T(128)} %dynamic_slice.31.length, f32[1024,1024]{1,0:T(8,128)} %get-tuple-element.111.dact, f32[24,1024]{1,0:T(8,128)} %get-tuple-element.112.c_rows, ...), custom_call_target="tpu_custom_call" | custom-call | flops 14400000000 | bytes 48000000 | tf_op jit(solution)/shard_map/weights/pallas_call | solution.py:627
  182.6 9.2 %through.1 = (bf16[384,1024]{1,0:T(8,128)(2,1)}, bf16[400,1024]{1,0:T(8,128)(2,1)}, f32[8,1024]{1,0:T(8,128)}) custom-call(bf16[768,1920]{1,0:T(8,128)(2,1)} %copy-done, bf16[1920,1024]{1,0:T(8,128)(2,1)} %get-tuple-element.121.dproj, bf16[768,1024]{1,0:T(8,128)(2,1)} %get-tuple-element.92.xT, f32[768,1]{1,0:T(8,128)} %copy.68.cd), custom_call_target="tpu_custom_call" | custom-call | flops 5400000000 | bytes 18000000 | tf_op jit(solution)/shard_map/through/pallas_call | solution.py:627
  197.5 3.4 %collective-permute-done.24 = bf16[48,1536]{1,0:T(8,128)(2,1)S(1)} collective-permute-done((bf16[48,1536]{1,0:T(8,128)(2,1)S(1)}, bf16[48,1536]{1,0:T(8,128)(2,1)S(1)}, u32[]{:S(2)}, u32[]{:S(2)}) %collective-permute-start.24) | collective-permute-done | bytes 147488 | tf_op jit(solution)/shard_map/ppermute | solution.py:646
  202.4 5.0 %collective-permute-done.25 = bf16[48,1536]{1,0:T(8,128)(2,1)S(1)} collective-permute-done((bf16[48,1536]{1,0:T(8,128)(2,1)S(1)}, bf16[48,1536]{1,0:T(8,128)(2,1)S(1)}, u32[]{:S(2)}, u32[]{:S(2)}) %collective-permute-start.25) | collective-permute-done | bytes 147488 | tf_op jit(solution)/shard_map/ppermute | solution.py:646
  209.6 5.3 %last.1 = bf16[1024,384]{1,0:T(8,128)(2,1)} custom-call(bf16[384,1024]{1,0:T(8,128)(2,1)} %get-tuple-element.122.dno, bf16[400,1024]{1,0:T(8,128)(2,1)} %collective-permute-done.10.dnr, f32[8,1024]{1,0:T(8,128)} %get-tuple-element.124.d0, bf16[768,1024]{1,0:T(8,128)(2,1)} %get-tuple-element.92.xT, bf16[768,1024]{1,0:T(8,128)(2,1)} %get-tuple-element.125.doT, ...), custom_call_target="tpu_custom_call" | custom-call | flops 4499999744 | bytes 15000000 | tf_op jit(solution)/shard_map/last/pallas_call | solution.py:627
  214.9 8.6 %collective-permute-done.12 = bf16[192,1152]{1,0:T(8,128)(2,1)S(1)} collective-permute-done((bf16[192,1152]{1,0:T(8,128)(2,1)}, bf16[192,1152]{1,0:T(8,128)(2,1)S(1)}, u32[]{:S(2)}, u32[]{:S(2)}) %collective-permute-start.12) | collective-permute-done | bytes 442400 | tf_op jit(solution)/shard_map/ppermute | solution.py:646
  224.1 3.1 collective-permute-start.15
  230.8 5.2 %collective-permute-done.15 = bf16[48,1152]{1,0:T(8,128)(2,1)S(1)} collective-permute-done((bf16[48,1152]{1,0:T(8,128)(2,1)S(1)}, bf16[48,1152]{1,0:T(8,128)(2,1)S(1)}, u32[]{:S(2)}, u32[]{:S(2)}) %collective-permute-start.15) | collective-permute-done | bytes 110624 | tf_op jit(solution)/shard_map/ppermute | solution.py:646
  242.2 4.4 %all-to-all-start.2 = ((bf16[16,64,384]{2,1,0:T(8,128)(2,1)}), bf16[16,64,384]{2,1,0:T(8,128)(2,1)S(1)}, u32[]{:S(2)}, u32[]{:S(2)}) async-start(bf16[16,64,384]{2,1,0:T(8,128)(2,1)} %bitcast.12), calls=%async_computation.2 | async-start | bytes 1572864 | tf_op jit(solution)/shard_map/all_to_all | solution.py:820
  247.5 14.4 %collective-permute-done.19 = bf16[48,1152]{1,0:T(8,128)(2,1)S(1)} collective-permute-done((bf16[48,1152]{1,0:T(8,128)(2,1)S(1)}, bf16[48,1152]{1,0:T(8,128)(2,1)S(1)}, u32[]{:S(2)}, u32[]{:S(2)}) %collective-permute-start.19) | collective-permute-done | bytes 110624 | tf_op jit(solution)/shard_map/ppermute | solution.py:646
  263.9 3.4 %collective-permute-start.22 = (bf16[192,1152]{1,0:T(8,128)(2,1)S(1)}, bf16[192,1152]{1,0:T(8,128)(2,1)S(1)}, u32[]{:S(2)}, u32[]{:S(2)}) collective-permute-start(bf16[192,1152]{1,0:T(8,128)(2,1)S(1)} %pad_maximum_fusion.g0), channel_id=1, source_target_pairs={{0,4},{2,6},{4,0},{6,2},{8,12},{10,14},{12,8},{14,10},{16,20},{18,... | collective-permute-start | bytes 1327112 | tf_op jit(solution)/shard_map/ppermute | solution.py:646
  267.3 17.7 %collective-permute-done.21.g1 = bf16[192,1152]{1,0:T(8,128)(2,1)S(1)} collective-permute-done((bf16[192,1152]{1,0:T(8,128)(2,1)S(1)}, bf16[192,1152]{1,0:T(8,128)(2,1)S(1)}, u32[]{:S(2)}, u32[]{:S(2)}) %collective-permute-start.21) | collective-permute-done | bytes 442400 | tf_op jit(solution)/shard_map/ppermute | solution.py:646
  285.1 10.4 %collective-permute-done.22.g2 = bf16[192,1152]{1,0:T(8,128)(2,1)S(1)} collective-permute-done((bf16[192,1152]{1,0:T(8,128)(2,1)S(1)}, bf16[192,1152]{1,0:T(8,128)(2,1)S(1)}, u32[]{:S(2)}, u32[]{:S(2)}) %collective-permute-start.22) | collective-permute-done | bytes 442400 | tf_op jit(solution)/shard_map/ppermute | solution.py:646
  297.0 3.6 %unpack.1 = (f32[768,768]{1,0:T(8,128)}, f32[768,24]{1,0:T(8,128)}, f32[768,256]{1,0:T(8,128)}, f32[768]{0:T(1024)}, f32[4,768]{1,0:T(4,128)}, /*index=5*/f32[76...) custom-call(bf16[192,1152]{1,0:T(8,128)(2,1)} %copy-done.6, ...), custom_call_target="tpu_custom_call" | custom-call | flops 2700000000 | bytes 9000000 | tf_op jit(solution)/shard_map/unpack/pallas_call | solution.py:627
  (162 shorter events, 66.4 us)
Async XLA Ops:
  9.2 15.2 %collective-permute-start = (f32[8,128]{1,0:T(8,128)S(1)}, f32[8,128]{1,0:T(8,128)S(1)}, u32[]{:S(2)}, u32[]{:S(2)}) collective-permute-start(f32[8,128]{1,0:T(8,128)S(1)} %broadcast_in_dim.63), channel_id=1, source_target_pairs={{0,2},{2,0},{4,6},{6,4},{8,10},{10,8},{12,14},{14,12},{16,18},{18,... | collective-permute-start | bytes 12296 | tf_op jit(solution)/shard_map/ppermute | solution.py:646
  14.8 34.4 %all-to-all-start = ((bf16[16,64,384]{2,1,0:T(8,128)(2,1)}), bf16[16,64,384]{2,1,0:T(8,128)(2,1)}, u32[]{:S(2)}, u32[]{:S(2)}) async-start(bf16[16,64,384]{2,1,0:T(8,128)(2,1)} %deal.1), calls=%async_computation | async-start | bytes 1572864 | tf_op jit(solution)/shard_map/all_to_all | solution.py:701
  33.4 14.5 %collective-permute-start.3 = (f32[8,128]{1,0:T(8,128)S(1)}, f32[8,128]{1,0:T(8,128)S(1)}, u32[]{:S(2)}, u32[]{:S(2)}) collective-permute-start(f32[8,128]{1,0:T(8,128)S(1)} %add.117), channel_id=1, source_target_pairs={{0,16},{2,18},{4,20},{6,22},{8,24},{10,26},{12,28},{14,30},{16,0},... | collective-permute-start | bytes 12296 | tf_op jit(solution)/shard_map/ppermute | solution.py:646
  53.7 42.9 %all-to-all-start.1 = ((bf16[16,64,384]{2,1,0:T(8,128)(2,1)}), bf16[16,64,384]{2,1,0:T(8,128)(2,1)S(1)}, u32[]{:S(2)}, u32[]{:S(2)}) async-start(bf16[16,64,384]{2,1,0:T(8,128)(2,1)} %deal_goal.1), calls=%async_computation.1 | async-start | bytes 1572864 | tf_op jit(solution)/shard_map/all_to_all | solution.py:737
  57.5 248.0 %all-gather.3.cloned.1.call-start = ((), (), s32[]{:S(2)}) async-start(), calls=%async_computation.3 | async-start | bytes 2506752 | tf_op jit(solution)/shard_map/all_gather | solution.py:799
  125.3 26.4 %collective-permute-start.7 = (bf16[192,1536]{1,0:T(8,128)(2,1)}, bf16[192,1536]{1,0:T(8,128)(2,1)S(1)}, u32[]{:S(2)}, u32[]{:S(2)}) collective-permute-start(bf16[192,1536]{1,0:T(8,128)(2,1)} %get-tuple-element.101), channel_id=1, source_target_pairs={{0,2},{2,0},{4,6},{6,4},{8,10},{10,8},{12,14},{14,12},{16,18},{18,... | collective-permute-start | bytes 1769480 | tf_op jit(solution)/shard_map/ppermute | solution.py:646
  127.2 28.0 %collective-permute-start.8 = (bf16[192,1536]{1,0:T(8,128)(2,1)}, bf16[192,1536]{1,0:T(8,128)(2,1)S(1)}, u32[]{:S(2)}, u32[]{:S(2)}) collective-permute-start(bf16[192,1536]{1,0:T(8,128)(2,1)} %get-tuple-element.102), channel_id=1, source_target_pairs={{0,4},{2,6},{4,0},{6,2},{8,12},{10,14},{12,8},{14,10},{16,20},{18,... | collective-permute-start | bytes 1769480 | tf_op jit(solution)/shard_map/ppermute | solution.py:646
  128.7 26.6 %collective-permute-start.9 = (bf16[192,1536]{1,0:T(8,128)(2,1)}, bf16[192,1536]{1,0:T(8,128)(2,1)S(1)}, u32[]{:S(2)}, u32[]{:S(2)}) collective-permute-start(bf16[192,1536]{1,0:T(8,128)(2,1)} %get-tuple-element.103), channel_id=1, source_target_pairs={{0,6},{2,4},{4,2},{6,0},{8,14},{10,12},{12,10},{14,8},{16,22},{18,... | collective-permute-start | bytes 1769480 | tf_op jit(solution)/shard_map/ppermute | solution.py:646
  191.9 17.8 %collective-permute-start.10 = (bf16[400,1024]{1,0:T(8,128)(2,1)}, bf16[400,1024]{1,0:T(8,128)(2,1)}, u32[]{:S(2)}, u32[]{:S(2)}) collective-permute-start(bf16[400,1024]{1,0:T(8,128)(2,1)} %get-tuple-element.123), channel_id=1, source_target_pairs={{0,1},{1,0},{2,3},{3,2},{4,5},{5,4},{6,7},{7,6},{8,9},{9,8},{10,11... | collective-permute-start | bytes 2457608 | tf_op jit(solution)/shard_map/ppermute | solution.py:642
  191.9 9.0 %collective-permute-start.24 = (bf16[48,1536]{1,0:T(8,128)(2,1)S(1)}, bf16[48,1536]{1,0:T(8,128)(2,1)S(1)}, u32[]{:S(2)}, u32[]{:S(2)}) collective-permute-start(bf16[48,1536]{1,0:T(8,128)(2,1)S(1)} %get-tuple-element.200), channel_id=1, source_target_pairs={{0,8},{2,10},{4,12},{6,14},{8,0},{10,2},{12,4},{14,6},{16,24},{18,... | collective-permute-start | bytes 442376 | tf_op jit(solution)/shard_map/ppermute | solution.py:646
  193.4 13.9 %collective-permute-start.25 = (bf16[48,1536]{1,0:T(8,128)(2,1)S(1)}, bf16[48,1536]{1,0:T(8,128)(2,1)S(1)}, u32[]{:S(2)}, u32[]{:S(2)}) collective-permute-start(bf16[48,1536]{1,0:T(8,128)(2,1)S(1)} %get-tuple-element.202), channel_id=1, source_target_pairs={{0,16},{2,18},{4,20},{6,22},{8,24},{10,26},{12,28},{14,30},{16,0},... | collective-permute-start | bytes 442376 | tf_op jit(solution)/shard_map/ppermute | solution.py:646
  195.8 13.1 %collective-permute-start.26 = (bf16[48,1536]{1,0:T(8,128)(2,1)S(1)}, bf16[48,1536]{1,0:T(8,128)(2,1)S(1)}, u32[]{:S(2)}, u32[]{:S(2)}) collective-permute-start(bf16[48,1536]{1,0:T(8,128)(2,1)S(1)} %get-tuple-element.201), channel_id=1, source_target_pairs={{0,24},{2,26},{4,28},{6,30},{8,16},{10,18},{12,20},{14,22},{16,8},... | collective-permute-start | bytes 442376 | tf_op jit(solution)/shard_map/ppermute | solution.py:646
  196.4 18.6 %collective-permute-start.11 = (bf16[192,1152]{1,0:T(8,128)(2,1)}, bf16[192,1152]{1,0:T(8,128)(2,1)S(1)}, u32[]{:S(2)}, u32[]{:S(2)}) collective-permute-start(bf16[192,1152]{1,0:T(8,128)(2,1)} %get-tuple-element.127), channel_id=1, source_target_pairs={{0,2},{2,0},{4,6},{6,4},{8,10},{10,8},{12,14},{14,12},{16,18},{18,... | collective-permute-start | bytes 1327112 | tf_op jit(solution)/shard_map/ppermute | solution.py:646
  200.9 22.5 %collective-permute-start.12 = (bf16[192,1152]{1,0:T(8,128)(2,1)}, bf16[192,1152]{1,0:T(8,128)(2,1)S(1)}, u32[]{:S(2)}, u32[]{:S(2)}) collective-permute-start(bf16[192,1152]{1,0:T(8,128)(2,1)} %get-tuple-element.128), channel_id=1, source_target_pairs={{0,4},{2,6},{4,0},{6,2},{8,12},{10,14},{12,8},{14,10},{16,20},{18,... | collective-permute-start | bytes 1327112 | tf_op jit(solution)/shard_map/ppermute | solution.py:646
  207.4 16.1 %collective-permute-start.13 = (bf16[192,1152]{1,0:T(8,128)(2,1)S(1)}, bf16[192,1152]{1,0:T(8,128)(2,1)S(1)}, u32[]{:S(2)}, u32[]{:S(2)}) collective-permute-start(bf16[192,1152]{1,0:T(8,128)(2,1)S(1)} %copy-done.19), channel_id=1, source_target_pairs={{0,6},{2,4},{4,2},{6,0},{8,14},{10,12},{12,10},{14,8},{16,22},{18,... | collective-permute-start | bytes 1327112 | tf_op jit(solution)/shard_map/ppermute | solution.py:646
  224.1 11.9 %collective-permute-start.15 = (bf16[48,1152]{1,0:T(8,128)(2,1)S(1)}, bf16[48,1152]{1,0:T(8,128)(2,1)S(1)}, u32[]{:S(2)}, u32[]{:S(2)}) collective-permute-start(bf16[48,1152]{1,0:T(8,128)(2,1)S(1)} %get-tuple-element.205), channel_id=1, source_target_pairs={{0,16},{2,18},{4,20},{6,22},{8,24},{10,26},{12,28},{14,30},{16,0},... | collective-permute-start | bytes 331784 | tf_op jit(solution)/shard_map/ppermute | solution.py:646
  227.2 8.8 %collective-permute-start.16 = (bf16[48,1152]{1,0:T(8,128)(2,1)S(1)}, bf16[48,1152]{1,0:T(8,128)(2,1)S(1)}, u32[]{:S(2)}, u32[]{:S(2)}) collective-permute-start(bf16[48,1152]{1,0:T(8,128)(2,1)S(1)} %get-tuple-element.204), channel_id=1, source_target_pairs={{0,24},{2,26},{4,28},{6,30},{8,16},{10,18},{12,20},{14,22},{16,8},... | collective-permute-start | bytes 331784 | tf_op jit(solution)/shard_map/ppermute | solution.py:646
  237.8 9.7 %collective-permute-start.18 = (bf16[48,1152]{1,0:T(8,128)(2,1)S(1)}, bf16[48,1152]{1,0:T(8,128)(2,1)S(1)}, u32[]{:S(2)}, u32[]{:S(2)}) collective-permute-start(bf16[48,1152]{1,0:T(8,128)(2,1)S(1)} %concatenate.43), channel_id=1, source_target_pairs={{0,24},{2,26},{4,28},{6,30},{8,16},{10,18},{12,20},{14,22},{16,8},... | collective-permute-start | bytes 331784 | tf_op jit(solution)/shard_map/ppermute | solution.py:646
  239.4 22.5 %collective-permute-start.19 = (bf16[48,1152]{1,0:T(8,128)(2,1)S(1)}, bf16[48,1152]{1,0:T(8,128)(2,1)S(1)}, u32[]{:S(2)}, u32[]{:S(2)}) collective-permute-start(bf16[48,1152]{1,0:T(8,128)(2,1)S(1)} %concatenate.43), channel_id=1, source_target_pairs={{0,16},{2,18},{4,20},{6,22},{8,24},{10,26},{12,28},{14,30},{16,0},... | collective-permute-start | bytes 331784 | tf_op jit(solution)/shard_map/ppermute | solution.py:646
  241.1 20.9 %collective-permute-start.20 = (bf16[48,1152]{1,0:T(8,128)(2,1)S(1)}, bf16[48,1152]{1,0:T(8,128)(2,1)S(1)}, u32[]{:S(2)}, u32[]{:S(2)}) collective-permute-start(bf16[48,1152]{1,0:T(8,128)(2,1)S(1)} %concatenate.43), channel_id=1, source_target_pairs={{0,8},{2,10},{4,12},{6,14},{8,0},{10,2},{12,4},{14,6},{16,24},{18,... | collective-permute-start | bytes 331784 | tf_op jit(solution)/shard_map/ppermute | solution.py:646
  242.2 60.3 %all-to-all-start.2 = ((bf16[16,64,384]{2,1,0:T(8,128)(2,1)}), bf16[16,64,384]{2,1,0:T(8,128)(2,1)S(1)}, u32[]{:S(2)}, u32[]{:S(2)}) async-start(bf16[16,64,384]{2,1,0:T(8,128)(2,1)} %bitcast.12), calls=%async_computation.2 | async-start | bytes 1572864 | tf_op jit(solution)/shard_map/all_to_all | solution.py:820
  262.1 23.0 %collective-permute-start.21 = (bf16[192,1152]{1,0:T(8,128)(2,1)S(1)}, bf16[192,1152]{1,0:T(8,128)(2,1)S(1)}, u32[]{:S(2)}, u32[]{:S(2)}) collective-permute-start(bf16[192,1152]{1,0:T(8,128)(2,1)S(1)} %pad_maximum_fusion.g0), channel_id=1, source_target_pairs={{0,2},{2,0},{4,6},{6,4},{8,10},{10,8},{12,14},{14,12},{16,18},{18,... | collective-permute-start | bytes 1327112 | tf_op jit(solution)/shard_map/ppermute | solution.py:646
  263.9 31.6 %collective-permute-start.22 = (bf16[192,1152]{1,0:T(8,128)(2,1)S(1)}, bf16[192,1152]{1,0:T(8,128)(2,1)S(1)}, u32[]{:S(2)}, u32[]{:S(2)}) collective-permute-start(bf16[192,1152]{1,0:T(8,128)(2,1)S(1)} %pad_maximum_fusion.g0), channel_id=1, source_target_pairs={{0,4},{2,6},{4,0},{6,2},{8,12},{10,14},{12,8},{14,10},{16,20},{18,... | collective-permute-start | bytes 1327112 | tf_op jit(solution)/shard_map/ppermute | solution.py:646
  267.3 28.1 %collective-permute-start.23 = (bf16[192,1152]{1,0:T(8,128)(2,1)S(1)}, bf16[192,1152]{1,0:T(8,128)(2,1)S(1)}, u32[]{:S(2)}, u32[]{:S(2)}) collective-permute-start(bf16[192,1152]{1,0:T(8,128)(2,1)S(1)} %pad_maximum_fusion.g0), channel_id=1, source_target_pairs={{0,6},{2,4},{4,2},{6,0},{8,14},{10,12},{12,10},{14,8},{16,22},{18,... | collective-permute-start | bytes 1327112 | tf_op jit(solution)/shard_map/ppermute | solution.py:646
  (33 other events, 319.5 us)
Sparse Core Ops, SparseCore 0:
  209.7 90.4 all-gather.2

commit v2 on v1

v2 whole, which is shorter than its diff:
```python
import functools
import inspect

import jax
import jax.numpy as jnp
from jax import lax
from jax.experimental import pallas as pl
from jax.experimental.pallas import tpu as pltpu
from jax.sharding import PartitionSpec as P

D = 768
INNER = 1536
PS = 64
N = 64
Q = 128
EPS = 1e-5
NOMARK = 256.0
BF = jnp.bfloat16
F32 = jnp.float32
HI = lax.Precision.HIGHEST


def pairs(count, before=None, after=None):
    def run(body):
        @pl.loop(0, count // 2)
        def _(k):
            if before:
                before(k)
            body(2 * k)
            body(2 * k + 1)
            if after:
                after(k)

    return run


ROWS = 32

NN = (((1,), (0,)), ((), ()))
NT = (((1,), (1,)), ((), ()))


def mm(a, b, dims=NN):
    return lax.dot_general(a, b, dims, preferred_element_type=F32)


def mm_hi(a, b):
    return lax.dot_general(a, b, NN, precision=HI, preferred_element_type=F32)


def lanes(c, width=Q):
    return pl.ds(pl.multiple_of(c * width, width), width)


def iota2(shape, dim):
    return lax.broadcasted_iota(jnp.int32, shape, dim)


def log1p_exp(z):
    w = 1.0 + z
    return jnp.where(w == 1.0, z, jnp.log(w) * (z / jnp.where(w == 1.0, 1.0, w - 1.0)))


RAW, DT, CUM, CUE, ROWV = 0, 24, 48, 72, 96


def deal_kernel(io, dealing, src, dst):
    count, _, width = dst.shape
    if src.shape[2] == width:
        col = pl.ds(0, width)
    else:
        col = pl.ds(pl.multiple_of(lax.axis_index("tensor") * width, width), width)

    @pl.loop(0, count)
    def _(j):
        dst[j] = src[dealing[j], :, col]


def prepare_kernel(io, wg, wv, ws, wst, wo, ng, wcat, wt, wot, cd):
    C = wg.shape[1]
    W = 2 * C + 256
    wcat[:, 0:C] = wg[...]
    wcat[:, C : 2 * C] = wv[...]
    wcat[:, 2 * C : W] = ws[...]
    wcat[:, W : W + Q] = jnp.concatenate([wst[...], jnp.zeros((D, Q - wst.shape[1]), BF)], 1)
    io.put("wcat")

    @pl.loop(0, (W + Q) // Q)
    def _(c):
        wt[lanes(c), :] = wcat[:, lanes(c)].astype(F32).T.astype(BF)

    io.put("wt")

    @pl.loop(0, D // Q)
    def _(c):
        wot[lanes(c), :] = wo[:, lanes(c)].astype(F32).T.astype(BF)

    cd[...] = jnp.broadcast_to(ng[...], (8, D)).T


def forward_kernel(
    io, length, xo, xs, wt, wot, cc, cd, rc,
    xT, nT, rows, dec, gate, uO, preO, act, cs, eO, mixed, sin, pO, inv_o,
    u_s, raw_s, w_s, dS, run, vw, bu,
):
    T = xo.shape[0]
    CH = T // Q
    C = gate.shape[0]
    HH = C // PS
    half = xo.shape[1]
    m = lax.axis_index("tensor")
    own = pl.multiple_of(m * half, half)
    other = pl.multiple_of((1 - m) * half, half)

    def arrive(k):
        io.need("xo", k)
        io.need("xs", k)

    @pairs(CH, arrive)
    def _(c):
        l = lanes(c)
        xT[pl.ds(own, half), l] = xo[l, :].astype(F32).T.astype(BF)
        xT[pl.ds(other, half), l] = xs[l, :].astype(F32).T.astype(BF)
        x = xT[:, l].astype(F32)
        inv = lax.rsqrt(jnp.sum(x * x, 0, keepdims=True) / D + EPS)
        inv_o[:, l] = jnp.broadcast_to(inv, (8, Q))
        nT[:, l] = (x * inv * cd[:, 0:1]).astype(BF)

    io.put("xT")
    io.put("nT")
    io.need("wt")

    @pl.loop(0, T // 256, unroll=2)
    def _(j):
        l = lanes(j, 256)
        n = nT[:, l]
        gate[:, l] = mm(wt[0:C, :], n)
        u_s[:, l] = mm(wt[C : 2 * C + 256, :], n)
        raw_s[:, l] = mm(wt[2 * C + 256 : 2 * C + 288, :], n)

    io.put("gate")

    raw = raw_s[0:24, :] + rc[:, 0:1]
    live = (iota2((1, T), 1) < length[0]).astype(F32)
    dt = (jnp.maximum(raw, 0.0) + log1p_exp(jnp.exp(-jnp.abs(raw)))) * live
    la = dt * rc[:, 1:2]
    rows[RAW : RAW + 24, :] = raw
    rows[DT : DT + 24, :] = dt
    upper = (iota2((Q, Q), 0) <= iota2((Q, Q), 1)).astype(F32)
    lower = (iota2((Q, Q), 0) >= iota2((Q, Q), 1)).astype(F32)
    stacked = jnp.concatenate([la[:, c * Q : (c + 1) * Q] for c in range(CH)], 0)
    cum_f = mm_hi(stacked, upper)
    cum_b = mm_hi(stacked, lower)
    first = iota2((24, Q), 0) < HH
    for c in range(CH):
        r = slice(24 * c, 24 * c + 24)
        k = slice(Q * c, Q * c + Q)
        cum = jnp.where(first, cum_f[r], cum_b[r])
        dtc = dt[:, k]
        rows[CUM : CUM + 24, k] = cum
        rows[CUE : CUE + 24, k] = cum - la[:, k]
        rows[ROWV : ROWV + 24, k] = jnp.where(
            dtc > 0.0, cum - jnp.log(jnp.where(dtc > 0.0, dtc, 1.0)), 1e30
        )
        tot = jnp.broadcast_to(jnp.sum(la[:, k], 1, keepdims=True), (24, Q))
        dec[c] = jnp.exp(tot)
        w_s[:, k] = jnp.exp(tot - cum) * dtc

    io.put("rows")
    io.put("dec")
    io.need("cc")

    at = iota2((ROWS, Q), 1)

    @pl.loop(0, u_s.shape[0] // ROWS, unroll=2)
    def _(b):
        r = pl.ds(pl.multiple_of(b * ROWS, ROWS), ROWS)
        col = cc[r, :]
        ks = [jnp.broadcast_to(col[:, k : k + 1], (ROWS, Q)) for k in range(5)]
        earlier = [jnp.zeros((ROWS, Q), F32)] * 4
        for c in range(CH):
            l = slice(c * Q, c * Q + Q)
            uu = u_s[r, l]
            pre = ks[4] + ks[3] * uu
            for back in (1, 2, 3):
                moved = pltpu.roll(uu, back, 1)
                pre = pre + ks[3 - back] * jnp.where(at >= back, moved, earlier[back])
                earlier[back] = moved
            uO[r, l] = uu.astype(BF)
            preO[r, l] = pre.astype(BF)
            act[r, l] = (pre * jax.nn.sigmoid(pre)).astype(BF)

    cs[0:64, :] = pltpu.roll(act[C + 64 : C + 128, :].astype(F32), 1, 1).astype(BF)
    cs[64:128, :] = pltpu.roll(act[C + 192 : C + 256, :].astype(F32), T - 1, 1).astype(BF)

    io.put("uO")
    io.put("preO")
    io.put("act")
    io.put("cs")

    zeros = jnp.zeros((64, Q), BF)

    @pairs(CH)
    def _(c):
        l = lanes(c)
        for h in range(HH):
            v = act[64 * h : 64 * h + 64, l].astype(F32)
            vw[64 * h : 64 * h + 64, 0:Q] = (v * w_s[h : h + 1, l]).astype(BF)
            vw[64 * h : 64 * h + 64, Q : 2 * Q] = (v * w_s[HH + h : HH + h + 1, l]).astype(BF)
        both = jnp.concatenate(
            [
                jnp.concatenate([act[C : C + 64, l], zeros], 1),
                jnp.concatenate([zeros, act[C + 128 : C + 192, l]], 1),
            ],
            0,
        )
        dS[c] = mm(vw[...], both, NT)

    run[...] = jnp.zeros_like(run)
    low = iota2((64, Q), 1) < 64
    low_h = iota2((HH, Q), 1) < 64

    @pairs(CH)
    def _(i):
        d = jnp.where(low_h, dec[i][0:HH], dec[CH - 1 - i][HH : 2 * HH])
        for h in range(HH):
            r = slice(64 * h, 64 * h + 64)
            now = run[r, :]
            sin[i, r, :] = now.astype(BF)
            run[r, :] = now * d[h : h + 1] + jnp.where(low, dS[i, r, :], dS[CH - 1 - i, r, :])

    io.put("sin")

    before = iota2((Q, Q), 1) < iota2((Q, Q), 0)
    after = iota2((Q, Q), 1) > iota2((Q, Q), 0)
    top = iota2((Q, Q), 0) < 64

    def leave(k):
        io.put("eO", k)
        io.put("mixed", k)

    @pairs(CH, after=leave)
    def _(c):
        l = lanes(c)
        bf = act[C : C + 64, l]
        bb = act[C + 128 : C + 192, l]
        cf = cs[0:64, l]
        cb = cs[64:128, l]
        gf = mm(cf.astype(F32).T.astype(BF), bf)
        gb = mm(cb.astype(F32).T.astype(BF), bb)
        g = jnp.where(before, gf, jnp.where(after, gb, 0.0))
        cue = rows[CUE : CUE + 24, l]
        cols = jnp.concatenate([cue, jnp.zeros((Q - 24, Q), F32)], 0).T
        ecue = jnp.exp(cue)
        zc = jnp.zeros((64, Q), BF)
        yf = mm(sin[c], jnp.concatenate([cf, zc], 0))
        yb = mm(sin[CH - 1 - c], jnp.concatenate([zc, cb], 0))
        total = jnp.zeros((1, Q), F32)
        for j in range(HH // 2):
            ms = []
            for h in (2 * j, 2 * j + 1):
                gap = jnp.where(
                    before,
                    cols[:, h : h + 1] - rows[ROWV + h : ROWV + h + 1, l],
                    cols[:, HH + h : HH + h + 1] - rows[ROWV + HH + h : ROWV + HH + h + 1, l],
                )
                e = jnp.exp(jnp.minimum(gap, 30.0))
                eO[c, h] = e.astype(BF)
                ms.append((e * g).astype(BF))
            v = act[128 * j : 128 * j + 128, l]
            vz = jnp.zeros_like(v)
            pair = jnp.concatenate([jnp.where(top, v, vz), jnp.where(top, vz, v)], 1)
            y = mm(pair, jnp.concatenate(ms, 1), NT)
            for k in (0, 1):
                h = 2 * j + k
                r = slice(64 * h, 64 * h + 64)
                mix = (
                    y[64 * k : 64 * k + 64]
                    + ecue[h : h + 1] * yf[r]
                    + ecue[HH + h : HH + h + 1] * yb[r]
                    + cc[r, 5:6] * v[64 * k : 64 * k + 64].astype(F32)
                )
                mixed[r, l] = mix
                gt = gate[r, l]
                gated = mix * (gt * jax.nn.sigmoid(gt))
                total = total + jnp.sum(gated * gated, 0, keepdims=True)
                bu[r, l] = (gated * cc[r, 6:7]).astype(BF)
        top_part = total.astype(BF).astype(F32)
        pO[D : D + 16, l] = jnp.where(
            iota2((16, Q), 0) == 0, top_part, jnp.where(iota2((16, Q), 0) == 1, total - top_part, 0.0)
        ).astype(BF)

    io.need("wot")

    @pl.loop(0, T // 256)
    def _(j):
        l = lanes(j, 256)
        pO[0:D, l] = mm(wot[...], bu[:, l]).astype(BF)
        io.put("pO", j)


def middle_kernel(
    io, p0, p1, xT, to, ts, wo, nT, gate, mixed, cc,
    lo, doh, dyT, dgate, small, m0, m1, m2, m3,
    res_s, tea_s, branch, dbr, dot_s, acc_g, q_s, doT,
):
    T = to.shape[0]
    CH = T // Q
    C = gate.shape[0]
    half = to.shape[1]
    m = lax.axis_index("tensor")
    own = pl.multiple_of(m * half, half)
    other = pl.multiple_of((1 - m) * half, half)

    def arrive(k):
        for n in ("p0", "p1", "xT", "to", "ts"):
            io.need(n, k)

    @pairs(CH, arrive)
    def _(c):
        l = lanes(c)
        tea_s[pl.ds(own, half), :] = to[l, :].astype(F32).T
        tea_s[pl.ds(other, half), :] = ts[l, :].astype(F32).T
        pt = p0[0:D, l].astype(F32) + p1[0:D, l].astype(F32)
        sums = p0[D : D + 16, l].astype(F32) + p1[D : D + 16, l].astype(F32)
        q = lax.rsqrt((sums[0:1] + sums[1:2]) / INNER + EPS)
        q_s[:, l] = jnp.broadcast_to(q, (8, Q))
        res = xT[:, l].astype(F32) + q * pt
        res_s[...] = res
        tea = tea_s[...]
        do = jnp.where(tea < 0.5 * NOMARK, res - tea, 0.0).astype(BF)
        doT[:, l] = do
        dot_s[:, l] = jnp.broadcast_to(jnp.sum(do.astype(F32) * pt, 0, keepdims=True), (8, Q))
        lo[l, :] = res_s[pl.ds(own, half), :].T.astype(BF)
        doh[:, l] = doT[pl.ds(own, half), l]

    io.put("doh")
    io.put("lo")
    acc_g[...] = jnp.zeros_like(acc_g)

    for n in ("wo", "cc"):
        io.need(n)

    @pl.loop(0, T // 256)
    def _(j):
        l = lanes(j, 256)
        io.need("gate", j)
        io.need("mixed", j)
        dbr[...] = mm(wo[...], doT[:, l])
        q = q_s[0:1, l]
        q3 = q * q * q * dot_s[0:1, l] / INNER

        @pl.loop(0, C // 64, unroll=2)
        def _(b):
            r = pl.ds(pl.multiple_of(b * 64, 64), 64)
            gain = jnp.broadcast_to(cc[r, 6:7], (64, Q))
            acc = acc_g[r, :]
            for t in (0, 1):
                k = slice(t * Q, t * Q + Q)
                l1 = pl.ds(pl.multiple_of(j * 256 + t * Q, Q), Q)
                d = dbr[r, k]
                g = gate[r, l1]
                mix = mixed[r, l1]
                sg = jax.nn.sigmoid(g)
                si = g * sg
                gated = mix * si
                gq = gated * q[:, k]
                branch[r, l1] = (gq * gain).astype(BF)
                acc = acc + d * gq
                dgt = q[:, k] * (d * gain) - gated * q3[:, k]
                dyT[r, l1] = (dgt * si).astype(BF)
                dgate[r, l1] = (dgt * mix * (sg * (1.0 + g * (1.0 - sg)))).astype(BF)
            acc_g[r, :] = acc

        io.put("dyT", j)

    io.put("dgate")
    io.need("nT")
    place = lax.axis_index("dp") % 4
    share = m0.shape[0]
    for k, ref in enumerate((m0, m1, m2, m3)):
        r = pl.ds(pl.multiple_of((place ^ k) * share, share), share)
        ref[:, 0:D] = mm(branch[r, :], doT[...], NT).astype(BF)
        ref[:, D : D + C] = mm(nT[r, :], dgate[...], NT).astype(BF)
        io.put("m%d" % k)
    small[...] = jnp.where(iota2((C, Q), 1) == 38, jnp.sum(acc_g[...], 1, keepdims=True), 0.0)


def backward_kernel(
    io, length, count, act, cs, rows, dec, e_in, sin, dyT, u_in, pre_in, dgate, nT, wcat, cc, cd, rc, small,
    b0, b1, b2, b3, dno, dnx, dots,
    acc, sk_rows, dact, c_rows, r_rows, ci_rows, ri_rows, kk, dA, ain, run, vw, dye, small_s, dla_s, sums, dproj, dn_s,
):
    T = act.shape[1]
    CH = T // Q
    C = dyT.shape[0]
    HH = C // PS
    zeros = jnp.zeros((64, Q), BF)

    io.need("rows")
    io.need("cs")

    @pairs(CH, lambda k: io.need("dyT", k))
    def _(c):
        l = lanes(c)
        ecue = jnp.exp(rows[CUE : CUE + 24, l])
        for h in range(HH):
            dy = dyT[64 * h : 64 * h + 64, l].astype(F32)
            dye[64 * h : 64 * h + 64, 0:Q] = (dy * ecue[h : h + 1]).astype(BF)
            dye[64 * h : 64 * h + 64, Q : 2 * Q] = (dy * ecue[HH + h : HH + h + 1]).astype(BF)
        both = jnp.concatenate(
            [
                jnp.concatenate([cs[0:64, l], zeros], 1),
                jnp.concatenate([zeros, cs[64:128, l]], 1),
            ],
            0,
        )
        dA[c] = mm(dye[...], both, NT)

    io.need("dec")
    io.need("sin")
    run[...] = jnp.zeros_like(run)
    low = iota2((64, Q), 1) < 64
    low_h = iota2((HH, Q), 1) < 64

    @pl.loop(0, CH)
    def _(i):
        f = CH - 1 - i
        d = jnp.where(low_h, dec[f][0:HH], dec[i][HH : 2 * HH])
        for h in range(HH):
            r = slice(64 * h, 64 * h + 64)
            now = run[r, :]
            ain[i, r, :] = now.astype(BF)
            flow = jnp.sum(now * sin[f, r, :].astype(F32), 0, keepdims=True) * d[h : h + 1]
            kk[i, h : h + 1, :] = flow
            run[r, :] = now * d[h : h + 1] + jnp.where(low, dA[f, r, :], dA[i, r, :])

    io.need("act")
    io.need("cc")
    sk_rows[...] = jnp.zeros_like(sk_rows)
    before = iota2((Q, Q), 1) < iota2((Q, Q), 0)
    after = iota2((Q, Q), 1) > iota2((Q, Q), 0)
    left = iota2((Q, Q), 1) < 64
    top = iota2((Q, Q), 0) < 64
    lane = iota2((Q, Q), 1)

    @pl.loop(0, CH)
    def _(c):
        l = lanes(c)

        @pl.when(c % 2 == 0)
        def _():
            io.need("e_in", c // 2)

        bf = act[C : C + 64, l]
        bb = act[C + 128 : C + 192, l]
        cf = cs[0:64, l]
        cb = cs[64:128, l]
        gf = mm(cf.astype(F32).T.astype(BF), bf)
        gb = mm(cb.astype(F32).T.astype(BF), bb)
        g = jnp.where(before, gf, jnp.where(after, gb, 0.0))
        ecue = jnp.exp(rows[CUE : CUE + 24, l])
        w = jnp.exp(
            jnp.where(
                iota2((24, Q), 0) < HH,
                rows[CUM : CUM + 24, l][:, Q - 1 : Q],
                rows[CUM : CUM + 24, l][:, 0:1],
            )
            - rows[CUM : CUM + 24, l]
        ) * rows[DT : DT + 24, l]
        for h in range(HH):
            r = slice(64 * h, 64 * h + 64)
            dy = dyT[r, l].astype(F32)
            v = act[r, l].astype(F32)
            dye[r, 0:Q] = (dy * ecue[h : h + 1]).astype(BF)
            dye[r, Q : 2 * Q] = (dy * ecue[HH + h : HH + h + 1]).astype(BF)
            vw[r, 0:Q] = (v * w[h : h + 1]).astype(BF)
            vw[r, Q : 2 * Q] = (v * w[HH + h : HH + h + 1]).astype(BF)
        zc = jnp.zeros((64, Q), BF)
        sf = sin[c]
        sb = sin[CH - 1 - c]
        af = ain[CH - 1 - c]
        ab = ain[c]
        yf = mm(sf, jnp.concatenate([cf, zc], 0))
        yb = mm(sb, jnp.concatenate([zc, cb], 0))
        vf = mm(af, jnp.concatenate([bf, zc], 0))
        vb = mm(ab, jnp.concatenate([zc, bb], 0))
        dcf = mm(sf.astype(F32).T.astype(BF)[0:64], dye[:, 0:Q])
        dcb = mm(sb.astype(F32).T.astype(BF)[64:128], dye[:, Q : 2 * Q])
        dbf = mm(af.astype(F32).T.astype(BF)[0:64], vw[:, 0:Q])
        dbb = mm(ab.astype(F32).T.astype(BF)[64:128], vw[:, Q : 2 * Q])
        dg = jnp.zeros((Q, Q), F32)
        rc_cols = jnp.zeros((Q, Q), F32)
        for j in range(HH // 2):
            r2 = slice(128 * j, 128 * j + 128)
            v = act[r2, l]
            dy = dyT[r2, l]
            dy_f = dy.astype(F32)
            dyt = dy_f.T.astype(BF)
            zb = jnp.zeros_like(dyt)
            dm2 = mm(jnp.concatenate([jnp.where(left, dyt, zb), jnp.where(left, zb, dyt)], 0), v)
            ms = []
            for k in (0, 1):
                h = 2 * j + k
                e = e_in[c, h].astype(F32)
                x = e * dm2[Q * k : Q * k + Q]
                dg = dg + x
                t = x * g
                tf = jnp.where(before, t, 0.0)
                ms.append((e * g).astype(BF))
                c_all = jnp.sum(t, 0, keepdims=True)
                c_f = jnp.sum(tf, 0, keepdims=True)
                c_rows[h : h + 1, l] = c_f
                c_rows[HH + h : HH + h + 1, l] = c_all - c_f
                r_all = jnp.sum(t, 1, keepdims=True)
                r_f = jnp.sum(tf, 1, keepdims=True)
                rc_cols = jnp.where(lane == h, r_f, rc_cols)
                rc_cols = jnp.where(lane == HH + h, r_all - r_f, rc_cols)
            dv = mm(
                jnp.concatenate([jnp.where(top, dy, zb), jnp.where(top, zb, dy)], 1),
                jnp.concatenate(ms, 0),
            )
            for k in (0, 1):
                h = 2 * j + k
                r = slice(64 * h, 64 * h + 64)
                v1 = v[64 * k : 64 * k + 64].astype(F32)
                dy1 = dy_f[64 * k : 64 * k + 64]
                sk_rows[h : h + 1, l] = jnp.sum(v1 * dy1, 0, keepdims=True)
                f_in = vf[r] * w[h : h + 1]
                b_in = vb[r] * w[HH + h : HH + h + 1]
                ci_rows[h : h + 1, l] = jnp.sum(f_in * v1, 0, keepdims=True)
                ci_rows[HH + h : HH + h + 1, l] = jnp.sum(b_in * v1, 0, keepdims=True)
                ri_rows[h : h + 1, l] = jnp.sum(yf[r] * dy1, 0, keepdims=True) * ecue[h : h + 1]
                ri_rows[HH + h : HH + h + 1, l] = (
                    jnp.sum(yb[r] * dy1, 0, keepdims=True) * ecue[HH + h : HH + h + 1]
                )
                dact[r, l] = dv[64 * k : 64 * k + 64] + f_in + b_in + cc[r, 5:6] * dy1
        r_rows[:, l] = rc_cols.T[0:24, :]
        dgf = jnp.where(before, dg, 0.0).astype(BF)
        dgb = jnp.where(after, dg, 0.0).astype(BF)
        dact[C : C + 64, l] = dbf + mm(cf, dgf)
        dact[C + 64 : C + 128, l] = dcf + mm(bf, dgf, NT)
        dact[C + 128 : C + 192, l] = dbb + mm(cb, dgb)
        dact[C + 192 : C + 256, l] = dcb + mm(bb, dgb, NT)

    dact[C + 64 : C + 128, :] = pltpu.roll(dact[C + 64 : C + 128, :], T - 1, 1)
    dact[C + 192 : C + 256, :] = pltpu.roll(dact[C + 192 : C + 256, :], 1, 1)

    ii, jj = iota2((Q, Q), 0), iota2((Q, Q), 1)
    gt = (ii > jj).astype(F32)
    ge = (ii >= jj).astype(F32)
    lt = (ii < jj).astype(F32)
    le = (ii <= jj).astype(F32)
    first = iota2((24, Q), 0) < HH
    cat = lambda ref: jnp.concatenate([ref[:, c * Q : (c + 1) * Q] for c in range(CH)], 0)
    r_in, c_in, c_x, r_x = cat(r_rows), cat(c_rows), cat(ci_rows), cat(ri_rows)
    rt = r_in + r_x
    as_f = mm_hi(rt, gt) - mm_hi(c_in, ge) + mm_hi(c_x, lt)
    as_b = mm_hi(rt, lt) - mm_hi(c_in, le) + mm_hi(c_x, gt)
    for c in range(CH):
        k = slice(24 * c, 24 * c + 24)
        l = slice(Q * c, Q * c + Q)
        kf = jnp.sum(jnp.where(low_h, kk[CH - 1 - c], 0.0), 1, keepdims=True)
        kb = jnp.sum(jnp.where(low_h, 0.0, kk[c]), 1, keepdims=True)
        dla_s[0:HH, l] = as_f[k][0:HH] + kf
        dla_s[HH : 2 * HH, l] = as_b[k][HH : 2 * HH] + kb
    dla = dla_s[...]
    dt = rows[DT : DT + 24, :]
    rate = rc[:, 1:2]
    live = (iota2((1, T), 1) < length[0]).astype(F32)
    sig = jax.nn.sigmoid(rows[RAW : RAW + 24, :])
    direct = (c_rows[...] + ci_rows[...]) * jnp.where(dt > 0.0, sig / jnp.where(dt > 0.0, dt, 1.0), 0.0)
    draw = (direct + rate * dla * sig) * live
    g_bias = jnp.sum(draw, 1, keepdims=True)
    g_decay = jnp.sum(dla * dt, 1, keepdims=True) * rate
    g_skip = jnp.sum(sk_rows[...], 1, keepdims=True)
    io.need("dgate")
    dproj[0:C, :] = dgate[...]
    dproj[2 * C + 256 : 2 * C + 384, :] = jnp.concatenate([draw, jnp.zeros((104, T), F32)], 0).astype(BF)

    io.need("u_in")
    io.need("pre_in")
    at = iota2((ROWS, Q), 1)

    @pl.loop(0, (C + 256) // ROWS, unroll=2)
    def _(b):
        r = pl.ds(pl.multiple_of(b * ROWS, ROWS), ROWS)
        r_out = pl.ds(pl.multiple_of(b * ROWS + C, ROWS), ROWS)
        col = cc[r, :]
        ks = [jnp.broadcast_to(col[:, k : k + 1], (ROWS, Q)) for k in range(4)]
        later = [jnp.zeros((ROWS, Q), F32)] * 4
        totals = [jnp.zeros((ROWS, Q), F32)] * 5
        for c in reversed(range(CH)):
            l = slice(c * Q, c * Q + Q)
            pre = pre_in[r, l].astype(F32)
            sg = jax.nn.sigmoid(pre)
            dp = dact[r, l] * (sg * (1.0 + pre * (1.0 - sg)))
            uu = u_in[r, l].astype(F32)
            du = ks[3] * dp
            totals[4] = totals[4] + dp
            totals[3] = totals[3] + dp * uu
            for back in (1, 2, 3):
                moved = pltpu.roll(dp, Q - back, 1)
                ahead = jnp.where(at < Q - back, moved, later[back])
                later[back] = moved
                totals[3 - back] = totals[3 - back] + ahead * uu
                du = du + ks[3 - back] * ahead
            dproj[r_out, l] = du.astype(BF)
        for k in range(5):
            sums[r, k * Q : k * Q + Q] = totals[k]

    def lane_sums(part, first_lane):
        upper = part.astype(BF)
        lower = (part - upper.astype(F32)).astype(BF)
        pick = (iota2((5 * Q, Q), 0) // Q + first_lane == iota2((5 * Q, Q), 1)).astype(BF)
        return mm(upper, pick) + mm(lower, pick)

    io.need("small")
    small_s[0:C, :] = lane_sums(sums[0:C, :], 32) + small[...]
    small_s[0:256, :] += lane_sums(sums[C : C + 256, :], 42)
    head_lane = iota2((24, Q), 1)
    heads_part = jnp.where(head_lane == 39, g_bias, jnp.where(head_lane == 40, g_decay, 0.0))
    small_s[0:24, :] += jnp.where(head_lane == 37, g_skip, heads_part)
    counted = (iota2((8, Q), 1) == 48) & (iota2((8, Q), 0) == 0)
    for k in range(4):
        at_row = k * (D // 4)
        small_s[at_row : at_row + 8, :] += jnp.where(counted, count[0], 0.0)
    io.need("nT")
    io.need("wcat")
    io.need("cd")
    half = dno.shape[0]
    m = lax.axis_index("tensor")
    own = pl.multiple_of(m * half, half)
    other = pl.multiple_of((1 - m) * half, half)
    W = 2 * C + 256
    acc[...] = jnp.zeros_like(acc)

    @pl.loop(0, T // 256, unroll=2)
    def _(j):
        l = lanes(j, 256)
        dn = mm(wcat[...], dproj[:, l])
        dn_s[...] = dn * cd[:, 0:1]
        part = dn * nT[:, l].astype(F32)
        acc[...] += part[:, 0:Q] + part[:, Q : 2 * Q]
        dot = jnp.sum(part, 0, keepdims=True)
        dots[:, l] = jnp.broadcast_to(dot, (8, 256))
        dno[:, l] = dn_s[pl.ds(own, half), :].astype(BF)
        dnx[0:half, l] = dn_s[pl.ds(other, half), :].astype(BF)
        top_part = dot.astype(BF).astype(F32)
        row = iota2((16, 256), 0)
        dnx[half : half + 16, l] = jnp.where(
            row == 0, top_part, jnp.where(row == 1, dot - top_part, 0.0)
        ).astype(BF)
        io.put("dno", j)
        io.put("dnx", j)

    wide = jnp.sum(acc[...], 1, keepdims=True) / cd[:, 0:1]
    small_s[...] += jnp.where(iota2((D, Q), 1) == 41, wide, 0.0)
    place = lax.axis_index("dp") % 4
    share = b0.shape[0]
    for k, ref in enumerate((b0, b1, b2, b3)):
        r = pl.ds(pl.multiple_of((place ^ k) * share, share), share)
        n = nT[r, :]
        ref[:, 0:C] = mm(n, dproj[C : 2 * C, :], NT).astype(BF)
        ref[:, C + Q : C + Q + 256] = mm(n, dproj[2 * C : W, :], NT).astype(BF)
        fine = mm(n, dproj[W : W + Q, :], NT) + small_s[r, :]
        upper = fine.astype(BF)
        ref[:, C : C + Q] = upper + pltpu.roll(fine - upper.astype(F32), 64, 1).astype(BF)
        io.put("b%d" % k)


def last_kernel(io, dno, dnr, do_s, d0, inv_s, xT, out, x_s, sems):
    T = xT.shape[1]
    half = dno.shape[0]
    own = pl.multiple_of(lax.axis_index("tensor") * half, half)

    def copy(k):
        return pltpu.make_async_copy(xT.at[pl.ds(own, half), lanes(k, 512)], x_s.at[:, lanes(k, 512)], sems.at[k])

    for k in range(T // 512):
        copy(k).start()

    def arrive(k):
        copy(k).wait()
        for n in ("dno", "dnr", "do_s"):
            io.need(n, k)

    @pairs(T // 256, arrive, lambda k: io.put("out", k))
    def _(c):
        l = lanes(c, 256)
        inv = inv_s[0:1, l]
        sent = dnr[half : half + 16, l].astype(F32)
        k3 = inv * inv * (d0[0:1, l] + sent[0:1] + sent[1:2]) / D
        e2 = dno[:, l].astype(F32) + dnr[0:half, l].astype(F32)
        dx = inv * e2 - x_s[:, l].astype(F32) * k3 + do_s[:, l].astype(F32)
        out[l, :] = dx.astype(BF).T


def finish_first_kernel(io, own, h0, h1, h2, h3, wo, wg, *, full_len):
    share = h0.shape[0]
    C = wg.shape[1]
    place = lax.axis_index("dp") % 4
    mid = own[...].astype(F32)
    scale = full_len / (mid + pltpu.roll(mid, 64, 1))[0:1, 48:49]
    for k, ref in enumerate((h0, h1, h2, h3)):
        io.need("h%d" % k)
        r = pl.ds(pl.multiple_of((place ^ k) * share, share), share)
        wo[r, :] = ref[:, 0:D].astype(F32) * scale
        wg[r, :] = ref[:, D : D + C].astype(F32) * scale
    io.put("wo")
    io.put("wg")


def finish_kernel(
    io, dealing, g0, g1, g2, g3, back,
    gv, gt, gs, ng, cv, vb, cst, sb, dl, sk, og, bias, grad_in,
    sm, *, full_len
):
    share = g0.shape[0]
    C = gv.shape[1]
    HH = C // PS
    place = lax.axis_index("dp") % 4
    scale = None
    for k, ref in enumerate((g0, g1, g2, g3)):
        r = pl.ds(pl.multiple_of((place ^ k) * share, share), share)
        io.need("g%d" % k)
        mid = ref[:, C : C + Q].astype(F32)
        mid = mid + pltpu.roll(mid, 64, 1)
        scale = full_len / mid[0:1, 48:49]
        sm[r, :] = mid * scale
        gv[r, :] = ref[:, 0:C].astype(F32) * scale
        gs[r, :] = ref[:, C + Q : C + Q + 256].astype(F32) * scale
    io.put("gv")
    io.put("gs")
    io.need("back")

    @pl.loop(0, grad_in.shape[0])
    def _(k):
        grad_in[dealing[k]] = (back[k].astype(F32) * scale).astype(BF)

    io.put("grad_in")
    scaled = sm[...]
    gt[...] = scaled[:, 0 : 2 * HH]
    turned = scaled.T
    ng[...] = turned[41]
    cv[...] = turned[32:36]
    vb[...] = turned[36]
    cst[...] = turned[42:46, 0:256]
    sb[...] = turned[46, 0:256]
    og[...] = turned[38]
    dl[...] = turned[40, 0:HH] + turned[40, HH : 2 * HH]
    bias[0:1, :] = turned[39:40, 0:HH]
    bias[1:2, :] = turned[39:40, HH : 2 * HH]
    sk[...] = turned[37, 0:HH]


class Flow:
    def __init__(self, sems):
        self.sems, self.table, self.used = sems, {}, 0

    def add(self, name, src, dst, axis, count):
        self.table[name] = (src, dst, axis, count, self.used)
        self.used += count

    def copy(self, name, piece):
        src, dst, axis, count, first = self.table[name]
        if count > 1:
            width = src.shape[axis] // count
            at = pl.ds(pl.multiple_of(piece * width, width), width)
            where = (at,) if axis == 0 else (slice(None), at)
            src, dst = src.at[where], dst.at[where]
        return pltpu.make_async_copy(src, dst, self.sems.at[first + piece])

    def put(self, name, piece=0):
        self.copy(name, piece).start()

    def need(self, name, piece=0):
        self.copy(name, piece).wait()


def call(body, outs, scratch, args, smem, name, us=1.0, late=None, early=None, raw=(), limit=58, static=None):
    late, early = late or {}, early or {}
    kinds = [pltpu.VMEM(*x) if isinstance(x, tuple) else x for x in scratch]
    names = list(inspect.signature(body).parameters)[1:]
    body = functools.partial(body, **static) if static else body
    n_in, n_out, n_own = len(args), len(outs), len(scratch)
    late_at = {n: names.index(n) for n in late}
    early_at = {n: names.index(n) - n_in for n in early}
    total = sum(c for _, c in late.values()) + sum(c for _, c in early.values())

    def wrapped(*refs):
        refs = list(refs)
        sems = refs.pop() if total else None
        flow = Flow(sems)
        bufs = refs[n_in + n_out + n_own :]
        for n, buf in zip([*late, *early], bufs):
            if n in late:
                at = late_at[n]
                flow.add(n, refs[at], buf, *late[n])
            else:
                at = n_in + early_at[n]
                flow.add(n, buf, refs[at], *early[n])
            refs[at] = buf
        waiting = list(late)
        while waiting:
            count = late[waiting[0]][1]
            group = []
            while waiting and late[waiting[0]][1] == count:
                group.append(waiting.pop(0))
            for piece in range(count):
                for n in group:
                    flow.put(n, piece)
        body(flow, *refs[: n_in + n_out + n_own])
        for n, (_, count) in early.items():
            for piece in range(count):
                flow.need(n, piece)

    vmem, any_ = pltpu.VMEM, pl.ANY
    in_specs = [
        pl.BlockSpec(
            memory_space=pltpu.SMEM if i < smem else any_ if i in late_at.values() or names[i] in raw else vmem
        )
        for i in range(n_in)
    ]
    out_specs = [
        pl.BlockSpec(memory_space=any_ if i in early_at.values() or names[n_in + i] in raw else vmem)
        for i in range(n_out)
    ]
    bufs = [pltpu.VMEM(args[late_at[n]].shape, args[late_at[n]].dtype) for n in late]
    bufs += [pltpu.VMEM(*outs[early_at[n]]) for n in early]
    return pl.pallas_call(
        wrapped,
        out_shape=[jax.ShapeDtypeStruct(s, d) for s, d in outs],
        in_specs=in_specs,
        out_specs=out_specs,
        scratch_shapes=kinds
        + bufs
        + ([pltpu.SemaphoreType.DMA((total,))] if total else []),
        compiler_params=pltpu.CompilerParams(vmem_limit_bytes=limit * 1024 * 1024),
        cost_estimate=pl.CostEstimate(
            flops=int(us * 9e8), bytes_accessed=int(us * 3e6), transcendentals=0
        ),
        name=name,
    )(*args)


def swap(x):
    return lax.ppermute(x, "tensor", [(0, 1), (1, 0)])


def across(x, groups, bit):
    return lax.ppermute(x, "dp", [(i, i ^ bit) for i in range(groups)])


def phases_of(groups):
    found, weight = [], 1
    while weight < groups:
        members = min(4, groups // weight)
        found.append((weight, members))
        weight *= members
    return found


def send_round(blocks, groups, weight):
    return [blocks[0]] + [across(b, groups, k * weight) for k, b in enumerate(blocks) if k]


def resplit(x, at):
    value = x[:, at : at + 64] + x[:, at + 64 : at + 128]
    upper = lax.reduce_precision(value, 8, 7)
    return jnp.concatenate([x[:, :at], upper, value - upper, x[:, at + 128 :]], 1)


def split(x, rank, weight, members):
    rows = x.shape[0] // members
    place = (rank // weight) % members
    return [lax.dynamic_slice_in_dim(x, (place ^ k) * rows, rows, 0) for k in range(members)]


def assemble(got, rank, weight):
    members = len(got)
    place = (rank // weight) % members
    parts = []
    for i in range(members):
        now = got[i]
        for p in range(1, members):
            now = jnp.where(place == p, got[i ^ p], now)
        parts.append(now)
    return jnp.concatenate(parts, 0)


def on_device(
    hidden_in, teacher, loss_mask, lengths, dealing, norm_gain, w_gate, w_value, w_state, w_step,
    step_bias, conv_value, conv_vbias, conv_state, conv_sbias, decay_log, skip_gain, out_gain, w_out,
):
    groups = lax.axis_size("dp")
    rank = lax.axis_index("dp")
    member = lax.axis_index("tensor")
    seqs, local, _ = hidden_in.shape
    half = teacher.shape[2]
    T = local * groups
    C = w_gate.shape[1]
    HH = decay_log.shape[0]
    CH = T // Q

    [dealt] = call(deal_kernel, [((seqs, local, half), BF)], [], (dealing, hidden_in), 1, "deal", 3.0)
    dealt, loss_mask, teacher, w_gate = lax.optimization_barrier((dealt, loss_mask, teacher, w_gate))
    xo = lax.all_to_all(dealt, "dp", split_axis=0, concat_axis=0, tiled=True).reshape(T, half)

    pos = rank * local + lax.broadcasted_iota(jnp.int32, (seqs, local), 1)
    marks = (loss_mask > 0) & (pos < lengths[:, None])
    count = jnp.sum(marks.astype(F32)).reshape(1)
    goal = jnp.where(marks[:, :, None], teacher, jnp.asarray(NOMARK, BF))
    [goal] = call(deal_kernel, [((seqs, local, half), BF)], [], (dealing, goal), 1, "deal_goal", 2.0)
    length = lax.dynamic_slice_in_dim(lengths, dealing[rank], 1, 0)

    wcat, wt, wot, cd = call(
        prepare_kernel,
        [((D, 2 * C + 384), BF), ((2 * C + 384, D), BF), ((D, C), BF), ((D, 8), F32)],
        [],
        (w_gate, w_value, w_state, w_step.reshape(D, 2 * HH), w_out, norm_gain[None]),
        0,
        "prepare",
        6.0,
        early={"wcat": (0, 1), "wt": (0, 1)},
    )
    zc = jnp.zeros((256,), F32)
    cc = jnp.concatenate(
        [
            jnp.concatenate([conv_value, conv_state], 1),
            jnp.concatenate([conv_vbias, conv_sbias])[None],
            jnp.concatenate([jnp.repeat(skip_gain, PS), zc])[None],
            jnp.concatenate([out_gain, zc])[None],
            jnp.zeros((1, C + 256), F32),
        ],
        0,
    ).T
    rate = -jnp.exp(decay_log)
    rc = jnp.stack([step_bias.reshape(-1), jnp.concatenate([rate, rate])], 1)

    xo, goal, wcat, wt, wot, cc, cd, rc, count, length = lax.optimization_barrier(
        (xo, goal, wcat, wt, wot, cc, cd, rc, count, length)
    )
    xs = swap(xo)
    to = lax.all_to_all(goal, "dp", split_axis=0, concat_axis=0, tiled=True).reshape(T, half)
    ts = swap(to)

    full = lambda n: ((n, T), BF)
    fullf = lambda n: ((n, T), F32)
    xT, nT, rows, dec, gate, u, pre, act, cs, e, mixed, sin, p0, inv = call(
        forward_kernel,
        [
            full(D), full(D), fullf(120), ((CH, 24, Q), F32), fullf(C), full(C + 256), full(C + 256),
            full(C + 256), full(128), ((CH, HH, Q, Q), BF), fullf(C), ((CH, C, Q), BF), full(D + 16), fullf(8),
        ],
        [
            ((C + 256, T), F32), ((32, T), F32), ((24, T), F32), ((CH, C, Q), F32), ((C, Q), F32),
            ((C, 2 * Q), BF), ((C, T), BF),
        ],
        (length, xo, xs, wt, wot, cc, cd, rc),
        1,
        "forward",
        26.0,
        late={"xo": (0, CH // 2), "xs": (0, CH // 2), "wt": (0, 1), "cc": (0, 1), "wot": (0, 1)},
        early={
            **{n: (0, 1) for n in ("xT", "nT", "rows", "dec", "gate", "uO", "preO", "act", "cs", "sin")},
            "mixed": (1, CH // 2),
            "eO": (0, CH // 2), "pO": (1, T // 256),
        },
    )
    p1 = swap(p0)
    lo, doh, dyT, dgate, small, *mids = call(
        middle_kernel,
        [((T, half), BF), full(half), full(C), full(C), ((C, Q), F32)] + [((D // 4, D + C), BF)] * 4,
        [
            ((D, Q), F32), ((D, Q), F32), ((C, T), BF), ((C, 256), F32), ((8, T), F32), ((C, Q), F32),
            ((8, T), F32), full(D),
        ],
        (p0, p1, xT, to, ts, w_out, nT, gate, mixed, cc),
        0,
        "middle",
        14.0,
        late={
            **{n: (1, CH // 2) for n in ("p0", "p1", "xT")}, "to": (0, CH // 2), "ts": (0, CH // 2),
            "wo": (0, 1), "cc": (0, 1), "gate": (1, T // 256), "mixed": (1, T // 256), "nT": (0, 1),
        },
        early={
            "dyT": (1, T // 256), **{n: (0, 1) for n in ("doh", "lo", "dgate", "m0", "m1", "m2", "m3")},
        },
    )
    phases = phases_of(groups)
    got_m = send_round(mids, groups, 1)
    rowsf = ((24, T), F32)
    width = C + Q + 256
    b0, b1, b2, b3, dno, dnx, dots = call(
        backward_kernel,
        [((D // 4, width), BF)] * 4 + [full(half), full(half + 16), fullf(8)],
        [
            ((D, Q), F32), rowsf, fullf(C + 256), rowsf, rowsf, rowsf, rowsf, ((CH, HH, Q), F32), ((CH, C, Q), F32),
            ((CH, C, Q), BF), ((C, Q), F32), ((C, 2 * Q), BF), ((C, 2 * Q), BF), ((C, Q), F32), rowsf,
            ((C + 256, 5 * Q), F32), full(2 * C + 384), ((D, 256), F32),
        ],
        (length, count, act, cs, rows, dec, e, sin, dyT, u, pre, dgate, nT, wcat, cc, cd, rc, small),
        2,
        "backward",
        30.0,
        late={
            **{n: (0, 1) for n in ("rows", "cs")},
            "dyT": (1, CH // 2),
            **{n: (0, 1) for n in ("dec", "sin", "act", "cc")},
            "e_in": (0, CH // 2),
            **{n: (0, 1) for n in ("dgate", "u_in", "pre_in", "small", "nT", "wcat", "cd")},
        },
        early={
            "dno": (1, T // 256), "dnx": (1, T // 256), **{n: (0, 1) for n in ("b0", "b1", "b2", "b3")},
        },
    )
    now_m = sum(g.astype(F32) for g in got_m)
    dnr = swap(dnx)
    now_m, dnr = lax.optimization_barrier((now_m, dnr))
    blocks = split(now_m, rank, *phases[1])
    got_m = send_round([b if k == 0 else b.astype(BF) for k, b in enumerate(blocks)], groups, phases[1][0])
    got = send_round([b0, b1, b2, b3], groups, 1)
    [dx] = call(
        last_kernel,
        [((T, half), BF)],
        [((half, T), BF), pltpu.SemaphoreType.DMA((CH,))],
        (dno, dnr, doh, dots, inv, xT),
        0,
        "last",
        3.0,
        late={n: (1, T // 512) for n in ("dno", "dnr", "do_s")},
        early={"out": (0, T // 512)},
        raw=("xT",),
    )
    dx, got, got_m = lax.optimization_barrier((dx, got, got_m))
    held = sum(g.astype(F32) for g in got_m)
    for weight, members in phases[2:]:
        blocks = split(held, rank, weight, members)
        got_m = send_round([b if k == 0 else b.astype(BF) for k, b in enumerate(blocks)], groups, weight)
        held = sum(g.astype(F32) for g in got_m)
    held = held.astype(BF)
    now = resplit(sum(g.astype(F32) for g in got), C)
    for weight, members in reversed(phases[1:]):
        pieces = send_round([held] * members, groups, weight)
        now, pieces = lax.optimization_barrier((now, pieces))
        held = assemble(pieces, rank, weight)
    held = send_round([held] * 4, groups, 1)
    for weight, members in phases[1:]:
        blocks = split(now, rank, weight, members)
        got = send_round([b if k == 0 else b.astype(BF) for k, b in enumerate(blocks)], groups, weight)
        now = resplit(sum(g.astype(F32) for g in got), C)
    lane = lax.broadcasted_iota(jnp.int32, (1, Q + 256), 1)
    both = (lane >= Q) | ((lane % 64 >= 41) & (lane % 64 < 47))
    tail = now[:, C:]
    tail = resplit(tail + jnp.where(both, swap(tail.astype(BF)).astype(F32), 0.0), 0)
    now = jnp.concatenate([now[:, :C], tail], 1).astype(BF)
    now, held = lax.optimization_barrier((now, held))
    for weight, members in reversed(phases[1:]):
        now = assemble(send_round([now] * members, groups, weight), rank, weight)
    got = send_round([now] * 4, groups, 1)
    back = lax.all_to_all(dx.reshape(seqs, local, half), "dp", split_axis=0, concat_axis=0, tiled=True)
    wo, wg = call(
        finish_first_kernel,
        [((C, D), F32), ((D, C), F32)],
        [],
        (now[0:8, C : C + Q], *held),
        0,
        "finish_first",
        5.0,
        late={n: (0, 1) for n in ("h0", "h1", "h2", "h3")},
        early={n: (0, 1) for n in ("wo", "wg")},
        static={"full_len": T},
    )
    gv, gt, gs, ng, cv, vb, cst, sb, dl, sk, og, bias, grad_in = call(
        finish_kernel,
        [
            ((D, C), F32), ((D, 2 * HH), F32), ((D, 256), F32), ((D,), F32), ((4, C), F32), ((C,), F32),
            ((4, 256), F32), ((256,), F32), ((HH,), F32), ((HH,), F32), ((C,), F32), ((2, HH), F32),
            ((seqs, local, half), BF),
        ],
        [((D, Q), F32)],
        (dealing, *got, back),
        1,
        "finish",
        4.0,
        late={n: (0, 1) for n in ("g0", "g1", "g2", "g3", "back")},
        early={n: (0, 1) for n in ("gv", "gs", "grad_in")},
        static={"full_len": T},
    )
    return (
        lo[None], grad_in, ng, wg, gv, gs, gt.reshape(D, 2, HH), bias, cv, vb, cst, sb, dl, sk, og, wo,
    )


def solution(mesh):
    dp, tp = "dp", "tensor"
    return jax.shard_map(
        on_device,
        mesh=mesh,
        in_specs=(
            P(None, dp, None), P(None, dp, tp), P(None, dp), P(), P(), P(), P(None, tp), P(None, tp), P(),
            P(None, None, tp), P(None, tp), P(None, tp), P(tp), P(), P(), P(tp), P(tp), P(tp), P(tp, None),
        ),
        out_specs=(
            P(dp, None, tp), P(None, dp, tp), P(), P(None, tp), P(None, tp), P(), P(None, None, tp),
            P(None, tp), P(None, tp), P(tp), P(), P(), P(tp), P(tp), P(tp), P(tp, None),
        ),
        check_vma=False,
    )
```

time: 318 us -> 243 us (0.76)
  Pallas kernels: 137 us -> 106 us
  waiting for transfers between devices: 80.4 us -> 63.4 us
  between operations: 17.2 us -> 3.21 us
  local copies, waits for them, and re-layouts: 22.7 us -> 11.5 us
  other arithmetic: 7.99 us -> 3.13 us
    pallas_call x10 -> x9, Pallas kernels: 137 us -> 106 us  [call(): pl.pallas_call(wrapped, out_shape=[jax.ShapeDtypeStruct(s, d) for s, d in...]
    ppermute x22 -> x24, waiting for transfers between devices: 75.1 us -> 56.6 us  [across(): return lax.ppermute(x, 'dp', [(i, i ^ bit) for i in range(groups)])]
    concatenate x1 -> x0, local copies, waits for them, and re-layouts: 3.73 us -> none  [on_device(): jnp.concatenate([w_gate, w_value, w_state, w_step.reshape(D, 2 * HH), jnp...]
    optimization_barrier x3 -> x1, local copies, waits for them, and re-layouts: 4.46 us -> 0.81 us  [on_device(): lax.optimization_barrier((xo, goal, wcat, wt, wot, cc, cd, rc, count, len...]
    ppermute x22 -> x24, starting transfers between devices: 37.7 us -> 35.8 us  [across(): return lax.ppermute(x, 'dp', [(i, i ^ bit) for i in range(groups)])]
  transfers between devices with their start and end apart: 31 -> 32, of which waited for: 14 -> 15; matrix products, arithmetic and copies ran while one was open for 6% -> 4% of each run, Pallas kernels for 24% -> 34%
where the time goes in v2:
time: 243 us; the launch traced here: 242 us
  Pallas kernels  106 us (44%)
  waiting for transfers between devices  63.4 us (26%)
  starting transfers between devices  55 us (23%)
  local copies, waits for them, and re-layouts  11.5 us (5%)
  between operations  3.21 us (1%)
  other arithmetic  3.13 us (1%)
    pallas_call x9, Pallas kernels, call(): pl.pallas_call(wrapped, out_shape=[jax.ShapeDtypeStruct(s, d) for s, d in...  106 us
    ppermute x24, waiting for transfers between devices, across(): return lax.ppermute(x, 'dp', [(i, i ^ bit) for i in range(groups)])  56.6 us
    ppermute x24, starting transfers between devices, across(): return lax.ppermute(x, 'dp', [(i, i ^ bit) for i in range(groups)])  35.8 us
    all_to_all x1, starting transfers between devices, on_device(): lax.all_to_all(dealt, 'dp', split_axis=0, concat_axis=0, tiled=True)  8.46 us
    all_to_all x1, starting transfers between devices, on_device(): lax.all_to_all(dx.reshape(seqs, local, half), 'dp', split_axis=0, concat_...  5.16 us
    all_to_all x1, starting transfers between devices, on_device(): lax.all_to_all(goal, 'dp', split_axis=0, concat_axis=0, tiled=True)  4.91 us
  transfers between devices with their start and end apart: 32, of which 15 were waited for; matrix products, arithmetic and copies ran while one was open for 4% of the time, Pallas kernels for 34%

profile of v2, /device:TPU:0, one launch (start us, length us, event | category | flops | bytes accessed | tf_op | source)
XLA Modules:
  0.0 242.3 jit_solution(6513416695172624503)
XLA Ops:
  0.6 2.5 %deal.1 = bf16[16,64,384]{2,1,0:T(8,128)(2,1)} custom-call(s32[16]{0:T(128)} %refs_0_.6, bf16[16,64,768]{2,1,0:T(8,128)(2,1)} %refs_1_.2), custom_call_target="tpu_custom_call" | custom-call | flops 2700000000 | bytes 9000000 | tf_op jit(solution)/shard_map/deal/pallas_call | solution.py:831
  3.3 8.5 %all-to-all-start = ((bf16[16,64,384]{2,1,0:T(8,128)(2,1)}), bf16[16,64,384]{2,1,0:T(8,128)(2,1)S(1)}, u32[]{:S(2)}, u32[]{:S(2)}) async-start(bf16[16,64,384]{2,1,0:T(8,128)(2,1)} %deal.1), calls=%async_computation | async-start | bytes 1572864 | tf_op jit(solution)/shard_map/all_to_all | solution.py:908
  21.8 7.2 %prepare.1 = (bf16[768,1920]{1,0:T(8,128)(2,1)}, bf16[1920,768]{1,0:T(8,128)(2,1)}, bf16[768,768]{1,0:T(8,128)(2,1)}, f32[768,8]{1,0:T(8,128)}) custom-call(bf16[768,768]{1,0:T(8,128)(2,1)} %refs_0_.5, bf16[768,768]{1,0:T(8,128)(2,1)} %refs_1_.3, bf16[768,256]{1,0:T(8,128)(2,1)} %refs_2_.1, bf16[768,24]{1,0:T(8,128)(2,1)} %copy.53.refs_3_, ...), custom_call_target="tpu_custom_call" | custom-call | flops 5400000000 | bytes 18000000 | tf_op jit(solution)/shard_map/prepare/pallas_call | solution.py:831
  29.0 2.5 %all-to-all-done = bf16[16,64,384]{2,1,0:T(8,128)(2,1)S(1)} async-done(((bf16[16,64,384]{2,1,0:T(8,128)(2,1)}), bf16[16,64,384]{2,1,0:T(8,128)(2,1)S(1)}, u32[]{:S(2)}, u32[]{:S(2)}) %all-to-all-start) | async-done | bytes 786464 | tf_op jit(solution)/shard_map/all_to_all | solution.py:908
  32.3 4.9 %all-to-all-start.1 = ((bf16[16,64,384]{2,1,0:T(8,128)(2,1)}), bf16[16,64,384]{2,1,0:T(8,128)(2,1)S(1)}, u32[]{:S(2)}, u32[]{:S(2)}) async-start(bf16[16,64,384]{2,1,0:T(8,128)(2,1)} %deal_goal.1), calls=%async_computation.1 | async-start | bytes 1572864 | tf_op jit(solution)/shard_map/all_to_all | solution.py:945
  38.1 28.1 %forward.1 = (bf16[768,1024]{1,0:T(8,128)(2,1)}, bf16[768,1024]{1,0:T(8,128)(2,1)}, f32[120,1024]{1,0:T(8,128)}, f32[8,24,128]{2,1,0:T(8,128)}, f32[768,1024]{1,...) custom-call(s32[1]{0:T(128)} %dynamic_slice.31.refs_0_, ...), custom_call_target="tpu_custom_call" | custom-call | flops 23399999488 | bytes 78000000 | tf_op jit(solution)/shard_map/forward/pallas_call | solution.py:831
  66.8 3.9 %collective-permute-done.2.refs_4_ = bf16[1024,384]{1,0:T(8,128)(2,1)S(1)} collective-permute-done((bf16[1024,384]{1,0:T(8,128)(2,1)S(1)}, bf16[1024,384]{1,0:T(8,128)(2,1)S(1)}, u32[]{:S(2)}, u32[]{:S(2)}) %collective-permute-start.2) | collective-permute-done | bytes 786464 | tf_op jit(solution)/shard_map/ppermute | solution.py:848
  72.3 16.2 %middle.1 = (bf16[1024,384]{1,0:T(8,128)(2,1)}, bf16[384,1024]{1,0:T(8,128)(2,1)}, bf16[768,1024]{1,0:T(8,128)(2,1)}, bf16[768,1024]{1,0:T(8,128)(2,1)}, f32[768...) custom-call(bf16[784,1024]{1,0:T(8,128)(2,1)} %get-tuple-element.115, ...), custom_call_target="tpu_custom_call" | custom-call | flops 12600000512 | bytes 42000000 | tf_op jit(solution)/shard_map/middle/pallas_call | solution.py:831
  92.1 35.8 %backward.1 = (bf16[192,1152]{1,0:T(8,128)(2,1)}, bf16[192,1152]{1,0:T(8,128)(2,1)}, bf16[192,1152]{1,0:T(8,128)(2,1)}, bf16[192,1152]{1,0:T(8,128)(2,1)}, bf16[...) custom-call(s32[1]{0:T(128)} %dynamic_slice.31.refs_0_, f32[1]{0:T(128)} %bitcast.6.refs_1_, ...), custom_call_target="tpu_custom_call" | custom-call | flops 27000000512 | bytes 90000000 | tf_op jit(solution)/shard_map/backward/pallas_call | solution.py:831
  134.0 2.4 collective-permute-start.11
  136.3 4.0 %last.1 = bf16[1024,384]{1,0:T(8,128)(2,1)} custom-call(bf16[384,1024]{1,0:T(8,128)(2,1)} %get-tuple-element.135.refs_0_, bf16[400,1024]{1,0:T(8,128)(2,1)} %collective-permute-done.6.refs_1_, bf16[384,1024]{1,0:T(8,128)(2,1)} %get-tuple-element.142.refs_2_, f32[8,1024]{1,0:T(8,128)} %get-tuple-element.143.refs_3_, f32[8,1024]{1,0:T(8,128)} %get-tuple-element.144.refs_4_, ...), custom_call_target="tpu_custom_call" | custom-call | flops 2700000000 | bytes 9000000 | tf_op jit(solution)/shard_map/last/pallas_call | solution.py:831
  141.3 3.8 %collective-permute-start.12 = (bf16[48,1536]{1,0:T(8,128)(2,1)S(1)}, bf16[48,1536]{1,0:T(8,128)(2,1)S(1)}, u32[]{:S(2)}, u32[]{:S(2)}) collective-permute-start(bf16[48,1536]{1,0:T(8,128)(2,1)S(1)} %get-tuple-element.234), channel_id=1, source_target_pairs={{0,24},{2,26},{4,28},{6,30},{8,16},{10,18},{12,20},{14,22},{16,8},... | collective-permute-start | bytes 442376 | tf_op jit(solution)/shard_map/ppermute | solution.py:852
  145.1 6.8 %collective-permute-done.8 = bf16[192,1152]{1,0:T(8,128)(2,1)S(1)} collective-permute-done((bf16[192,1152]{1,0:T(8,128)(2,1)}, bf16[192,1152]{1,0:T(8,128)(2,1)S(1)}, u32[]{:S(2)}, u32[]{:S(2)}) %collective-permute-start.8) | collective-permute-done | bytes 442400 | tf_op jit(solution)/shard_map/ppermute | solution.py:852
  159.0 8.1 %collective-permute-done.14 = bf16[48,1536]{1,0:T(8,128)(2,1)S(1)} collective-permute-done((bf16[48,1536]{1,0:T(8,128)(2,1)S(1)}, bf16[48,1536]{1,0:T(8,128)(2,1)S(1)}, u32[]{:S(2)}, u32[]{:S(2)}) %collective-permute-start.14) | collective-permute-done | bytes 147488 | tf_op jit(solution)/shard_map/ppermute | solution.py:852
  175.5 3.7 %collective-permute-done.17 = bf16[48,1152]{1,0:T(8,128)(2,1)S(1)} collective-permute-done((bf16[48,1152]{1,0:T(8,128)(2,1)S(1)}, bf16[48,1152]{1,0:T(8,128)(2,1)S(1)}, u32[]{:S(2)}, u32[]{:S(2)}) %collective-permute-start.17) | collective-permute-done | bytes 110624 | tf_op jit(solution)/shard_map/ppermute | solution.py:852
  179.6 5.2 %all-to-all-start.2 = ((bf16[16,64,384]{2,1,0:T(8,128)(2,1)}), bf16[16,64,384]{2,1,0:T(8,128)(2,1)S(1)}, u32[]{:S(2)}, u32[]{:S(2)}) async-start(bf16[16,64,384]{2,1,0:T(8,128)(2,1)} %bitcast.10), calls=%async_computation.2 | async-start | bytes 1572864 | tf_op jit(solution)/shard_map/all_to_all | solution.py:1062
  185.0 3.3 %collective-permute-done.20.refs_2_ = bf16[192,1536]{1,0:T(8,128)(2,1)S(1)} collective-permute-done((bf16[192,1536]{1,0:T(8,128)(2,1)S(1)}, bf16[192,1536]{1,0:T(8,128)(2,1)S(1)}, u32[]{:S(2)}, u32[]{:S(2)}) %collective-permute-start.20) | collective-permute-done | bytes 589856 | tf_op jit(solution)/shard_map/ppermute | solution.py:852
  188.3 10.2 %collective-permute-done.21.refs_3_ = bf16[192,1536]{1,0:T(8,128)(2,1)} collective-permute-done((bf16[192,1536]{1,0:T(8,128)(2,1)S(1)}, bf16[192,1536]{1,0:T(8,128)(2,1)}, u32[]{:S(2)}, u32[]{:S(2)}) %collective-permute-start.21) | collective-permute-done | bytes 589856 | tf_op jit(solution)/shard_map/ppermute | solution.py:852
  198.5 9.2 %collective-permute-done.22.refs_4_ = bf16[192,1536]{1,0:T(8,128)(2,1)} collective-permute-done((bf16[192,1536]{1,0:T(8,128)(2,1)S(1)}, bf16[192,1536]{1,0:T(8,128)(2,1)}, u32[]{:S(2)}, u32[]{:S(2)}) %collective-permute-start.22) | collective-permute-done | bytes 589856 | tf_op jit(solution)/shard_map/ppermute | solution.py:852
  207.8 3.0 %collective-permute-start.23 = (bf16[48,1152]{1,0:T(8,128)(2,1)S(1)}, bf16[48,1152]{1,0:T(8,128)(2,1)S(1)}, u32[]{:S(2)}, u32[]{:S(2)}) collective-permute-start(bf16[48,1152]{1,0:T(8,128)(2,1)S(1)} %concatenate.42), channel_id=1, source_target_pairs={{0,24},{2,26},{4,28},{6,30},{8,16},{10,18},{12,20},{14,22},{16,8},... | collective-permute-start | bytes 331784 | tf_op jit(solution)/shard_map/ppermute | solution.py:852
  214.3 2.8 %collective-permute-done.24 = bf16[48,1152]{1,0:T(8,128)(2,1)S(1)} collective-permute-done((bf16[48,1152]{1,0:T(8,128)(2,1)S(1)}, bf16[48,1152]{1,0:T(8,128)(2,1)S(1)}, u32[]{:S(2)}, u32[]{:S(2)}) %collective-permute-start.24) | collective-permute-done | bytes 110624 | tf_op jit(solution)/shard_map/ppermute | solution.py:852
  221.4 4.6 %finish_first.1 = (f32[768,768]{1,0:T(8,128)}, f32[768,768]{1,0:T(8,128)}) custom-call(bf16[8,128]{1,0:T(8,128)(2,1)} %slice.61.refs_0_, bf16[192,1536]{1,0:T(8,128)(2,1)} %copy-done.5, bf16[192,1536]{1,0:T(8,128)(2,1)} %copy-done.21, bf16[192,1536]{1,0:T(8,128)(2,1)} %collective-permute-done.21.refs_3_, bf16[192,1536]{1,0:T(8,128)(2,1)} %collective-permute-done.22.refs_4_), custom_call_target="tpu_custom_call" | custom-call | flops 4499999744 | bytes 15000000 | tf_op jit(solution)/shard_map/finish_first/pallas_call | solution.py:831
  227.8 5.5 %collective-permute-done.27.refs_3_ = bf16[192,1152]{1,0:T(8,128)(2,1)S(1)} collective-permute-done((bf16[192,1152]{1,0:T(8,128)(2,1)S(1)}, bf16[192,1152]{1,0:T(8,128)(2,1)S(1)}, u32[]{:S(2)}, u32[]{:S(2)}) %collective-permute-start.27) | collective-permute-done | bytes 442400 | tf_op jit(solution)/shard_map/ppermute | solution.py:852
  235.1 5.4 %finish.1 = (f32[768,768]{1,0:T(8,128)}, f32[768,24]{1,0:T(8,128)}, f32[768,256]{1,0:T(8,128)}, f32[768]{0:T(1024)}, f32[4,768]{1,0:T(4,128)}, /*index=5*/f32[76...) custom-call(s32[16]{0:T(128)} %refs_0_.6, ...), custom_call_target="tpu_custom_call" | custom-call | flops 3600000000 | bytes 12000000 | tf_op jit(solution)/shard_map/finish/pallas_call | solution.py:831
  (156 shorter events, 51.6 us)
Async XLA Ops:
  3.3 28.2 %all-to-all-start = ((bf16[16,64,384]{2,1,0:T(8,128)(2,1)}), bf16[16,64,384]{2,1,0:T(8,128)(2,1)S(1)}, u32[]{:S(2)}, u32[]{:S(2)}) async-start(bf16[16,64,384]{2,1,0:T(8,128)(2,1)} %deal.1), calls=%async_computation | async-start | bytes 1572864 | tf_op jit(solution)/shard_map/all_to_all | solution.py:908
  32.3 34.1 %all-to-all-start.1 = ((bf16[16,64,384]{2,1,0:T(8,128)(2,1)}), bf16[16,64,384]{2,1,0:T(8,128)(2,1)S(1)}, u32[]{:S(2)}, u32[]{:S(2)}) async-start(bf16[16,64,384]{2,1,0:T(8,128)(2,1)} %deal_goal.1), calls=%async_computation.1 | async-start | bytes 1572864 | tf_op jit(solution)/shard_map/all_to_all | solution.py:945
  88.5 41.5 %collective-permute-start.3 = (bf16[192,1536]{1,0:T(8,128)(2,1)}, bf16[192,1536]{1,0:T(8,128)(2,1)S(1)}, u32[]{:S(2)}, u32[]{:S(2)}) collective-permute-start(bf16[192,1536]{1,0:T(8,128)(2,1)} %get-tuple-element.137), channel_id=1, source_target_pairs={{0,2},{2,0},{4,6},{6,4},{8,10},{10,8},{12,14},{14,12},{16,18},{18,... | collective-permute-start | bytes 1769480 | tf_op jit(solution)/shard_map/ppermute | solution.py:852
  90.5 41.0 %collective-permute-start.4 = (bf16[192,1536]{1,0:T(8,128)(2,1)}, bf16[192,1536]{1,0:T(8,128)(2,1)S(1)}, u32[]{:S(2)}, u32[]{:S(2)}) collective-permute-start(bf16[192,1536]{1,0:T(8,128)(2,1)} %get-tuple-element.138), channel_id=1, source_target_pairs={{0,4},{2,6},{4,0},{6,2},{8,12},{10,14},{12,8},{14,10},{16,20},{18,... | collective-permute-start | bytes 1769480 | tf_op jit(solution)/shard_map/ppermute | solution.py:852
  91.9 39.7 %collective-permute-start.5 = (bf16[192,1536]{1,0:T(8,128)(2,1)}, bf16[192,1536]{1,0:T(8,128)(2,1)S(1)}, u32[]{:S(2)}, u32[]{:S(2)}) collective-permute-start(bf16[192,1536]{1,0:T(8,128)(2,1)} %get-tuple-element.139), channel_id=1, source_target_pairs={{0,6},{2,4},{4,2},{6,0},{8,14},{10,12},{12,10},{14,8},{16,22},{18,... | collective-permute-start | bytes 1769480 | tf_op jit(solution)/shard_map/ppermute | solution.py:852
  128.0 13.2 %collective-permute-start.7 = (bf16[192,1152]{1,0:T(8,128)(2,1)}, bf16[192,1152]{1,0:T(8,128)(2,1)S(1)}, u32[]{:S(2)}, u32[]{:S(2)}) collective-permute-start(bf16[192,1152]{1,0:T(8,128)(2,1)} %get-tuple-element.146), channel_id=1, source_target_pairs={{0,2},{2,0},{4,6},{6,4},{8,10},{10,8},{12,14},{14,12},{16,18},{18,... | collective-permute-start | bytes 1327112 | tf_op jit(solution)/shard_map/ppermute | solution.py:852
  130.0 21.8 %collective-permute-start.8 = (bf16[192,1152]{1,0:T(8,128)(2,1)}, bf16[192,1152]{1,0:T(8,128)(2,1)S(1)}, u32[]{:S(2)}, u32[]{:S(2)}) collective-permute-start(bf16[192,1152]{1,0:T(8,128)(2,1)} %get-tuple-element.147), channel_id=1, source_target_pairs={{0,4},{2,6},{4,0},{6,2},{8,12},{10,14},{12,8},{14,10},{16,20},{18,... | collective-permute-start | bytes 1327112 | tf_op jit(solution)/shard_map/ppermute | solution.py:852
  131.5 20.4 %collective-permute-start.9 = (bf16[192,1152]{1,0:T(8,128)(2,1)}, bf16[192,1152]{1,0:T(8,128)(2,1)S(1)}, u32[]{:S(2)}, u32[]{:S(2)}) collective-permute-start(bf16[192,1152]{1,0:T(8,128)(2,1)} %get-tuple-element.148), channel_id=1, source_target_pairs={{0,6},{2,4},{4,2},{6,0},{8,14},{10,12},{12,10},{14,8},{16,22},{18,... | collective-permute-start | bytes 1327112 | tf_op jit(solution)/shard_map/ppermute | solution.py:852
  132.0 19.9 %collective-permute-start.10 = (bf16[48,1536]{1,0:T(8,128)(2,1)S(1)}, bf16[48,1536]{1,0:T(8,128)(2,1)S(1)}, u32[]{:S(2)}, u32[]{:S(2)}) collective-permute-start(bf16[48,1536]{1,0:T(8,128)(2,1)S(1)} %get-tuple-element.236), channel_id=1, source_target_pairs={{0,8},{2,10},{4,12},{6,14},{8,0},{10,2},{12,4},{14,6},{16,24},{18,... | collective-permute-start | bytes 442376 | tf_op jit(solution)/shard_map/ppermute | solution.py:852
  134.0 17.9 %collective-permute-start.11 = (bf16[48,1536]{1,0:T(8,128)(2,1)S(1)}, bf16[48,1536]{1,0:T(8,128)(2,1)S(1)}, u32[]{:S(2)}, u32[]{:S(2)}) collective-permute-start(bf16[48,1536]{1,0:T(8,128)(2,1)S(1)} %get-tuple-element.235), channel_id=1, source_target_pairs={{0,16},{2,18},{4,20},{6,22},{8,24},{10,26},{12,28},{14,30},{16,0},... | collective-permute-start | bytes 442376 | tf_op jit(solution)/shard_map/ppermute | solution.py:852
  141.3 10.6 %collective-permute-start.12 = (bf16[48,1536]{1,0:T(8,128)(2,1)S(1)}, bf16[48,1536]{1,0:T(8,128)(2,1)S(1)}, u32[]{:S(2)}, u32[]{:S(2)}) collective-permute-start(bf16[48,1536]{1,0:T(8,128)(2,1)S(1)} %get-tuple-element.234), channel_id=1, source_target_pairs={{0,24},{2,26},{4,28},{6,30},{8,16},{10,18},{12,20},{14,22},{16,8},... | collective-permute-start | bytes 442376 | tf_op jit(solution)/shard_map/ppermute | solution.py:852
  152.0 7.0 %collective-permute-start.13 = (bf16[48,1536]{1,0:T(8,128)(2,1)S(1)}, bf16[48,1536]{1,0:T(8,128)(2,1)S(1)}, u32[]{:S(2)}, u32[]{:S(2)}) collective-permute-start(bf16[48,1536]{1,0:T(8,128)(2,1)S(1)} %add_convert_fusion), channel_id=1, source_target_pairs={{0,8},{2,10},{4,12},{6,14},{8,0},{10,2},{12,4},{14,6},{16,24},{18,... | collective-permute-start | bytes 442376 | tf_op jit(solution)/shard_map/ppermute | solution.py:852
  153.5 13.6 %collective-permute-start.14 = (bf16[48,1536]{1,0:T(8,128)(2,1)S(1)}, bf16[48,1536]{1,0:T(8,128)(2,1)S(1)}, u32[]{:S(2)}, u32[]{:S(2)}) collective-permute-start(bf16[48,1536]{1,0:T(8,128)(2,1)S(1)} %add_convert_fusion), channel_id=1, source_target_pairs={{0,16},{2,18},{4,20},{6,22},{8,24},{10,26},{12,28},{14,30},{16,0},... | collective-permute-start | bytes 442376 | tf_op jit(solution)/shard_map/ppermute | solution.py:852
  155.9 11.2 %collective-permute-start.15 = (bf16[48,1536]{1,0:T(8,128)(2,1)S(1)}, bf16[48,1536]{1,0:T(8,128)(2,1)S(1)}, u32[]{:S(2)}, u32[]{:S(2)}) collective-permute-start(bf16[48,1536]{1,0:T(8,128)(2,1)S(1)} %add_convert_fusion), channel_id=1, source_target_pairs={{0,24},{2,26},{4,28},{6,30},{8,16},{10,18},{12,20},{14,22},{16,8},... | collective-permute-start | bytes 442376 | tf_op jit(solution)/shard_map/ppermute | solution.py:852
  167.2 6.9 %collective-permute-start.16 = (bf16[48,1152]{1,0:T(8,128)(2,1)S(1)}, bf16[48,1152]{1,0:T(8,128)(2,1)S(1)}, u32[]{:S(2)}, u32[]{:S(2)}) collective-permute-start(bf16[48,1152]{1,0:T(8,128)(2,1)S(1)} %get-tuple-element.237), channel_id=1, source_target_pairs={{0,8},{2,10},{4,12},{6,14},{8,0},{10,2},{12,4},{14,6},{16,24},{18,... | collective-permute-start | bytes 331784 | tf_op jit(solution)/shard_map/ppermute | solution.py:852
  169.4 9.9 %collective-permute-start.17 = (bf16[48,1152]{1,0:T(8,128)(2,1)S(1)}, bf16[48,1152]{1,0:T(8,128)(2,1)S(1)}, u32[]{:S(2)}, u32[]{:S(2)}) collective-permute-start(bf16[48,1152]{1,0:T(8,128)(2,1)S(1)} %get-tuple-element.239), channel_id=1, source_target_pairs={{0,16},{2,18},{4,20},{6,22},{8,24},{10,26},{12,28},{14,30},{16,0},... | collective-permute-start | bytes 331784 | tf_op jit(solution)/shard_map/ppermute | solution.py:852
  170.3 8.9 %collective-permute-start.18 = (bf16[48,1152]{1,0:T(8,128)(2,1)S(1)}, bf16[48,1152]{1,0:T(8,128)(2,1)S(1)}, u32[]{:S(2)}, u32[]{:S(2)}) collective-permute-start(bf16[48,1152]{1,0:T(8,128)(2,1)S(1)} %get-tuple-element.238), channel_id=1, source_target_pairs={{0,24},{2,26},{4,28},{6,30},{8,16},{10,18},{12,20},{14,22},{16,8},... | collective-permute-start | bytes 331784 | tf_op jit(solution)/shard_map/ppermute | solution.py:852
  172.0 16.3 %collective-permute-start.20 = (bf16[192,1536]{1,0:T(8,128)(2,1)S(1)}, bf16[192,1536]{1,0:T(8,128)(2,1)S(1)}, u32[]{:S(2)}, u32[]{:S(2)}) collective-permute-start(bf16[192,1536]{1,0:T(8,128)(2,1)S(1)} %pad_maximum_fusion.refs_1_), channel_id=1, source_target_pairs={{0,2},{2,0},{4,6},{6,4},{8,10},{10,8},{12,14},{14,12},{16,18},{18,... | collective-permute-start | bytes 1769480 | tf_op jit(solution)/shard_map/ppermute | solution.py:852
  173.5 25.1 %collective-permute-start.21 = (bf16[192,1536]{1,0:T(8,128)(2,1)S(1)}, bf16[192,1536]{1,0:T(8,128)(2,1)}, u32[]{:S(2)}, u32[]{:S(2)}) collective-permute-start(bf16[192,1536]{1,0:T(8,128)(2,1)S(1)} %pad_maximum_fusion.refs_1_), channel_id=1, source_target_pairs={{0,4},{2,6},{4,0},{6,2},{8,12},{10,14},{12,8},{14,10},{16,20},{18,... | collective-permute-start | bytes 1769480 | tf_op jit(solution)/shard_map/ppermute | solution.py:852
  174.1 33.7 %collective-permute-start.22 = (bf16[192,1536]{1,0:T(8,128)(2,1)S(1)}, bf16[192,1536]{1,0:T(8,128)(2,1)}, u32[]{:S(2)}, u32[]{:S(2)}) collective-permute-start(bf16[192,1536]{1,0:T(8,128)(2,1)S(1)} %pad_maximum_fusion.refs_1_), channel_id=1, source_target_pairs={{0,6},{2,4},{4,2},{6,0},{8,14},{10,12},{12,10},{14,8},{16,22},{18,... | collective-permute-start | bytes 1769480 | tf_op jit(solution)/shard_map/ppermute | solution.py:852
  179.6 53.7 %all-to-all-start.2 = ((bf16[16,64,384]{2,1,0:T(8,128)(2,1)}), bf16[16,64,384]{2,1,0:T(8,128)(2,1)S(1)}, u32[]{:S(2)}, u32[]{:S(2)}) async-start(bf16[16,64,384]{2,1,0:T(8,128)(2,1)} %bitcast.10), calls=%async_computation.2 | async-start | bytes 1572864 | tf_op jit(solution)/shard_map/all_to_all | solution.py:1062
  217.3 10.5 %collective-permute-start.26 = (bf16[192,1152]{1,0:T(8,128)(2,1)S(1)}, bf16[192,1152]{1,0:T(8,128)(2,1)S(1)}, u32[]{:S(2)}, u32[]{:S(2)}) collective-permute-start(bf16[192,1152]{1,0:T(8,128)(2,1)S(1)} %pad_maximum_fusion.1.refs_1_), channel_id=1, source_target_pairs={{0,2},{2,0},{4,6},{6,4},{8,10},{10,8},{12,14},{14,12},{16,18},{18,... | collective-permute-start | bytes 1327112 | tf_op jit(solution)/shard_map/ppermute | solution.py:852
  218.5 14.8 %collective-permute-start.27 = (bf16[192,1152]{1,0:T(8,128)(2,1)S(1)}, bf16[192,1152]{1,0:T(8,128)(2,1)S(1)}, u32[]{:S(2)}, u32[]{:S(2)}) collective-permute-start(bf16[192,1152]{1,0:T(8,128)(2,1)S(1)} %pad_maximum_fusion.1.refs_1_), channel_id=1, source_target_pairs={{0,4},{2,6},{4,0},{6,2},{8,12},{10,14},{12,8},{14,10},{16,20},{18,... | collective-permute-start | bytes 1327112 | tf_op jit(solution)/shard_map/ppermute | solution.py:852
  219.2 14.1 %collective-permute-start.28 = (bf16[192,1152]{1,0:T(8,128)(2,1)S(1)}, bf16[192,1152]{1,0:T(8,128)(2,1)S(1)}, u32[]{:S(2)}, u32[]{:S(2)}) collective-permute-start(bf16[192,1152]{1,0:T(8,128)(2,1)S(1)} %pad_maximum_fusion.1.refs_1_), channel_id=1, source_target_pairs={{0,6},{2,4},{4,2},{6,0},{8,14},{10,12},{12,10},{14,8},{16,22},{18,... | collective-permute-start | bytes 1327112 | tf_op jit(solution)/shard_map/ppermute | solution.py:852
  (36 other events, 343.0 us)

commit v3 on v2

--- a/solution.py
+++ b/solution.py
@@ -696,7 +696,7 @@
         out[l, :] = dx.astype(BF).T
 
 
-def finish_first_kernel(io, own, h0, h1, h2, h3, wo, wg, *, full_len):
+def finish_first_kernel(io, dealing, own, h0, h1, h2, h3, back, wo, wg, grad_in, *, full_len):
     share = h0.shape[0]
     C = wg.shape[1]
     place = lax.axis_index("dp") % 4
@@ -709,11 +709,18 @@
         wg[r, :] = ref[:, D : D + C].astype(F32) * scale
     io.put("wo")
     io.put("wg")
+    io.need("back")
+
+    @pl.loop(0, grad_in.shape[0])
+    def _(k):
+        grad_in[dealing[k]] = (back[k].astype(F32) * scale).astype(BF)
+
+    io.put("grad_in")
 
 
 def finish_kernel(
-    io, dealing, g0, g1, g2, g3, back,
-    gv, gt, gs, ng, cv, vb, cst, sb, dl, sk, og, bias, grad_in,
+    io, g0, g1, g2, g3,
+    gv, gt, gs, ng, cv, vb, cst, sb, dl, sk, og, bias,
     sm, *, full_len
 ):
     share = g0.shape[0]
@@ -732,13 +739,6 @@
         gs[r, :] = ref[:, C + Q : C + Q + 256].astype(F32) * scale
     io.put("gv")
     io.put("gs")
-    io.need("back")
-
-    @pl.loop(0, grad_in.shape[0])
-    def _(k):
-        grad_in[dealing[k]] = (back[k].astype(F32) * scale).astype(BF)
-
-    io.put("grad_in")
     scaled = sm[...]
     gt[...] = scaled[:, 0 : 2 * HH]
     turned = scaled.T
@@ -1058,34 +1058,34 @@
     now, held = lax.optimization_barrier((now, held))
     for weight, members in reversed(phases[1:]):
         now = assemble(send_round([now] * members, groups, weight), rank, weight)
+    back = lax.all_to_all(dx.reshape(seqs, local, half), "dp", split_axis=0, concat_axis=0, tiled=True)
+    now, back = lax.optimization_barrier((now, back))
     got = send_round([now] * 4, groups, 1)
-    back = lax.all_to_all(dx.reshape(seqs, local, half), "dp", split_axis=0, concat_axis=0, tiled=True)
-    wo, wg = call(
+    wo, wg, grad_in = call(
         finish_first_kernel,
-        [((C, D), F32), ((D, C), F32)],
+        [((C, D), F32), ((D, C), F32), ((seqs, local, half), BF)],
         [],
-        (now[0:8, C : C + Q], *held),
-        0,
+        (dealing, now[0:8, C : C + Q], *held, back),
+        1,
         "finish_first",
         5.0,
-        late={n: (0, 1) for n in ("h0", "h1", "h2", "h3")},
-        early={n: (0, 1) for n in ("wo", "wg")},
+        late={n: (0, 1) for n in ("h0", "h1", "h2", "h3", "back")},
+        early={n: (0, 1) for n in ("wo", "wg", "grad_in")},
         static={"full_len": T},
     )
-    gv, gt, gs, ng, cv, vb, cst, sb, dl, sk, og, bias, grad_in = call(
+    gv, gt, gs, ng, cv, vb, cst, sb, dl, sk, og, bias = call(
         finish_kernel,
         [
             ((D, C), F32), ((D, 2 * HH), F32), ((D, 256), F32), ((D,), F32), ((4, C), F32), ((C,), F32),
             ((4, 256), F32), ((256,), F32), ((HH,), F32), ((HH,), F32), ((C,), F32), ((2, HH), F32),
-            ((seqs, local, half), BF),
         ],
         [((D, Q), F32)],
-        (dealing, *got, back),
-        1,
+        tuple(got),
+        0,
         "finish",
         4.0,
-        late={n: (0, 1) for n in ("g0", "g1", "g2", "g3", "back")},
-        early={n: (0, 1) for n in ("gv", "gs", "grad_in")},
+        late={n: (0, 1) for n in ("g0", "g1", "g2", "g3")},
+        early={n: (0, 1) for n in ("gv", "gs")},
         static={"full_len": T},
     )
     return (

time: 243 us -> 239 us (0.984)
  waiting for transfers between devices: 63.4 us -> 53.9 us
  starting transfers between devices: 55 us -> 61.1 us
    ppermute x24, waiting for transfers between devices: 56.6 us -> 46.2 us  [across(): return lax.ppermute(x, 'dp', [(i, i ^ bit) for i in range(groups)])]
    ppermute x24, starting transfers between devices: 35.8 us -> 41.5 us  [across(): return lax.ppermute(x, 'dp', [(i, i ^ bit) for i in range(groups)])]
  transfers between devices with their start and end apart: 32 -> 32, of which waited for: 15 -> 12; matrix products, arithmetic and copies ran while one was open for 4% -> 4% of each run, Pallas kernels for 34% -> 34%
where the time goes in v3:
time: 239 us; the launch traced here: 238 us
  Pallas kernels  105 us (44%)
  starting transfers between devices  61.1 us (26%)
  waiting for transfers between devices  53.9 us (23%)
  local copies, waits for them, and re-layouts  11.5 us (5%)
  between operations  3.25 us (1%)
  other arithmetic  3.12 us (1%)
    pallas_call x9, Pallas kernels, call(): pl.pallas_call(wrapped, out_shape=[jax.ShapeDtypeStruct(s, d) for s, d in...  105 us
    ppermute x24, waiting for transfers between devices, across(): return lax.ppermute(x, 'dp', [(i, i ^ bit) for i in range(groups)])  46.2 us
    ppermute x24, starting transfers between devices, across(): return lax.ppermute(x, 'dp', [(i, i ^ bit) for i in range(groups)])  41.5 us
    all_to_all x1, starting transfers between devices, on_device(): lax.all_to_all(dealt, 'dp', split_axis=0, concat_axis=0, tiled=True)  8.46 us
    all_to_all x1, starting transfers between devices, on_device(): lax.all_to_all(dx.reshape(seqs, local, half), 'dp', split_axis=0, concat_...  5.56 us
    ppermute x5, waiting for transfers between devices, swap(): return lax.ppermute(x, 'tensor', [(0, 1), (1, 0)])  5.24 us
    all_to_all x1, starting transfers between devices, on_device(): lax.all_to_all(goal, 'dp', split_axis=0, concat_axis=0, tiled=True)  4.9 us
  transfers between devices with their start and end apart: 32, of which 12 were waited for; matrix products, arithmetic and copies ran while one was open for 4% of the time, Pallas kernels for 34%

profile of v3, /device:TPU:0, one launch (start us, length us, event | category | flops | bytes accessed | tf_op | source)
XLA Modules:
  0.0 238.3 jit_solution(9178784474564420656)
XLA Ops:
  0.6 2.5 %deal.1 = bf16[16,64,384]{2,1,0:T(8,128)(2,1)} custom-call(s32[16]{0:T(128)} %refs_0_.6, bf16[16,64,768]{2,1,0:T(8,128)(2,1)} %refs_1_.2), custom_call_target="tpu_custom_call" | custom-call | flops 2700000000 | bytes 9000000 | tf_op jit(solution)/shard_map/deal/pallas_call | solution.py:831
  3.3 8.5 %all-to-all-start = ((bf16[16,64,384]{2,1,0:T(8,128)(2,1)}), bf16[16,64,384]{2,1,0:T(8,128)(2,1)S(1)}, u32[]{:S(2)}, u32[]{:S(2)}) async-start(bf16[16,64,384]{2,1,0:T(8,128)(2,1)} %deal.1), calls=%async_computation | async-start | bytes 1572864 | tf_op jit(solution)/shard_map/all_to_all | solution.py:908
  21.8 7.2 %prepare.1 = (bf16[768,1920]{1,0:T(8,128)(2,1)}, bf16[1920,768]{1,0:T(8,128)(2,1)}, bf16[768,768]{1,0:T(8,128)(2,1)}, f32[768,8]{1,0:T(8,128)}) custom-call(bf16[768,768]{1,0:T(8,128)(2,1)} %refs_0_.5, bf16[768,768]{1,0:T(8,128)(2,1)} %refs_1_.3, bf16[768,256]{1,0:T(8,128)(2,1)} %refs_2_.1, bf16[768,24]{1,0:T(8,128)(2,1)} %copy.53.refs_3_, ...), custom_call_target="tpu_custom_call" | custom-call | flops 5400000000 | bytes 18000000 | tf_op jit(solution)/shard_map/prepare/pallas_call | solution.py:831
  29.0 2.5 %all-to-all-done = bf16[16,64,384]{2,1,0:T(8,128)(2,1)S(1)} async-done(((bf16[16,64,384]{2,1,0:T(8,128)(2,1)}), bf16[16,64,384]{2,1,0:T(8,128)(2,1)S(1)}, u32[]{:S(2)}, u32[]{:S(2)}) %all-to-all-start) | async-done | bytes 786464 | tf_op jit(solution)/shard_map/all_to_all | solution.py:908
  32.3 4.9 %all-to-all-start.1 = ((bf16[16,64,384]{2,1,0:T(8,128)(2,1)}), bf16[16,64,384]{2,1,0:T(8,128)(2,1)S(1)}, u32[]{:S(2)}, u32[]{:S(2)}) async-start(bf16[16,64,384]{2,1,0:T(8,128)(2,1)} %deal_goal.1), calls=%async_computation.1 | async-start | bytes 1572864 | tf_op jit(solution)/shard_map/all_to_all | solution.py:945
  38.1 28.1 %forward.1 = (bf16[768,1024]{1,0:T(8,128)(2,1)}, bf16[768,1024]{1,0:T(8,128)(2,1)}, f32[120,1024]{1,0:T(8,128)}, f32[8,24,128]{2,1,0:T(8,128)}, f32[768,1024]{1,...) custom-call(s32[1]{0:T(128)} %dynamic_slice.31.refs_0_, ...), custom_call_target="tpu_custom_call" | custom-call | flops 23399999488 | bytes 78000000 | tf_op jit(solution)/shard_map/forward/pallas_call | solution.py:831
  66.8 4.1 %collective-permute-done.2.refs_4_ = bf16[1024,384]{1,0:T(8,128)(2,1)S(1)} collective-permute-done((bf16[1024,384]{1,0:T(8,128)(2,1)S(1)}, bf16[1024,384]{1,0:T(8,128)(2,1)S(1)}, u32[]{:S(2)}, u32[]{:S(2)}) %collective-permute-start.2) | collective-permute-done | bytes 786464 | tf_op jit(solution)/shard_map/ppermute | solution.py:848
  72.3 16.2 %middle.1 = (bf16[1024,384]{1,0:T(8,128)(2,1)}, bf16[384,1024]{1,0:T(8,128)(2,1)}, bf16[768,1024]{1,0:T(8,128)(2,1)}, bf16[768,1024]{1,0:T(8,128)(2,1)}, f32[768...) custom-call(bf16[784,1024]{1,0:T(8,128)(2,1)} %get-tuple-element.117, ...), custom_call_target="tpu_custom_call" | custom-call | flops 12600000512 | bytes 42000000 | tf_op jit(solution)/shard_map/middle/pallas_call | solution.py:831
  92.1 35.8 %backward.1 = (bf16[192,1152]{1,0:T(8,128)(2,1)}, bf16[192,1152]{1,0:T(8,128)(2,1)}, bf16[192,1152]{1,0:T(8,128)(2,1)}, bf16[192,1152]{1,0:T(8,128)(2,1)}, bf16[...) custom-call(s32[1]{0:T(128)} %dynamic_slice.31.refs_0_, f32[1]{0:T(128)} %bitcast.6.refs_1_, ...), custom_call_target="tpu_custom_call" | custom-call | flops 27000000512 | bytes 90000000 | tf_op jit(solution)/shard_map/backward/pallas_call | solution.py:831
  134.0 2.4 collective-permute-start.11
  136.3 4.0 %last.1 = bf16[1024,384]{1,0:T(8,128)(2,1)} custom-call(bf16[384,1024]{1,0:T(8,128)(2,1)} %get-tuple-element.137.refs_0_, bf16[400,1024]{1,0:T(8,128)(2,1)} %copy-done.19, bf16[384,1024]{1,0:T(8,128)(2,1)} %get-tuple-element.144.refs_2_, f32[8,1024]{1,0:T(8,128)} %get-tuple-element.145.refs_3_, f32[8,1024]{1,0:T(8,128)} %get-tuple-element.146.refs_4_, ...), custom_call_target="tpu_custom_call" | custom-call | flops 2700000000 | bytes 9000000 | tf_op jit(solution)/shard_map/last/pallas_call | solution.py:831
  141.3 3.7 %collective-permute-start.12 = (bf16[48,1536]{1,0:T(8,128)(2,1)S(1)}, bf16[48,1536]{1,0:T(8,128)(2,1)S(1)}, u32[]{:S(2)}, u32[]{:S(2)}) collective-permute-start(bf16[48,1536]{1,0:T(8,128)(2,1)S(1)} %get-tuple-element.238), channel_id=1, source_target_pairs={{0,24},{2,26},{4,28},{6,30},{8,16},{10,18},{12,20},{14,22},{16,8},... | collective-permute-start | bytes 442376 | tf_op jit(solution)/shard_map/ppermute | solution.py:852
  145.0 6.8 %collective-permute-done.8 = bf16[192,1152]{1,0:T(8,128)(2,1)S(1)} collective-permute-done((bf16[192,1152]{1,0:T(8,128)(2,1)}, bf16[192,1152]{1,0:T(8,128)(2,1)S(1)}, u32[]{:S(2)}, u32[]{:S(2)}) %collective-permute-start.8) | collective-permute-done | bytes 442400 | tf_op jit(solution)/shard_map/ppermute | solution.py:852
  153.5 2.4 collective-permute-start.14
  156.7 5.6 %all-to-all-start.2 = ((bf16[16,64,384]{2,1,0:T(8,128)(2,1)}), bf16[16,64,384]{2,1,0:T(8,128)(2,1)S(1)}, u32[]{:S(2)}, u32[]{:S(2)}) async-start(bf16[16,64,384]{2,1,0:T(8,128)(2,1)} %bitcast.10), calls=%async_computation.2 | async-start | bytes 1572864 | tf_op jit(solution)/shard_map/all_to_all | solution.py:1061
  162.5 10.9 %collective-permute-done.14 = bf16[48,1536]{1,0:T(8,128)(2,1)S(1)} collective-permute-done((bf16[48,1536]{1,0:T(8,128)(2,1)S(1)}, bf16[48,1536]{1,0:T(8,128)(2,1)S(1)}, u32[]{:S(2)}, u32[]{:S(2)}) %collective-permute-start.14) | collective-permute-done | bytes 147488 | tf_op jit(solution)/shard_map/ppermute | solution.py:852
  173.5 6.9 %collective-permute-start.16 = (bf16[48,1152]{1,0:T(8,128)(2,1)S(1)}, bf16[48,1152]{1,0:T(8,128)(2,1)S(1)}, u32[]{:S(2)}, u32[]{:S(2)}) collective-permute-start(bf16[48,1152]{1,0:T(8,128)(2,1)S(1)} %get-tuple-element.241), channel_id=1, source_target_pairs={{0,8},{2,10},{4,12},{6,14},{8,0},{10,2},{12,4},{14,6},{16,24},{18,... | collective-permute-start | bytes 331784 | tf_op jit(solution)/shard_map/ppermute | solution.py:852
  187.6 6.3 %collective-permute-done.17 = bf16[48,1152]{1,0:T(8,128)(2,1)S(1)} collective-permute-done((bf16[48,1152]{1,0:T(8,128)(2,1)S(1)}, bf16[48,1152]{1,0:T(8,128)(2,1)S(1)}, u32[]{:S(2)}, u32[]{:S(2)}) %collective-permute-start.17) | collective-permute-done | bytes 110624 | tf_op jit(solution)/shard_map/ppermute | solution.py:852
  195.7 4.3 %collective-permute-done.20.refs_3_ = bf16[192,1536]{1,0:T(8,128)(2,1)S(1)} collective-permute-done((bf16[192,1536]{1,0:T(8,128)(2,1)S(1)}, bf16[192,1536]{1,0:T(8,128)(2,1)S(1)}, u32[]{:S(2)}, u32[]{:S(2)}) %collective-permute-start.20) | collective-permute-done | bytes 589856 | tf_op jit(solution)/shard_map/ppermute | solution.py:852
  200.0 7.0 %collective-permute-done.21.refs_4_ = bf16[192,1536]{1,0:T(8,128)(2,1)} collective-permute-done((bf16[192,1536]{1,0:T(8,128)(2,1)S(1)}, bf16[192,1536]{1,0:T(8,128)(2,1)}, u32[]{:S(2)}, u32[]{:S(2)}) %collective-permute-start.21) | collective-permute-done | bytes 589856 | tf_op jit(solution)/shard_map/ppermute | solution.py:852
  213.6 2.3 collective-permute-done.24
  220.2 4.8 %finish_first.1 = (f32[768,768]{1,0:T(8,128)}, f32[768,768]{1,0:T(8,128)}, bf16[16,64,384]{2,1,0:T(8,128)(2,1)}) custom-call(s32[16]{0:T(128)} %refs_0_.6, bf16[8,128]{1,0:T(8,128)(2,1)} %slice.49.refs_1_, bf16[192,1536]{1,0:T(8,128)(2,1)} %copy-done.5, bf16[192,1536]{1,0:T(8,128)(2,1)} %copy-done.22, bf16[192,1536]{1,0:T(8,128)(2,1)} %collective-permute-done.21.refs_4_, ...), custom_call_target="tpu_custom_call" | custom-call | flops 4499999744 | bytes 15000000 | tf_op jit(solution)/shard_map/finish_first/pallas_call | solution.py:831
  225.1 5.3 %collective-permute-done.27.refs_2_ = bf16[192,1152]{1,0:T(8,128)(2,1)S(1)} collective-permute-done((bf16[192,1152]{1,0:T(8,128)(2,1)S(1)}, bf16[192,1152]{1,0:T(8,128)(2,1)S(1)}, u32[]{:S(2)}, u32[]{:S(2)}) %collective-permute-start.27) | collective-permute-done | bytes 442400 | tf_op jit(solution)/shard_map/ppermute | solution.py:852
  231.9 4.5 %finish.1 = (f32[768,768]{1,0:T(8,128)}, f32[768,24]{1,0:T(8,128)}, f32[768,256]{1,0:T(8,128)}, f32[768]{0:T(1024)}, f32[4,768]{1,0:T(4,128)}, /*index=5*/f32[76...) custom-call(bf16[192,1152]{1,0:T(8,128)(2,1)} %copy-done.6, ...), custom_call_target="tpu_custom_call" | custom-call | flops 3600000000 | bytes 12000000 | tf_op jit(solution)/shard_map/finish/pallas_call | solution.py:831
  (158 shorter events, 48.1 us)
Async XLA Ops:
  3.3 28.2 %all-to-all-start = ((bf16[16,64,384]{2,1,0:T(8,128)(2,1)}), bf16[16,64,384]{2,1,0:T(8,128)(2,1)S(1)}, u32[]{:S(2)}, u32[]{:S(2)}) async-start(bf16[16,64,384]{2,1,0:T(8,128)(2,1)} %deal.1), calls=%async_computation | async-start | bytes 1572864 | tf_op jit(solution)/shard_map/all_to_all | solution.py:908
  32.3 34.1 %all-to-all-start.1 = ((bf16[16,64,384]{2,1,0:T(8,128)(2,1)}), bf16[16,64,384]{2,1,0:T(8,128)(2,1)S(1)}, u32[]{:S(2)}, u32[]{:S(2)}) async-start(bf16[16,64,384]{2,1,0:T(8,128)(2,1)} %deal_goal.1), calls=%async_computation.1 | async-start | bytes 1572864 | tf_op jit(solution)/shard_map/all_to_all | solution.py:945
  88.5 41.5 %collective-permute-start.3 = (bf16[192,1536]{1,0:T(8,128)(2,1)}, bf16[192,1536]{1,0:T(8,128)(2,1)S(1)}, u32[]{:S(2)}, u32[]{:S(2)}) collective-permute-start(bf16[192,1536]{1,0:T(8,128)(2,1)} %get-tuple-element.139), channel_id=1, source_target_pairs={{0,2},{2,0},{4,6},{6,4},{8,10},{10,8},{12,14},{14,12},{16,18},{18,... | collective-permute-start | bytes 1769480 | tf_op jit(solution)/shard_map/ppermute | solution.py:852
  90.5 41.0 %collective-permute-start.4 = (bf16[192,1536]{1,0:T(8,128)(2,1)}, bf16[192,1536]{1,0:T(8,128)(2,1)S(1)}, u32[]{:S(2)}, u32[]{:S(2)}) collective-permute-start(bf16[192,1536]{1,0:T(8,128)(2,1)} %get-tuple-element.140), channel_id=1, source_target_pairs={{0,4},{2,6},{4,0},{6,2},{8,12},{10,14},{12,8},{14,10},{16,20},{18,... | collective-permute-start | bytes 1769480 | tf_op jit(solution)/shard_map/ppermute | solution.py:852
  91.9 39.7 %collective-permute-start.5 = (bf16[192,1536]{1,0:T(8,128)(2,1)}, bf16[192,1536]{1,0:T(8,128)(2,1)S(1)}, u32[]{:S(2)}, u32[]{:S(2)}) collective-permute-start(bf16[192,1536]{1,0:T(8,128)(2,1)} %get-tuple-element.141), channel_id=1, source_target_pairs={{0,6},{2,4},{4,2},{6,0},{8,14},{10,12},{12,10},{14,8},{16,22},{18,... | collective-permute-start | bytes 1769480 | tf_op jit(solution)/shard_map/ppermute | solution.py:852
  128.1 13.3 %collective-permute-start.7 = (bf16[192,1152]{1,0:T(8,128)(2,1)}, bf16[192,1152]{1,0:T(8,128)(2,1)S(1)}, u32[]{:S(2)}, u32[]{:S(2)}) collective-permute-start(bf16[192,1152]{1,0:T(8,128)(2,1)} %get-tuple-element.148), channel_id=1, source_target_pairs={{0,2},{2,0},{4,6},{6,4},{8,10},{10,8},{12,14},{14,12},{16,18},{18,... | collective-permute-start | bytes 1327112 | tf_op jit(solution)/shard_map/ppermute | solution.py:852
  130.0 21.8 %collective-permute-start.8 = (bf16[192,1152]{1,0:T(8,128)(2,1)}, bf16[192,1152]{1,0:T(8,128)(2,1)S(1)}, u32[]{:S(2)}, u32[]{:S(2)}) collective-permute-start(bf16[192,1152]{1,0:T(8,128)(2,1)} %get-tuple-element.149), channel_id=1, source_target_pairs={{0,4},{2,6},{4,0},{6,2},{8,12},{10,14},{12,8},{14,10},{16,20},{18,... | collective-permute-start | bytes 1327112 | tf_op jit(solution)/shard_map/ppermute | solution.py:852
  131.5 20.4 %collective-permute-start.9 = (bf16[192,1152]{1,0:T(8,128)(2,1)}, bf16[192,1152]{1,0:T(8,128)(2,1)S(1)}, u32[]{:S(2)}, u32[]{:S(2)}) collective-permute-start(bf16[192,1152]{1,0:T(8,128)(2,1)} %get-tuple-element.150), channel_id=1, source_target_pairs={{0,6},{2,4},{4,2},{6,0},{8,14},{10,12},{12,10},{14,8},{16,22},{18,... | collective-permute-start | bytes 1327112 | tf_op jit(solution)/shard_map/ppermute | solution.py:852
  132.0 19.8 %collective-permute-start.10 = (bf16[48,1536]{1,0:T(8,128)(2,1)S(1)}, bf16[48,1536]{1,0:T(8,128)(2,1)S(1)}, u32[]{:S(2)}, u32[]{:S(2)}) collective-permute-start(bf16[48,1536]{1,0:T(8,128)(2,1)S(1)} %get-tuple-element.240), channel_id=1, source_target_pairs={{0,8},{2,10},{4,12},{6,14},{8,0},{10,2},{12,4},{14,6},{16,24},{18,... | collective-permute-start | bytes 442376 | tf_op jit(solution)/shard_map/ppermute | solution.py:852
  134.0 17.9 %collective-permute-start.11 = (bf16[48,1536]{1,0:T(8,128)(2,1)S(1)}, bf16[48,1536]{1,0:T(8,128)(2,1)S(1)}, u32[]{:S(2)}, u32[]{:S(2)}) collective-permute-start(bf16[48,1536]{1,0:T(8,128)(2,1)S(1)} %get-tuple-element.239), channel_id=1, source_target_pairs={{0,16},{2,18},{4,20},{6,22},{8,24},{10,26},{12,28},{14,30},{16,0},... | collective-permute-start | bytes 442376 | tf_op jit(solution)/shard_map/ppermute | solution.py:852
  141.3 10.6 %collective-permute-start.12 = (bf16[48,1536]{1,0:T(8,128)(2,1)S(1)}, bf16[48,1536]{1,0:T(8,128)(2,1)S(1)}, u32[]{:S(2)}, u32[]{:S(2)}) collective-permute-start(bf16[48,1536]{1,0:T(8,128)(2,1)S(1)} %get-tuple-element.238), channel_id=1, source_target_pairs={{0,24},{2,26},{4,28},{6,30},{8,16},{10,18},{12,20},{14,22},{16,8},... | collective-permute-start | bytes 442376 | tf_op jit(solution)/shard_map/ppermute | solution.py:852
  152.0 10.5 %collective-permute-start.13 = (bf16[48,1536]{1,0:T(8,128)(2,1)S(1)}, bf16[48,1536]{1,0:T(8,128)(2,1)S(1)}, u32[]{:S(2)}, u32[]{:S(2)}) collective-permute-start(bf16[48,1536]{1,0:T(8,128)(2,1)S(1)} %add_convert_fusion), channel_id=1, source_target_pairs={{0,8},{2,10},{4,12},{6,14},{8,0},{10,2},{12,4},{14,6},{16,24},{18,... | collective-permute-start | bytes 442376 | tf_op jit(solution)/shard_map/ppermute | solution.py:852
  153.5 19.9 %collective-permute-start.14 = (bf16[48,1536]{1,0:T(8,128)(2,1)S(1)}, bf16[48,1536]{1,0:T(8,128)(2,1)S(1)}, u32[]{:S(2)}, u32[]{:S(2)}) collective-permute-start(bf16[48,1536]{1,0:T(8,128)(2,1)S(1)} %add_convert_fusion), channel_id=1, source_target_pairs={{0,16},{2,18},{4,20},{6,22},{8,24},{10,26},{12,28},{14,30},{16,0},... | collective-permute-start | bytes 442376 | tf_op jit(solution)/shard_map/ppermute | solution.py:852
  155.9 17.6 %collective-permute-start.15 = (bf16[48,1536]{1,0:T(8,128)(2,1)S(1)}, bf16[48,1536]{1,0:T(8,128)(2,1)S(1)}, u32[]{:S(2)}, u32[]{:S(2)}) collective-permute-start(bf16[48,1536]{1,0:T(8,128)(2,1)S(1)} %add_convert_fusion), channel_id=1, source_target_pairs={{0,24},{2,26},{4,28},{6,30},{8,16},{10,18},{12,20},{14,22},{16,8},... | collective-permute-start | bytes 442376 | tf_op jit(solution)/shard_map/ppermute | solution.py:852
  156.7 59.3 %all-to-all-start.2 = ((bf16[16,64,384]{2,1,0:T(8,128)(2,1)}), bf16[16,64,384]{2,1,0:T(8,128)(2,1)S(1)}, u32[]{:S(2)}, u32[]{:S(2)}) async-start(bf16[16,64,384]{2,1,0:T(8,128)(2,1)} %bitcast.10), calls=%async_computation.2 | async-start | bytes 1572864 | tf_op jit(solution)/shard_map/all_to_all | solution.py:1061
  173.5 12.7 %collective-permute-start.16 = (bf16[48,1152]{1,0:T(8,128)(2,1)S(1)}, bf16[48,1152]{1,0:T(8,128)(2,1)S(1)}, u32[]{:S(2)}, u32[]{:S(2)}) collective-permute-start(bf16[48,1152]{1,0:T(8,128)(2,1)S(1)} %get-tuple-element.241), channel_id=1, source_target_pairs={{0,8},{2,10},{4,12},{6,14},{8,0},{10,2},{12,4},{14,6},{16,24},{18,... | collective-permute-start | bytes 331784 | tf_op jit(solution)/shard_map/ppermute | solution.py:852
  180.4 13.5 %collective-permute-start.17 = (bf16[48,1152]{1,0:T(8,128)(2,1)S(1)}, bf16[48,1152]{1,0:T(8,128)(2,1)S(1)}, u32[]{:S(2)}, u32[]{:S(2)}) collective-permute-start(bf16[48,1152]{1,0:T(8,128)(2,1)S(1)} %get-tuple-element.243), channel_id=1, source_target_pairs={{0,16},{2,18},{4,20},{6,22},{8,24},{10,26},{12,28},{14,30},{16,0},... | collective-permute-start | bytes 331784 | tf_op jit(solution)/shard_map/ppermute | solution.py:852
  182.5 11.3 %collective-permute-start.18 = (bf16[48,1152]{1,0:T(8,128)(2,1)S(1)}, bf16[48,1152]{1,0:T(8,128)(2,1)S(1)}, u32[]{:S(2)}, u32[]{:S(2)}) collective-permute-start(bf16[48,1152]{1,0:T(8,128)(2,1)S(1)} %get-tuple-element.242), channel_id=1, source_target_pairs={{0,24},{2,26},{4,28},{6,30},{8,16},{10,18},{12,20},{14,22},{16,8},... | collective-permute-start | bytes 331784 | tf_op jit(solution)/shard_map/ppermute | solution.py:852
  184.1 15.9 %collective-permute-start.20 = (bf16[192,1536]{1,0:T(8,128)(2,1)S(1)}, bf16[192,1536]{1,0:T(8,128)(2,1)S(1)}, u32[]{:S(2)}, u32[]{:S(2)}) collective-permute-start(bf16[192,1536]{1,0:T(8,128)(2,1)S(1)} %pad_maximum_fusion.refs_2_), channel_id=1, source_target_pairs={{0,2},{2,0},{4,6},{6,4},{8,10},{10,8},{12,14},{14,12},{16,18},{18,... | collective-permute-start | bytes 1769480 | tf_op jit(solution)/shard_map/ppermute | solution.py:852
  185.4 21.5 %collective-permute-start.21 = (bf16[192,1536]{1,0:T(8,128)(2,1)S(1)}, bf16[192,1536]{1,0:T(8,128)(2,1)}, u32[]{:S(2)}, u32[]{:S(2)}) collective-permute-start(bf16[192,1536]{1,0:T(8,128)(2,1)S(1)} %pad_maximum_fusion.refs_2_), channel_id=1, source_target_pairs={{0,4},{2,6},{4,0},{6,2},{8,12},{10,14},{12,8},{14,10},{16,20},{18,... | collective-permute-start | bytes 1769480 | tf_op jit(solution)/shard_map/ppermute | solution.py:852
  186.2 20.8 %collective-permute-start.22 = (bf16[192,1536]{1,0:T(8,128)(2,1)S(1)}, bf16[192,1536]{1,0:T(8,128)(2,1)}, u32[]{:S(2)}, u32[]{:S(2)}) collective-permute-start(bf16[192,1536]{1,0:T(8,128)(2,1)S(1)} %pad_maximum_fusion.refs_2_), channel_id=1, source_target_pairs={{0,6},{2,4},{4,2},{6,0},{8,14},{10,12},{12,10},{14,8},{16,22},{18,... | collective-permute-start | bytes 1769480 | tf_op jit(solution)/shard_map/ppermute | solution.py:852
  216.0 9.0 %collective-permute-start.26 = (bf16[192,1152]{1,0:T(8,128)(2,1)S(1)}, bf16[192,1152]{1,0:T(8,128)(2,1)S(1)}, u32[]{:S(2)}, u32[]{:S(2)}) collective-permute-start(bf16[192,1152]{1,0:T(8,128)(2,1)S(1)} %pad_maximum_fusion.1.refs_0_), channel_id=1, source_target_pairs={{0,2},{2,0},{4,6},{6,4},{8,10},{10,8},{12,14},{14,12},{16,18},{18,... | collective-permute-start | bytes 1327112 | tf_op jit(solution)/shard_map/ppermute | solution.py:852
  217.3 13.0 %collective-permute-start.27 = (bf16[192,1152]{1,0:T(8,128)(2,1)S(1)}, bf16[192,1152]{1,0:T(8,128)(2,1)S(1)}, u32[]{:S(2)}, u32[]{:S(2)}) collective-permute-start(bf16[192,1152]{1,0:T(8,128)(2,1)S(1)} %pad_maximum_fusion.1.refs_0_), channel_id=1, source_target_pairs={{0,4},{2,6},{4,0},{6,2},{8,12},{10,14},{12,8},{14,10},{16,20},{18,... | collective-permute-start | bytes 1327112 | tf_op jit(solution)/shard_map/ppermute | solution.py:852
  218.7 11.6 %collective-permute-start.28 = (bf16[192,1152]{1,0:T(8,128)(2,1)S(1)}, bf16[192,1152]{1,0:T(8,128)(2,1)S(1)}, u32[]{:S(2)}, u32[]{:S(2)}) collective-permute-start(bf16[192,1152]{1,0:T(8,128)(2,1)S(1)} %pad_maximum_fusion.1.refs_0_), channel_id=1, source_target_pairs={{0,6},{2,4},{4,2},{6,0},{8,14},{10,12},{12,10},{14,8},{16,22},{18,... | collective-permute-start | bytes 1327112 | tf_op jit(solution)/shard_map/ppermute | solution.py:852
  (37 other events, 358.8 us)

commit v4 on v3

--- a/solution.py
+++ b/solution.py
@@ -34,7 +34,7 @@
     return run
 
 
-ROWS = 32
+ROWS = 64
 
 NN = (((1,), (0,)), ((), ()))
 NT = (((1,), (1,)), ((), ()))

time: 239 us -> 238 us (level)
  no operation moved by 1% of the time
where the time goes in v4:
time: 238 us
  Pallas kernels  105 us (44%)
  starting transfers between devices  61.1 us (26%)
  waiting for transfers between devices  53.9 us (23%)
  local copies, waits for them, and re-layouts  11.5 us (5%)
  between operations  3.25 us (1%)
  other arithmetic  3.12 us (1%)
    pallas_call x9, Pallas kernels, call(): pl.pallas_call(wrapped, out_shape=[jax.ShapeDtypeStruct(s, d) for s, d in...  105 us
    ppermute x24, waiting for transfers between devices, across(): return lax.ppermute(x, 'dp', [(i, i ^ bit) for i in range(groups)])  46.2 us
    ppermute x24, starting transfers between devices, across(): return lax.ppermute(x, 'dp', [(i, i ^ bit) for i in range(groups)])  41.5 us
    all_to_all x1, starting transfers between devices, on_device(): lax.all_to_all(dealt, 'dp', split_axis=0, concat_axis=0, tiled=True)  8.46 us
    all_to_all x1, starting transfers between devices, on_device(): lax.all_to_all(dx.reshape(seqs, local, half), 'dp', split_axis=0, concat_...  5.56 us
    ppermute x5, waiting for transfers between devices, swap(): return lax.ppermute(x, 'tensor', [(0, 1), (1, 0)])  5.24 us
    all_to_all x1, starting transfers between devices, on_device(): lax.all_to_all(goal, 'dp', split_axis=0, concat_axis=0, tiled=True)  4.9 us
  transfers between devices with their start and end apart: 32, of which 12 were waited for; matrix products, arithmetic and copies ran while one was open for 4% of the time, Pallas kernels for 34%

profile of v4, /device:TPU:0, one launch (start us, length us, event | category | flops | bytes accessed | tf_op | source)
XLA Modules:
  0.0 237.6 jit_solution(4753959580001539445)
XLA Ops:
  0.6 2.5 %deal.1 = bf16[16,64,384]{2,1,0:T(8,128)(2,1)} custom-call(s32[16]{0:T(128)} %refs_0_.6, bf16[16,64,768]{2,1,0:T(8,128)(2,1)} %refs_1_.2), custom_call_target="tpu_custom_call" | custom-call | flops 2700000000 | bytes 9000000 | tf_op jit(solution)/shard_map/deal/pallas_call | solution.py:831
  3.3 8.5 %all-to-all-start = ((bf16[16,64,384]{2,1,0:T(8,128)(2,1)}), bf16[16,64,384]{2,1,0:T(8,128)(2,1)S(1)}, u32[]{:S(2)}, u32[]{:S(2)}) async-start(bf16[16,64,384]{2,1,0:T(8,128)(2,1)} %deal.1), calls=%async_computation | async-start | bytes 1572864 | tf_op jit(solution)/shard_map/all_to_all | solution.py:908
  21.8 7.2 %prepare.1 = (bf16[768,1920]{1,0:T(8,128)(2,1)}, bf16[1920,768]{1,0:T(8,128)(2,1)}, bf16[768,768]{1,0:T(8,128)(2,1)}, f32[768,8]{1,0:T(8,128)}) custom-call(bf16[768,768]{1,0:T(8,128)(2,1)} %refs_0_.5, bf16[768,768]{1,0:T(8,128)(2,1)} %refs_1_.3, bf16[768,256]{1,0:T(8,128)(2,1)} %refs_2_.1, bf16[768,24]{1,0:T(8,128)(2,1)} %copy.53.refs_3_, ...), custom_call_target="tpu_custom_call" | custom-call | flops 5400000000 | bytes 18000000 | tf_op jit(solution)/shard_map/prepare/pallas_call | solution.py:831
  29.0 2.5 %all-to-all-done = bf16[16,64,384]{2,1,0:T(8,128)(2,1)S(1)} async-done(((bf16[16,64,384]{2,1,0:T(8,128)(2,1)}), bf16[16,64,384]{2,1,0:T(8,128)(2,1)S(1)}, u32[]{:S(2)}, u32[]{:S(2)}) %all-to-all-start) | async-done | bytes 786464 | tf_op jit(solution)/shard_map/all_to_all | solution.py:908
  32.3 4.9 %all-to-all-start.1 = ((bf16[16,64,384]{2,1,0:T(8,128)(2,1)}), bf16[16,64,384]{2,1,0:T(8,128)(2,1)S(1)}, u32[]{:S(2)}, u32[]{:S(2)}) async-start(bf16[16,64,384]{2,1,0:T(8,128)(2,1)} %deal_goal.1), calls=%async_computation.1 | async-start | bytes 1572864 | tf_op jit(solution)/shard_map/all_to_all | solution.py:945
  38.1 27.5 %forward.1 = (bf16[768,1024]{1,0:T(8,128)(2,1)}, bf16[768,1024]{1,0:T(8,128)(2,1)}, f32[120,1024]{1,0:T(8,128)}, f32[8,24,128]{2,1,0:T(8,128)}, f32[768,1024]{1,...) custom-call(s32[1]{0:T(128)} %dynamic_slice.31.refs_0_, ...), custom_call_target="tpu_custom_call" | custom-call | flops 23399999488 | bytes 78000000 | tf_op jit(solution)/shard_map/forward/pallas_call | solution.py:831
  66.2 4.1 %collective-permute-done.2.refs_4_ = bf16[1024,384]{1,0:T(8,128)(2,1)S(1)} collective-permute-done((bf16[1024,384]{1,0:T(8,128)(2,1)S(1)}, bf16[1024,384]{1,0:T(8,128)(2,1)S(1)}, u32[]{:S(2)}, u32[]{:S(2)}) %collective-permute-start.2) | collective-permute-done | bytes 786464 | tf_op jit(solution)/shard_map/ppermute | solution.py:848
  71.8 16.2 %middle.1 = (bf16[1024,384]{1,0:T(8,128)(2,1)}, bf16[384,1024]{1,0:T(8,128)(2,1)}, bf16[768,1024]{1,0:T(8,128)(2,1)}, bf16[768,1024]{1,0:T(8,128)(2,1)}, f32[768...) custom-call(bf16[784,1024]{1,0:T(8,128)(2,1)} %get-tuple-element.117, ...), custom_call_target="tpu_custom_call" | custom-call | flops 12600000512 | bytes 42000000 | tf_op jit(solution)/shard_map/middle/pallas_call | solution.py:831
  91.5 35.7 %backward.1 = (bf16[192,1152]{1,0:T(8,128)(2,1)}, bf16[192,1152]{1,0:T(8,128)(2,1)}, bf16[192,1152]{1,0:T(8,128)(2,1)}, bf16[192,1152]{1,0:T(8,128)(2,1)}, bf16[...) custom-call(s32[1]{0:T(128)} %dynamic_slice.31.refs_0_, f32[1]{0:T(128)} %bitcast.6.refs_1_, ...), custom_call_target="tpu_custom_call" | custom-call | flops 27000000512 | bytes 90000000 | tf_op jit(solution)/shard_map/backward/pallas_call | solution.py:831
  133.2 2.4 collective-permute-start.11
  135.6 4.0 %last.1 = bf16[1024,384]{1,0:T(8,128)(2,1)} custom-call(bf16[384,1024]{1,0:T(8,128)(2,1)} %get-tuple-element.137.refs_0_, bf16[400,1024]{1,0:T(8,128)(2,1)} %copy-done.19, bf16[384,1024]{1,0:T(8,128)(2,1)} %get-tuple-element.144.refs_2_, f32[8,1024]{1,0:T(8,128)} %get-tuple-element.145.refs_3_, f32[8,1024]{1,0:T(8,128)} %get-tuple-element.146.refs_4_, ...), custom_call_target="tpu_custom_call" | custom-call | flops 2700000000 | bytes 9000000 | tf_op jit(solution)/shard_map/last/pallas_call | solution.py:831
  140.6 3.7 %collective-permute-start.12 = (bf16[48,1536]{1,0:T(8,128)(2,1)S(1)}, bf16[48,1536]{1,0:T(8,128)(2,1)S(1)}, u32[]{:S(2)}, u32[]{:S(2)}) collective-permute-start(bf16[48,1536]{1,0:T(8,128)(2,1)S(1)} %get-tuple-element.238), channel_id=1, source_target_pairs={{0,24},{2,26},{4,28},{6,30},{8,16},{10,18},{12,20},{14,22},{16,8},... | collective-permute-start | bytes 442376 | tf_op jit(solution)/shard_map/ppermute | solution.py:852
  144.3 6.8 %collective-permute-done.8 = bf16[192,1152]{1,0:T(8,128)(2,1)S(1)} collective-permute-done((bf16[192,1152]{1,0:T(8,128)(2,1)}, bf16[192,1152]{1,0:T(8,128)(2,1)S(1)}, u32[]{:S(2)}, u32[]{:S(2)}) %collective-permute-start.8) | collective-permute-done | bytes 442400 | tf_op jit(solution)/shard_map/ppermute | solution.py:852
  152.8 2.4 collective-permute-start.14
  156.0 5.6 %all-to-all-start.2 = ((bf16[16,64,384]{2,1,0:T(8,128)(2,1)}), bf16[16,64,384]{2,1,0:T(8,128)(2,1)S(1)}, u32[]{:S(2)}, u32[]{:S(2)}) async-start(bf16[16,64,384]{2,1,0:T(8,128)(2,1)} %bitcast.10), calls=%async_computation.2 | async-start | bytes 1572864 | tf_op jit(solution)/shard_map/all_to_all | solution.py:1061
  161.8 10.9 %collective-permute-done.14 = bf16[48,1536]{1,0:T(8,128)(2,1)S(1)} collective-permute-done((bf16[48,1536]{1,0:T(8,128)(2,1)S(1)}, bf16[48,1536]{1,0:T(8,128)(2,1)S(1)}, u32[]{:S(2)}, u32[]{:S(2)}) %collective-permute-start.14) | collective-permute-done | bytes 147488 | tf_op jit(solution)/shard_map/ppermute | solution.py:852
  172.8 6.9 %collective-permute-start.16 = (bf16[48,1152]{1,0:T(8,128)(2,1)S(1)}, bf16[48,1152]{1,0:T(8,128)(2,1)S(1)}, u32[]{:S(2)}, u32[]{:S(2)}) collective-permute-start(bf16[48,1152]{1,0:T(8,128)(2,1)S(1)} %get-tuple-element.241), channel_id=1, source_target_pairs={{0,8},{2,10},{4,12},{6,14},{8,0},{10,2},{12,4},{14,6},{16,24},{18,... | collective-permute-start | bytes 331784 | tf_op jit(solution)/shard_map/ppermute | solution.py:852
  186.9 6.3 %collective-permute-done.17 = bf16[48,1152]{1,0:T(8,128)(2,1)S(1)} collective-permute-done((bf16[48,1152]{1,0:T(8,128)(2,1)S(1)}, bf16[48,1152]{1,0:T(8,128)(2,1)S(1)}, u32[]{:S(2)}, u32[]{:S(2)}) %collective-permute-start.17) | collective-permute-done | bytes 110624 | tf_op jit(solution)/shard_map/ppermute | solution.py:852
  194.9 4.3 %collective-permute-done.20.refs_3_ = bf16[192,1536]{1,0:T(8,128)(2,1)S(1)} collective-permute-done((bf16[192,1536]{1,0:T(8,128)(2,1)S(1)}, bf16[192,1536]{1,0:T(8,128)(2,1)S(1)}, u32[]{:S(2)}, u32[]{:S(2)}) %collective-permute-start.20) | collective-permute-done | bytes 589856 | tf_op jit(solution)/shard_map/ppermute | solution.py:852
  199.3 7.0 %collective-permute-done.21.refs_4_ = bf16[192,1536]{1,0:T(8,128)(2,1)} collective-permute-done((bf16[192,1536]{1,0:T(8,128)(2,1)S(1)}, bf16[192,1536]{1,0:T(8,128)(2,1)}, u32[]{:S(2)}, u32[]{:S(2)}) %collective-permute-start.21) | collective-permute-done | bytes 589856 | tf_op jit(solution)/shard_map/ppermute | solution.py:852
  212.9 2.3 collective-permute-done.24
  219.5 4.8 %finish_first.1 = (f32[768,768]{1,0:T(8,128)}, f32[768,768]{1,0:T(8,128)}, bf16[16,64,384]{2,1,0:T(8,128)(2,1)}) custom-call(s32[16]{0:T(128)} %refs_0_.6, bf16[8,128]{1,0:T(8,128)(2,1)} %slice.49.refs_1_, bf16[192,1536]{1,0:T(8,128)(2,1)} %copy-done.5, bf16[192,1536]{1,0:T(8,128)(2,1)} %copy-done.22, bf16[192,1536]{1,0:T(8,128)(2,1)} %collective-permute-done.21.refs_4_, ...), custom_call_target="tpu_custom_call" | custom-call | flops 4499999744 | bytes 15000000 | tf_op jit(solution)/shard_map/finish_first/pallas_call | solution.py:831
  224.3 5.3 %collective-permute-done.27.refs_2_ = bf16[192,1152]{1,0:T(8,128)(2,1)S(1)} collective-permute-done((bf16[192,1152]{1,0:T(8,128)(2,1)S(1)}, bf16[192,1152]{1,0:T(8,128)(2,1)S(1)}, u32[]{:S(2)}, u32[]{:S(2)}) %collective-permute-start.27) | collective-permute-done | bytes 442400 | tf_op jit(solution)/shard_map/ppermute | solution.py:852
  231.2 4.5 %finish.1 = (f32[768,768]{1,0:T(8,128)}, f32[768,24]{1,0:T(8,128)}, f32[768,256]{1,0:T(8,128)}, f32[768]{0:T(1024)}, f32[4,768]{1,0:T(4,128)}, /*index=5*/f32[76...) custom-call(bf16[192,1152]{1,0:T(8,128)(2,1)} %copy-done.6, ...), custom_call_target="tpu_custom_call" | custom-call | flops 3600000000 | bytes 12000000 | tf_op jit(solution)/shard_map/finish/pallas_call | solution.py:831
  (158 shorter events, 48.1 us)
Async XLA Ops:
  3.3 28.2 %all-to-all-start = ((bf16[16,64,384]{2,1,0:T(8,128)(2,1)}), bf16[16,64,384]{2,1,0:T(8,128)(2,1)S(1)}, u32[]{:S(2)}, u32[]{:S(2)}) async-start(bf16[16,64,384]{2,1,0:T(8,128)(2,1)} %deal.1), calls=%async_computation | async-start | bytes 1572864 | tf_op jit(solution)/shard_map/all_to_all | solution.py:908
  32.3 33.5 %all-to-all-start.1 = ((bf16[16,64,384]{2,1,0:T(8,128)(2,1)}), bf16[16,64,384]{2,1,0:T(8,128)(2,1)S(1)}, u32[]{:S(2)}, u32[]{:S(2)}) async-start(bf16[16,64,384]{2,1,0:T(8,128)(2,1)} %deal_goal.1), calls=%async_computation.1 | async-start | bytes 1572864 | tf_op jit(solution)/shard_map/all_to_all | solution.py:945
  88.0 41.4 %collective-permute-start.3 = (bf16[192,1536]{1,0:T(8,128)(2,1)}, bf16[192,1536]{1,0:T(8,128)(2,1)S(1)}, u32[]{:S(2)}, u32[]{:S(2)}) collective-permute-start(bf16[192,1536]{1,0:T(8,128)(2,1)} %get-tuple-element.139), channel_id=1, source_target_pairs={{0,2},{2,0},{4,6},{6,4},{8,10},{10,8},{12,14},{14,12},{16,18},{18,... | collective-permute-start | bytes 1769480 | tf_op jit(solution)/shard_map/ppermute | solution.py:852
  89.9 40.9 %collective-permute-start.4 = (bf16[192,1536]{1,0:T(8,128)(2,1)}, bf16[192,1536]{1,0:T(8,128)(2,1)S(1)}, u32[]{:S(2)}, u32[]{:S(2)}) collective-permute-start(bf16[192,1536]{1,0:T(8,128)(2,1)} %get-tuple-element.140), channel_id=1, source_target_pairs={{0,4},{2,6},{4,0},{6,2},{8,12},{10,14},{12,8},{14,10},{16,20},{18,... | collective-permute-start | bytes 1769480 | tf_op jit(solution)/shard_map/ppermute | solution.py:852
  91.4 39.6 %collective-permute-start.5 = (bf16[192,1536]{1,0:T(8,128)(2,1)}, bf16[192,1536]{1,0:T(8,128)(2,1)S(1)}, u32[]{:S(2)}, u32[]{:S(2)}) collective-permute-start(bf16[192,1536]{1,0:T(8,128)(2,1)} %get-tuple-element.141), channel_id=1, source_target_pairs={{0,6},{2,4},{4,2},{6,0},{8,14},{10,12},{12,10},{14,8},{16,22},{18,... | collective-permute-start | bytes 1769480 | tf_op jit(solution)/shard_map/ppermute | solution.py:852
  127.4 13.3 %collective-permute-start.7 = (bf16[192,1152]{1,0:T(8,128)(2,1)}, bf16[192,1152]{1,0:T(8,128)(2,1)S(1)}, u32[]{:S(2)}, u32[]{:S(2)}) collective-permute-start(bf16[192,1152]{1,0:T(8,128)(2,1)} %get-tuple-element.148), channel_id=1, source_target_pairs={{0,2},{2,0},{4,6},{6,4},{8,10},{10,8},{12,14},{14,12},{16,18},{18,... | collective-permute-start | bytes 1327112 | tf_op jit(solution)/shard_map/ppermute | solution.py:852
  129.3 21.8 %collective-permute-start.8 = (bf16[192,1152]{1,0:T(8,128)(2,1)}, bf16[192,1152]{1,0:T(8,128)(2,1)S(1)}, u32[]{:S(2)}, u32[]{:S(2)}) collective-permute-start(bf16[192,1152]{1,0:T(8,128)(2,1)} %get-tuple-element.149), channel_id=1, source_target_pairs={{0,4},{2,6},{4,0},{6,2},{8,12},{10,14},{12,8},{14,10},{16,20},{18,... | collective-permute-start | bytes 1327112 | tf_op jit(solution)/shard_map/ppermute | solution.py:852
  130.8 20.4 %collective-permute-start.9 = (bf16[192,1152]{1,0:T(8,128)(2,1)}, bf16[192,1152]{1,0:T(8,128)(2,1)S(1)}, u32[]{:S(2)}, u32[]{:S(2)}) collective-permute-start(bf16[192,1152]{1,0:T(8,128)(2,1)} %get-tuple-element.150), channel_id=1, source_target_pairs={{0,6},{2,4},{4,2},{6,0},{8,14},{10,12},{12,10},{14,8},{16,22},{18,... | collective-permute-start | bytes 1327112 | tf_op jit(solution)/shard_map/ppermute | solution.py:852
  131.3 19.8 %collective-permute-start.10 = (bf16[48,1536]{1,0:T(8,128)(2,1)S(1)}, bf16[48,1536]{1,0:T(8,128)(2,1)S(1)}, u32[]{:S(2)}, u32[]{:S(2)}) collective-permute-start(bf16[48,1536]{1,0:T(8,128)(2,1)S(1)} %get-tuple-element.240), channel_id=1, source_target_pairs={{0,8},{2,10},{4,12},{6,14},{8,0},{10,2},{12,4},{14,6},{16,24},{18,... | collective-permute-start | bytes 442376 | tf_op jit(solution)/shard_map/ppermute | solution.py:852
  133.2 17.9 %collective-permute-start.11 = (bf16[48,1536]{1,0:T(8,128)(2,1)S(1)}, bf16[48,1536]{1,0:T(8,128)(2,1)S(1)}, u32[]{:S(2)}, u32[]{:S(2)}) collective-permute-start(bf16[48,1536]{1,0:T(8,128)(2,1)S(1)} %get-tuple-element.239), channel_id=1, source_target_pairs={{0,16},{2,18},{4,20},{6,22},{8,24},{10,26},{12,28},{14,30},{16,0},... | collective-permute-start | bytes 442376 | tf_op jit(solution)/shard_map/ppermute | solution.py:852
  140.6 10.6 %collective-permute-start.12 = (bf16[48,1536]{1,0:T(8,128)(2,1)S(1)}, bf16[48,1536]{1,0:T(8,128)(2,1)S(1)}, u32[]{:S(2)}, u32[]{:S(2)}) collective-permute-start(bf16[48,1536]{1,0:T(8,128)(2,1)S(1)} %get-tuple-element.238), channel_id=1, source_target_pairs={{0,24},{2,26},{4,28},{6,30},{8,16},{10,18},{12,20},{14,22},{16,8},... | collective-permute-start | bytes 442376 | tf_op jit(solution)/shard_map/ppermute | solution.py:852
  151.3 10.5 %collective-permute-start.13 = (bf16[48,1536]{1,0:T(8,128)(2,1)S(1)}, bf16[48,1536]{1,0:T(8,128)(2,1)S(1)}, u32[]{:S(2)}, u32[]{:S(2)}) collective-permute-start(bf16[48,1536]{1,0:T(8,128)(2,1)S(1)} %add_convert_fusion), channel_id=1, source_target_pairs={{0,8},{2,10},{4,12},{6,14},{8,0},{10,2},{12,4},{14,6},{16,24},{18,... | collective-permute-start | bytes 442376 | tf_op jit(solution)/shard_map/ppermute | solution.py:852
  152.8 19.9 %collective-permute-start.14 = (bf16[48,1536]{1,0:T(8,128)(2,1)S(1)}, bf16[48,1536]{1,0:T(8,128)(2,1)S(1)}, u32[]{:S(2)}, u32[]{:S(2)}) collective-permute-start(bf16[48,1536]{1,0:T(8,128)(2,1)S(1)} %add_convert_fusion), channel_id=1, source_target_pairs={{0,16},{2,18},{4,20},{6,22},{8,24},{10,26},{12,28},{14,30},{16,0},... | collective-permute-start | bytes 442376 | tf_op jit(solution)/shard_map/ppermute | solution.py:852
  155.1 17.6 %collective-permute-start.15 = (bf16[48,1536]{1,0:T(8,128)(2,1)S(1)}, bf16[48,1536]{1,0:T(8,128)(2,1)S(1)}, u32[]{:S(2)}, u32[]{:S(2)}) collective-permute-start(bf16[48,1536]{1,0:T(8,128)(2,1)S(1)} %add_convert_fusion), channel_id=1, source_target_pairs={{0,24},{2,26},{4,28},{6,30},{8,16},{10,18},{12,20},{14,22},{16,8},... | collective-permute-start | bytes 442376 | tf_op jit(solution)/shard_map/ppermute | solution.py:852
  156.0 59.3 %all-to-all-start.2 = ((bf16[16,64,384]{2,1,0:T(8,128)(2,1)}), bf16[16,64,384]{2,1,0:T(8,128)(2,1)S(1)}, u32[]{:S(2)}, u32[]{:S(2)}) async-start(bf16[16,64,384]{2,1,0:T(8,128)(2,1)} %bitcast.10), calls=%async_computation.2 | async-start | bytes 1572864 | tf_op jit(solution)/shard_map/all_to_all | solution.py:1061
  172.8 12.7 %collective-permute-start.16 = (bf16[48,1152]{1,0:T(8,128)(2,1)S(1)}, bf16[48,1152]{1,0:T(8,128)(2,1)S(1)}, u32[]{:S(2)}, u32[]{:S(2)}) collective-permute-start(bf16[48,1152]{1,0:T(8,128)(2,1)S(1)} %get-tuple-element.241), channel_id=1, source_target_pairs={{0,8},{2,10},{4,12},{6,14},{8,0},{10,2},{12,4},{14,6},{16,24},{18,... | collective-permute-start | bytes 331784 | tf_op jit(solution)/shard_map/ppermute | solution.py:852
  179.7 13.5 %collective-permute-start.17 = (bf16[48,1152]{1,0:T(8,128)(2,1)S(1)}, bf16[48,1152]{1,0:T(8,128)(2,1)S(1)}, u32[]{:S(2)}, u32[]{:S(2)}) collective-permute-start(bf16[48,1152]{1,0:T(8,128)(2,1)S(1)} %get-tuple-element.243), channel_id=1, source_target_pairs={{0,16},{2,18},{4,20},{6,22},{8,24},{10,26},{12,28},{14,30},{16,0},... | collective-permute-start | bytes 331784 | tf_op jit(solution)/shard_map/ppermute | solution.py:852
  181.8 11.3 %collective-permute-start.18 = (bf16[48,1152]{1,0:T(8,128)(2,1)S(1)}, bf16[48,1152]{1,0:T(8,128)(2,1)S(1)}, u32[]{:S(2)}, u32[]{:S(2)}) collective-permute-start(bf16[48,1152]{1,0:T(8,128)(2,1)S(1)} %get-tuple-element.242), channel_id=1, source_target_pairs={{0,24},{2,26},{4,28},{6,30},{8,16},{10,18},{12,20},{14,22},{16,8},... | collective-permute-start | bytes 331784 | tf_op jit(solution)/shard_map/ppermute | solution.py:852
  183.4 15.9 %collective-permute-start.20 = (bf16[192,1536]{1,0:T(8,128)(2,1)S(1)}, bf16[192,1536]{1,0:T(8,128)(2,1)S(1)}, u32[]{:S(2)}, u32[]{:S(2)}) collective-permute-start(bf16[192,1536]{1,0:T(8,128)(2,1)S(1)} %pad_maximum_fusion.refs_2_), channel_id=1, source_target_pairs={{0,2},{2,0},{4,6},{6,4},{8,10},{10,8},{12,14},{14,12},{16,18},{18,... | collective-permute-start | bytes 1769480 | tf_op jit(solution)/shard_map/ppermute | solution.py:852
  184.7 21.5 %collective-permute-start.21 = (bf16[192,1536]{1,0:T(8,128)(2,1)S(1)}, bf16[192,1536]{1,0:T(8,128)(2,1)}, u32[]{:S(2)}, u32[]{:S(2)}) collective-permute-start(bf16[192,1536]{1,0:T(8,128)(2,1)S(1)} %pad_maximum_fusion.refs_2_), channel_id=1, source_target_pairs={{0,4},{2,6},{4,0},{6,2},{8,12},{10,14},{12,8},{14,10},{16,20},{18,... | collective-permute-start | bytes 1769480 | tf_op jit(solution)/shard_map/ppermute | solution.py:852
  185.5 20.8 %collective-permute-start.22 = (bf16[192,1536]{1,0:T(8,128)(2,1)S(1)}, bf16[192,1536]{1,0:T(8,128)(2,1)}, u32[]{:S(2)}, u32[]{:S(2)}) collective-permute-start(bf16[192,1536]{1,0:T(8,128)(2,1)S(1)} %pad_maximum_fusion.refs_2_), channel_id=1, source_target_pairs={{0,6},{2,4},{4,2},{6,0},{8,14},{10,12},{12,10},{14,8},{16,22},{18,... | collective-permute-start | bytes 1769480 | tf_op jit(solution)/shard_map/ppermute | solution.py:852
  215.3 9.0 %collective-permute-start.26 = (bf16[192,1152]{1,0:T(8,128)(2,1)S(1)}, bf16[192,1152]{1,0:T(8,128)(2,1)S(1)}, u32[]{:S(2)}, u32[]{:S(2)}) collective-permute-start(bf16[192,1152]{1,0:T(8,128)(2,1)S(1)} %pad_maximum_fusion.1.refs_0_), channel_id=1, source_target_pairs={{0,2},{2,0},{4,6},{6,4},{8,10},{10,8},{12,14},{14,12},{16,18},{18,... | collective-permute-start | bytes 1327112 | tf_op jit(solution)/shard_map/ppermute | solution.py:852
  216.6 13.0 %collective-permute-start.27 = (bf16[192,1152]{1,0:T(8,128)(2,1)S(1)}, bf16[192,1152]{1,0:T(8,128)(2,1)S(1)}, u32[]{:S(2)}, u32[]{:S(2)}) collective-permute-start(bf16[192,1152]{1,0:T(8,128)(2,1)S(1)} %pad_maximum_fusion.1.refs_0_), channel_id=1, source_target_pairs={{0,4},{2,6},{4,0},{6,2},{8,12},{10,14},{12,8},{14,10},{16,20},{18,... | collective-permute-start | bytes 1327112 | tf_op jit(solution)/shard_map/ppermute | solution.py:852
  218.0 11.6 %collective-permute-start.28 = (bf16[192,1152]{1,0:T(8,128)(2,1)S(1)}, bf16[192,1152]{1,0:T(8,128)(2,1)S(1)}, u32[]{:S(2)}, u32[]{:S(2)}) collective-permute-start(bf16[192,1152]{1,0:T(8,128)(2,1)S(1)} %pad_maximum_fusion.1.refs_0_), channel_id=1, source_target_pairs={{0,6},{2,4},{4,2},{6,0},{8,14},{10,12},{12,10},{14,8},{16,22},{18,... | collective-permute-start | bytes 1327112 | tf_op jit(solution)/shard_map/ppermute | solution.py:852
  (37 other events, 358.7 us)
